TPU v7x, 32 devices: a whole 2x2x4 slice. The times are simulated.
32 devices in a mesh: parts: 2 (over y), blk: 4 (over z), col: 4 (over x, core).
Axes of the slice: x: 2, y: 2, z: 4, core: 2. Of those that a mesh axis runs over, the one named last changes fastest.
Arguments:
- tiles: bfloat16 [8, 4, 4, 10, 128, 128], P(('parts', 'blk'), 'col'), parts along dimension 0
- tile_dest: int32 [8, 4, 4, 10], P(('parts', 'blk'), 'col'), parts along dimension 0, may hold values from 0 to 3
- tile_count: int32 [8, 4, 4], P(('parts', 'blk'), 'col'), parts along dimension 0, may hold values from 1 to 10, as said below
- topic_seeds: int32 [512, 64], P('parts'), parts along dimension 0, may hold values from 0 to 2047
Outputs:
- scores: float32 [4096, 256], P(('parts', 'blk', 'col')), parts along dimension 0
There are 2 independent parts, one for each index of `parts`. A program takes and returns all parts, laid end to end along the dimension named above; each array names one. Nothing has to cross between parts.
Inputs may be any that keep to these rules, and one draw needn't show every extreme that they name: `tile_count`: live tiles of a group of slots; the largest value is 10 in every draw.
All inputs are finite; a program needn't handle non-finite values.
Results may differ from a plain program's by a relative error of at most 0.01.
Values may be sent and summed in bfloat16 or wider, within the bound.
No kernel may reach another device: no remote copies, remote signals or barrier semaphores. Data moves between devices by JAX's collectives and lax.ppermute only.
A program may use at most 64 MiB of HBM per device.

v0:
```python
import jax
import jax.numpy as jnp
from jax import lax
from jax.sharding import PartitionSpec as P

ITERS = 3


damping = 0.85


def from_behind(block, axis, distance):
    devices = range(lax.axis_size(axis))
    route = [((i - distance) % len(devices), i) for i in devices]
    return lax.ppermute(block, axis, route)


def body(tiles, tile_dest, tile_count, topic_seeds):
    tile_stack = tiles[0, 0]
    dest_table = tile_dest[0, 0]
    live_counts = tile_count[0, 0]
    per_step = tile_stack.shape[1]
    tile_edge = tile_stack.shape[2]
    columns = lax.axis_size("col")
    cycle_size = lax.axis_size("blk")
    topics = topic_seeds.shape[0]
    restart_scale = cycle_size * columns * tile_edge / topic_seeds.shape[1]
    own_row = lax.axis_index("blk")
    host_base = (own_row * columns + lax.axis_index("col")) * tile_edge
    host_ids = host_base + jnp.arange(tile_edge, dtype=jnp.int32)
    seed_hits = jnp.sum(
        (topic_seeds[None, :, :] == host_ids[:, None, None]).astype(jnp.float32), axis=2
    )
    restart = restart_scale * seed_hits
    slot_ids = jnp.arange(per_step, dtype=jnp.int32)
    block_ids = jnp.arange(columns, dtype=jnp.int32)
    half_rows = columns * tile_edge

    def step_terms(held_block, step_index):
        group_tiles = lax.dynamic_index_in_dim(tile_stack, step_index, 0, keepdims=False)
        group_dest = lax.dynamic_index_in_dim(dest_table, step_index, 0, keepdims=False)
        group_count = lax.dynamic_index_in_dim(live_counts, step_index, 0, keepdims=False)
        live_mask = slot_ids < group_count
        placing = ((group_dest[:, None] == block_ids[None, :]) & live_mask[:, None]).astype(
            jnp.float32
        )
        products = jnp.dot(
            group_tiles.reshape(per_step * tile_edge, tile_edge),
            held_block,
            preferred_element_type=jnp.float32,
        )
        products = products.reshape(per_step, tile_edge * topics)
        result = jnp.dot(placing.T, products, precision=lax.Precision.HIGHEST)
        return result.reshape(half_rows, topics)

    scores = restart
    for iteration in range(ITERS):
        sent_scores = scores.astype(jnp.bfloat16)

        def cycle_turn(step_index, carry):
            held_block, running = carry
            held_block = from_behind(held_block, "blk", 1)
            return (held_block, running + step_terms(held_block, step_index))

        first_part = step_terms(sent_scores, 0)
        cycle_out = lax.fori_loop(1, cycle_size, cycle_turn, (sent_scores, first_part))
        partial_rows = cycle_out[1]
        propagated = lax.psum_scatter(
            partial_rows.astype(jnp.bfloat16), "col", scatter_dimension=0, tiled=True
        ).astype(jnp.float32)
        scores = damping * propagated + (1.0 - damping) * restart
    return scores


def solution(mesh):
    return jax.shard_map(
        body,
        mesh=mesh,
        in_specs=(
            P(("parts", "blk"), "col", None, None, None, None),
            P(("parts", "blk"), "col", None, None),
            P(("parts", "blk"), "col", None),
            P("parts", None),
        ),
        out_specs=P(("parts", "blk", "col"), None),
        check_vma=False,
    )
```

profile of v0, /device:TPU:0, one launch (start us, length us, event | category | flops | bytes accessed | tf_op | source)
XLA Modules:
  0.0 180.5 jit_solution(5633523729935172365)
XLA Ops:
  6.5 1.9 %convert_reduce_fusion = f32[128,256]{1,0:T(8,128)S(1)} fusion(s32[256,64]{0,1:T(8,128)} %param.13, s32[128]{0:T(128)S(1)} %iota_add_fusion), kind=kLoop, calls=%fused_computation.30 | loop fusion | flops 6258688 | bytes 197120 | tf_op jit(solution)/shard_map/reduce_sum | solution.py:31
  8.5 1.8 dynamic_slice.110
  10.3 1.3 convolution_bitcast_fusion.2
  13.4 0.9 fusion.32
  14.3 1.2 reshape.160
  15.5 27.9 %while.54 = (s32[]{:T(128)}, bf16[128,256]{1,0:T(8,128)(2,1)S(1)}, f32[512,256]{1,0:T(8,128)}, s32[4,10]{1,0:T(4,128)}, s32[4]{0:T(128)S(1)}, /*index=5*/bf16[4,...) while((s32[]{:T(128)}, bf16[128,256]{1,0:T(8,128)(2,1)S(1)}, ...), condition=%wide.region_2.3_spmd.clone, body=%wide.region_1.2_spmd.clone.sunk | while | flops 99745880 | bytes 14025199 | solution.py:66
  15.5 3.0 %collective-permute-start = (bf16[128,256]{1,0:T(8,128)(2,1)S(1)}, bf16[128,256]{1,0:T(8,128)(2,1)S(1)}, u32[]{:S(2)}, u32[]{:S(2)}) collective-permute-start(bf16[128,256]{1,0:T(8,128)(2,1)S(1)} %get-tuple-element.804), channel_id=1, source_target_pairs={{12,0},{0,4},{4,8},{8,12},{13,1},{1,5},{5,9},{9,13},{14,2},{2,6},{... | collective-permute-start | bytes 196616 | tf_op jit(solution)/shard_map/while/body/eval_jaxpr/ppermute | solution.py:15
  18.5 1.0 constant_dynamic-slice_fusion.6
  20.7 0.7 dynamic-slice_bitcast_fusion.6
  21.4 1.4 collective-permute-done
  23.4 0.9 fusion.84
  24.8 0.8 copy-done.1
  25.8 1.0 constant_dynamic-slice_fusion.6
  27.9 0.7 dynamic-slice_bitcast_fusion.6
  28.6 3.0 %collective-permute-done = bf16[128,256]{1,0:T(8,128)(2,1)S(1)} collective-permute-done((bf16[128,256]{1,0:T(8,128)(2,1)S(1)}, bf16[128,256]{1,0:T(8,128)(2,1)S(1)}, u32[]{:S(2)}, u32[]{:S(2)}) %collective-permute-start) | collective-permute-done | bytes 65568 | tf_op jit(solution)/shard_map/while/body/eval_jaxpr/ppermute | solution.py:15
  32.3 0.9 fusion.84
  33.7 0.8 copy-done.1
  34.5 1.0 constant_dynamic-slice_fusion.6
  37.4 3.2 %collective-permute-done = bf16[128,256]{1,0:T(8,128)(2,1)S(1)} collective-permute-done((bf16[128,256]{1,0:T(8,128)(2,1)S(1)}, bf16[128,256]{1,0:T(8,128)(2,1)S(1)}, u32[]{:S(2)}, u32[]{:S(2)}) %collective-permute-start) | collective-permute-done | bytes 65568 | tf_op jit(solution)/shard_map/while/body/eval_jaxpr/ppermute | solution.py:15
  41.2 0.9 fusion.84
  42.6 0.8 copy-done.1
  43.4 1.8 convert_element_type.44
  45.3 18.6 %reduce-scatter.4.cloned.1.call-done = bf16[128,256]{1,0:T(8,128)(2,1)} async-done(((bf16[512,256]{1,0:T(8,128)(2,1)}), bf16[128,256]{1,0:T(8,128)(2,1)}) %reduce-scatter.4.cloned.1.call-update) | async-done | bytes 65552 | tf_op jit(solution)/shard_map/reduce_scatter | solution.py:68
  63.9 1.0 add_convert_fusion.1
  64.9 1.3 convolution_bitcast_fusion.1
  66.9 0.9 fusion.30
  67.8 1.2 reshape.162
  69.0 29.8 %while.55 = (s32[]{:T(128)}, bf16[128,256]{1,0:T(8,128)(2,1)S(1)}, f32[512,256]{1,0:T(8,128)}, s32[4,10]{1,0:T(4,128)}, s32[4]{0:T(128)S(1)}, /*index=5*/bf16[4,...) while((s32[]{:T(128)}, bf16[128,256]{1,0:T(8,128)(2,1)S(1)}, f32[512,256]{1,0:T(8,128)}, ...), condition=%wide.region_5.6_spmd.clone, body=%wide.region_4.5_spmd.clone.sunk | while | flops 99745880 | bytes 9830923 | solution.py:66
  69.0 1.5 collective-permute-start.1
  70.5 1.0 constant_dynamic-slice_fusion.7
  73.4 1.6 collective-permute-done.1
  75.6 0.9 fusion.90
  76.9 1.9 %add.209 = f32[512,256]{1,0:T(8,128)} add(f32[512,256]{1,0:T(8,128)} %get-tuple-element.832, f32[512,256]{1,0:T(8,128)S(1)} %reshape.183) | non-fusion elementwise | flops 131072 | bytes 1572864 | tf_op jit(solution)/shard_map/while/body/eval_jaxpr/add | solution.py:63
  78.9 1.0 constant_dynamic-slice_fusion.7
  81.9 3.1 %collective-permute-done.1 = bf16[128,256]{1,0:T(8,128)(2,1)S(1)} collective-permute-done((bf16[128,256]{1,0:T(8,128)(2,1)S(1)}, bf16[128,256]{1,0:T(8,128)(2,1)S(1)}, u32[]{:S(2)}, u32[]{:S(2)}) %collective-permute-start.1) | collective-permute-done | bytes 65568 | tf_op jit(solution)/shard_map/while/body/eval_jaxpr/ppermute | solution.py:15
  85.6 0.9 fusion.90
  86.9 1.9 %add.209 = f32[512,256]{1,0:T(8,128)} add(f32[512,256]{1,0:T(8,128)} %get-tuple-element.832, f32[512,256]{1,0:T(8,128)S(1)} %reshape.183) | non-fusion elementwise | flops 131072 | bytes 1572864 | tf_op jit(solution)/shard_map/while/body/eval_jaxpr/add | solution.py:63
  88.9 1.0 constant_dynamic-slice_fusion.7
  91.9 3.1 %collective-permute-done.1 = bf16[128,256]{1,0:T(8,128)(2,1)S(1)} collective-permute-done((bf16[128,256]{1,0:T(8,128)(2,1)S(1)}, bf16[128,256]{1,0:T(8,128)(2,1)S(1)}, u32[]{:S(2)}, u32[]{:S(2)}) %collective-permute-start.1) | collective-permute-done | bytes 65568 | tf_op jit(solution)/shard_map/while/body/eval_jaxpr/ppermute | solution.py:15
  95.5 0.9 fusion.90
  96.8 1.9 %add.209 = f32[512,256]{1,0:T(8,128)} add(f32[512,256]{1,0:T(8,128)} %get-tuple-element.832, f32[512,256]{1,0:T(8,128)S(1)} %reshape.183) | non-fusion elementwise | flops 131072 | bytes 1572864 | tf_op jit(solution)/shard_map/while/body/eval_jaxpr/add | solution.py:63
  98.8 1.8 convert_element_type.47
  100.8 17.3 %reduce-scatter.6.cloned.1.call-done = bf16[128,256]{1,0:T(8,128)(2,1)} async-done(((bf16[512,256]{1,0:T(8,128)(2,1)}), bf16[128,256]{1,0:T(8,128)(2,1)}) %reduce-scatter.6.cloned.1.call-update) | async-done | bytes 65552 | tf_op jit(solution)/shard_map/reduce_scatter | solution.py:68
  118.1 1.0 add_convert_fusion
  119.1 1.3 convolution_bitcast_fusion
  121.1 0.9 fusion.28
  122.0 1.2 reshape.164
  123.2 29.8 %while.56 = (s32[]{:T(128)}, bf16[128,256]{1,0:T(8,128)(2,1)S(1)}, f32[512,256]{1,0:T(8,128)}, s32[4,10]{1,0:T(4,128)}, s32[4]{0:T(128)S(1)}, /*index=5*/bf16[4,...) while((s32[]{:T(128)}, bf16[128,256]{1,0:T(8,128)(2,1)S(1)}, f32[512,256]{1,0:T(8,128)}, ...), condition=%wide.region_8.9_spmd.clone, body=%wide.region_7.8_spmd.clone.sunk | while | flops 99745880 | bytes 9830923 | solution.py:66
  123.2 1.5 collective-permute-start.2
  124.6 1.0 constant_dynamic-slice_fusion.8
  127.7 1.5 collective-permute-done.2
  129.8 0.9 fusion.96
  131.1 1.9 %add.212 = f32[512,256]{1,0:T(8,128)} add(f32[512,256]{1,0:T(8,128)} %get-tuple-element.859, f32[512,256]{1,0:T(8,128)S(1)} %reshape.185) | non-fusion elementwise | flops 131072 | bytes 1572864 | tf_op jit(solution)/shard_map/while/body/eval_jaxpr/add | solution.py:63
  133.1 1.0 constant_dynamic-slice_fusion.8
  136.2 3.0 %collective-permute-done.2 = bf16[128,256]{1,0:T(8,128)(2,1)S(1)} collective-permute-done((bf16[128,256]{1,0:T(8,128)(2,1)S(1)}, bf16[128,256]{1,0:T(8,128)(2,1)S(1)}, u32[]{:S(2)}, u32[]{:S(2)}) %collective-permute-start.2) | collective-permute-done | bytes 65568 | tf_op jit(solution)/shard_map/while/body/eval_jaxpr/ppermute | solution.py:15
  139.8 0.9 fusion.96
  141.1 1.9 %add.212 = f32[512,256]{1,0:T(8,128)} add(f32[512,256]{1,0:T(8,128)} %get-tuple-element.859, f32[512,256]{1,0:T(8,128)S(1)} %reshape.185) | non-fusion elementwise | flops 131072 | bytes 1572864 | tf_op jit(solution)/shard_map/while/body/eval_jaxpr/add | solution.py:63
  143.1 1.0 constant_dynamic-slice_fusion.8
  146.1 3.0 %collective-permute-done.2 = bf16[128,256]{1,0:T(8,128)(2,1)S(1)} collective-permute-done((bf16[128,256]{1,0:T(8,128)(2,1)S(1)}, bf16[128,256]{1,0:T(8,128)(2,1)S(1)}, u32[]{:S(2)}, u32[]{:S(2)}) %collective-permute-start.2) | collective-permute-done | bytes 65568 | tf_op jit(solution)/shard_map/while/body/eval_jaxpr/ppermute | solution.py:15
  149.7 0.9 fusion.96
  151.0 1.9 %add.212 = f32[512,256]{1,0:T(8,128)} add(f32[512,256]{1,0:T(8,128)} %get-tuple-element.859, f32[512,256]{1,0:T(8,128)S(1)} %reshape.185) | non-fusion elementwise | flops 131072 | bytes 1572864 | tf_op jit(solution)/shard_map/while/body/eval_jaxpr/add | solution.py:63
  152.9 1.8 convert_element_type.50
  154.7 17.7 %reduce-scatter.8.cloned.1.call-done = bf16[128,256]{1,0:T(8,128)(2,1)} async-done(((bf16[512,256]{1,0:T(8,128)(2,1)}), bf16[128,256]{1,0:T(8,128)(2,1)}) %reduce-scatter.8.cloned.1.call-update) | async-done | bytes 65552 | tf_op jit(solution)/shard_map/reduce_scatter | solution.py:68
  172.4 1.6 multiply_add_fusion
  (129 shorter events, 28.8 us)
Async XLA Ops:
  6.5 57.4 %reduce-scatter.4.cloned.1.call-start = ((), (), s32[]{:S(2)}) async-start(), calls=%async_computation.3 | async-start | bytes 327680 | tf_op jit(solution)/shard_map/reduce_scatter | solution.py:68
  8.5 1.8 copy-start.2
  12.0 0.7 copy-start.3
  15.5 7.3 %collective-permute-start = (bf16[128,256]{1,0:T(8,128)(2,1)S(1)}, bf16[128,256]{1,0:T(8,128)(2,1)S(1)}, u32[]{:S(2)}, u32[]{:S(2)}) collective-permute-start(bf16[128,256]{1,0:T(8,128)(2,1)S(1)} %get-tuple-element.804), channel_id=1, source_target_pairs={{12,0},{0,4},{4,8},{8,12},{13,1},{1,5},{5,9},{9,13},{14,2},{2,6},{... | collective-permute-start | bytes 196616 | tf_op jit(solution)/shard_map/while/body/eval_jaxpr/ppermute | solution.py:15
  23.4 1.3 copy-start
  24.3 1.3 copy-start.4
  24.8 0.8 copy-start.1
  25.6 6.1 %collective-permute-start = (bf16[128,256]{1,0:T(8,128)(2,1)S(1)}, bf16[128,256]{1,0:T(8,128)(2,1)S(1)}, u32[]{:S(2)}, u32[]{:S(2)}) collective-permute-start(bf16[128,256]{1,0:T(8,128)(2,1)S(1)} %get-tuple-element.804), channel_id=1, source_target_pairs={{12,0},{0,4},{4,8},{8,12},{13,1},{1,5},{5,9},{9,13},{14,2},{2,6},{... | collective-permute-start | bytes 196616 | tf_op jit(solution)/shard_map/while/body/eval_jaxpr/ppermute | solution.py:15
  32.3 1.3 copy-start
  33.2 1.3 copy-start.4
  33.7 0.8 copy-start.1
  34.5 6.1 %collective-permute-start = (bf16[128,256]{1,0:T(8,128)(2,1)S(1)}, bf16[128,256]{1,0:T(8,128)(2,1)S(1)}, u32[]{:S(2)}, u32[]{:S(2)}) collective-permute-start(bf16[128,256]{1,0:T(8,128)(2,1)S(1)} %get-tuple-element.804), channel_id=1, source_target_pairs={{12,0},{0,4},{4,8},{8,12},{13,1},{1,5},{5,9},{9,13},{14,2},{2,6},{... | collective-permute-start | bytes 196616 | tf_op jit(solution)/shard_map/while/body/eval_jaxpr/ppermute | solution.py:15
  41.2 1.3 copy-start
  42.1 1.3 copy-start.4
  42.6 0.8 copy-start.1
  45.2 72.9 %reduce-scatter.6.cloned.1.call-start = ((), (), s32[]{:S(2)}) async-start(), calls=%async_computation.4 | async-start | bytes 327680 | tf_op jit(solution)/shard_map/reduce_scatter | solution.py:68
  69.0 3.1 %copy-start.5 = (s32[4]{0:T(128)}, s32[4]{0:T(128)S(1)}, u32[]{:S(2)}) copy-start(s32[4]{0:T(128)S(1)} %get-tuple-element.843) | copy-start | bytes 52 | tf_op jit(solution)/shard_map/while
  69.0 6.1 %collective-permute-start.1 = (bf16[128,256]{1,0:T(8,128)(2,1)S(1)}, bf16[128,256]{1,0:T(8,128)(2,1)S(1)}, u32[]{:S(2)}, u32[]{:S(2)}) collective-permute-start(bf16[128,256]{1,0:T(8,128)(2,1)S(1)} %get-tuple-element.831), channel_id=1, source_target_pairs={{12,0},{0,4},{4,8},{8,12},{13,1},{1,5},{5,9},{9,13},{14,2},{2,6},{... | collective-permute-start | bytes 196616 | tf_op jit(solution)/shard_map/while/body/eval_jaxpr/ppermute | solution.py:15
  76.5 2.3 %copy-start.6 = (s32[4]{0:T(128)S(1)}, s32[4]{0:T(128)}, u32[]{:S(2)}) copy-start(s32[4]{0:T(128)} %copy-done.5) | copy-start | bytes 52 | tf_op jit(solution)/shard_map/while
  78.9 1.7 copy-start.5
  78.9 6.1 %collective-permute-start.1 = (bf16[128,256]{1,0:T(8,128)(2,1)S(1)}, bf16[128,256]{1,0:T(8,128)(2,1)S(1)}, u32[]{:S(2)}, u32[]{:S(2)}) collective-permute-start(bf16[128,256]{1,0:T(8,128)(2,1)S(1)} %get-tuple-element.831), channel_id=1, source_target_pairs={{12,0},{0,4},{4,8},{8,12},{13,1},{1,5},{5,9},{9,13},{14,2},{2,6},{... | collective-permute-start | bytes 196616 | tf_op jit(solution)/shard_map/while/body/eval_jaxpr/ppermute | solution.py:15
  86.5 2.3 %copy-start.6 = (s32[4]{0:T(128)S(1)}, s32[4]{0:T(128)}, u32[]{:S(2)}) copy-start(s32[4]{0:T(128)} %copy-done.5) | copy-start | bytes 52 | tf_op jit(solution)/shard_map/while
  88.8 1.7 copy-start.5
  88.8 6.1 %collective-permute-start.1 = (bf16[128,256]{1,0:T(8,128)(2,1)S(1)}, bf16[128,256]{1,0:T(8,128)(2,1)S(1)}, u32[]{:S(2)}, u32[]{:S(2)}) collective-permute-start(bf16[128,256]{1,0:T(8,128)(2,1)S(1)} %get-tuple-element.831), channel_id=1, source_target_pairs={{12,0},{0,4},{4,8},{8,12},{13,1},{1,5},{5,9},{9,13},{14,2},{2,6},{... | collective-permute-start | bytes 196616 | tf_op jit(solution)/shard_map/while/body/eval_jaxpr/ppermute | solution.py:15
  96.4 2.3 %copy-start.6 = (s32[4]{0:T(128)S(1)}, s32[4]{0:T(128)}, u32[]{:S(2)}) copy-start(s32[4]{0:T(128)} %copy-done.5) | copy-start | bytes 52 | tf_op jit(solution)/shard_map/while
  100.6 71.8 %reduce-scatter.8.cloned.1.call-start = ((), (), s32[]{:S(2)}) async-start(), calls=%async_computation.5 | async-start | bytes 327680 | tf_op jit(solution)/shard_map/reduce_scatter | solution.py:68
  123.2 3.1 %copy-start.7 = (s32[4]{0:T(128)}, s32[4]{0:T(128)S(1)}, u32[]{:S(2)}) copy-start(s32[4]{0:T(128)S(1)} %get-tuple-element.870) | copy-start | bytes 52 | tf_op jit(solution)/shard_map/while
  123.2 6.1 %collective-permute-start.2 = (bf16[128,256]{1,0:T(8,128)(2,1)S(1)}, bf16[128,256]{1,0:T(8,128)(2,1)S(1)}, u32[]{:S(2)}, u32[]{:S(2)}) collective-permute-start(bf16[128,256]{1,0:T(8,128)(2,1)S(1)} %get-tuple-element.858), channel_id=1, source_target_pairs={{12,0},{0,4},{4,8},{8,12},{13,1},{1,5},{5,9},{9,13},{14,2},{2,6},{... | collective-permute-start | bytes 196616 | tf_op jit(solution)/shard_map/while/body/eval_jaxpr/ppermute | solution.py:15
  130.7 2.3 %copy-start.8 = (s32[4]{0:T(128)S(1)}, s32[4]{0:T(128)}, u32[]{:S(2)}) copy-start(s32[4]{0:T(128)} %copy-done.7) | copy-start | bytes 52 | tf_op jit(solution)/shard_map/while
  133.0 1.7 copy-start.7
  133.1 6.1 %collective-permute-start.2 = (bf16[128,256]{1,0:T(8,128)(2,1)S(1)}, bf16[128,256]{1,0:T(8,128)(2,1)S(1)}, u32[]{:S(2)}, u32[]{:S(2)}) collective-permute-start(bf16[128,256]{1,0:T(8,128)(2,1)S(1)} %get-tuple-element.858), channel_id=1, source_target_pairs={{12,0},{0,4},{4,8},{8,12},{13,1},{1,5},{5,9},{9,13},{14,2},{2,6},{... | collective-permute-start | bytes 196616 | tf_op jit(solution)/shard_map/while/body/eval_jaxpr/ppermute | solution.py:15
  140.7 2.3 %copy-start.8 = (s32[4]{0:T(128)S(1)}, s32[4]{0:T(128)}, u32[]{:S(2)}) copy-start(s32[4]{0:T(128)} %copy-done.7) | copy-start | bytes 52 | tf_op jit(solution)/shard_map/while
  143.0 1.7 copy-start.7
  143.0 6.1 %collective-permute-start.2 = (bf16[128,256]{1,0:T(8,128)(2,1)S(1)}, bf16[128,256]{1,0:T(8,128)(2,1)S(1)}, u32[]{:S(2)}, u32[]{:S(2)}) collective-permute-start(bf16[128,256]{1,0:T(8,128)(2,1)S(1)} %get-tuple-element.858), channel_id=1, source_target_pairs={{12,0},{0,4},{4,8},{8,12},{13,1},{1,5},{5,9},{9,13},{14,2},{2,6},{... | collective-permute-start | bytes 196616 | tf_op jit(solution)/shard_map/while/body/eval_jaxpr/ppermute | solution.py:15
  150.6 2.3 %copy-start.8 = (s32[4]{0:T(128)S(1)}, s32[4]{0:T(128)}, u32[]{:S(2)}) copy-start(s32[4]{0:T(128)} %copy-done.7) | copy-start | bytes 52 | tf_op jit(solution)/shard_map/while
Sparse Core Ops, SparseCore 0:
  45.3 18.5 reduce-scatter.3
  100.7 17.3 reduce-scatter.5
  154.8 17.5 reduce-scatter.7
where the time goes:
time: 182 us; the launch traced here: 181 us
  waiting for transfers between devices  76.7 us (42%)
  local copies, waits for them, and re-layouts  37.2 us (20%)
  other arithmetic  28.3 us (16%)
  matrix products  17.7 us (10%)
  between operations  13.3 us (7%)
  starting transfers between devices  6.66 us (4%)
    reduce_scatter x3, waiting for transfers between devices, body(): lax.psum_scatter(partial_rows.astype(jnp.bfloat16), 'col', scatter_dimens...  53.6 us
    ppermute x9, waiting for transfers between devices, from_behind(): return lax.ppermute(block, axis, route)  23 us
    add x9, other arithmetic, cycle_turn(): return (held_block, running + step_terms(held_block, step_index))  11.8 us
    dot_general x12, matrix products, step_terms(): result = jnp.dot(placing.T, products, precision=lax.Precision.HIGHEST)  10.9 us
    dynamic_slice x10, local copies, waits for them, and re-layouts, step_terms(): lax.dynamic_index_in_dim(tile_stack, step_index, 0, keepdims=False)  10.7 us
    eq x10, local copies, waits for them, and re-layouts, step_terms(): group_dest[:, None] == block_ids[None, :]  6.92 us
    dot_general x12, matrix products, step_terms(): jnp.dot(group_tiles.reshape(per_step * tile_edge, tile_edge), held_block,...  6.76 us
    reshape x12, local copies, waits for them, and re-layouts, step_terms(): return result.reshape(half_rows, topics)  6.75 us
  transfers between devices with their start and end apart: 12, of which 12 were waited for; matrix products, arithmetic and copies ran while one was open for 15% of the time, Pallas kernels for 0%

commit v1 on v0

v1 whole, which is shorter than its diff:
```python
import functools

import jax
import jax.numpy as jnp
from jax import lax
from jax.experimental import pallas as pl
from jax.experimental.pallas import tpu as pltpu
from jax.sharding import PartitionSpec as P

ITERS = 3
CORES = 2
FIELD = 8
PACKED = 4

damping = 0.85

VMEM = pl.BlockSpec(memory_space=pltpu.VMEM)
SMEM = pl.BlockSpec(memory_space=pltpu.SMEM)
HBM = pl.BlockSpec(memory_space=pltpu.HBM)
MIB = 1 << 20


def place():
    col = lax.axis_index("col")
    return lax.axis_index("blk"), col // CORES, col % CORES


def packed_counts(ids, weights, edge):
    seeds, lanes = ids.shape
    rows = lax.broadcasted_iota(jnp.int32, (edge, lanes), 0)

    def add_seed(j, total):
        hit = rows == ids[pl.ds(j, 1), :]
        return [t + jnp.where(hit, w[pl.ds(j, 1), :], 0) for t, w in zip(total, weights)]

    zero = jnp.zeros((edge, lanes), jnp.int32)
    return lax.fori_loop(0, seeds, add_seed, [zero for _ in weights], unroll=16)


def field(packed, index):
    return ((packed >> (FIELD * index)) & ((1 << FIELD) - 1)).astype(jnp.float32)


def first_kernel(
    steps, columns, scale, tiles, dest, count, seeds,
    dense, keep, send, seed_rows, tile_buf, seed_buf, total, ids, weights, tile_sem, seed_sem,
):
    slots, edge = tile_buf.shape[1], tile_buf.shape[2]
    topics = seed_buf.shape[1]
    row, chip, core = place()
    col = chip * CORES + core
    fetch_seeds = [
        pltpu.make_async_copy(
            seeds.at[pl.ds(lax.rem(core + h, CORES) * topics, topics), :], seed_buf.at[h], seed_sem.at[h]
        )
        for h in range(CORES)
    ]
    fetch_tiles = [
        pltpu.make_async_copy(tiles.at[0, 0, s], tile_buf.at[s], tile_sem.at[s]) for s in range(steps)
    ]
    for fetch in fetch_seeds + fetch_tiles:
        fetch.start()

    groups = -(-steps // PACKED)
    counts = []
    for h in range(CORES):
        fetch_seeds[h].wait()
        hosts = seed_buf[h].astype(jnp.float32).T.astype(jnp.int32)
        if h == 0:
            seed_rows[...] = hosts
        ids[h] = hosts & (edge - 1)
        block = hosts >> (edge.bit_length() - 1)
        step = lax.rem(row - block // columns + steps, steps)
        mine = lax.rem(block, columns) == col
        one = 1 << (FIELD * lax.rem(step, PACKED))
        for g in range(groups):
            weights[h, g] = jnp.where(mine & (step // PACKED == g), one, 0)
        counts.append(packed_counts(ids.at[h], [weights.at[h, g] for g in range(groups)], edge))
    restart = [
        jnp.concatenate(
            [scale * field(counts[h][s // PACKED], s % PACKED) for s in range(steps)], axis=0
        ).astype(jnp.bfloat16)
        for h in range(CORES)
    ]

    for s in range(steps):
        fetch_tiles[s].wait()
        total[...] = jnp.zeros_like(total)

        def add_tile(t, carry):
            rows = pl.ds(pl.multiple_of(dest[0, 0, s, t] * edge, edge), edge)
            total[rows, :] += tile_buf[s, t].astype(jnp.float32)
            return carry

        lax.fori_loop(0, count[0, 0, s], add_tile, 0)
        dense[:, s * edge : (s + 1) * edge] = total[...].astype(jnp.bfloat16)

    keep[...] = jnp.dot(dense[...], restart[0], preferred_element_type=jnp.float32)
    send[...] = jnp.dot(dense[...], restart[1], preferred_element_type=jnp.float32).astype(jnp.bfloat16)


def restart_kernel(columns, scale, seed_rows, restart, ids, weight):
    edge = restart.shape[0] // CORES
    row, chip, core = place()
    hosts = seed_rows[...]
    ids[...] = hosts & (edge - 1)
    block = hosts >> (edge.bit_length() - 1)
    offset = block - row * columns - chip * CORES
    weight[...] = jnp.where(
        (offset >= 0) & (offset < CORES), 1 << (FIELD * jnp.clip(offset, 0, CORES - 1)), 0
    )
    (packed,) = packed_counts(ids, [weight], edge)
    for c in range(CORES):
        restart[c * edge : (c + 1) * edge, :] = (1.0 - damping) * (scale * field(packed, c))


def split_kernel(chips, keep, recv, mine, *sends):
    _, chip, _ = place()
    size = mine.shape[0]
    for d in range(chips):
        rows = pl.ds(pl.multiple_of(lax.rem(chip + d, chips) * size, size), size)
        part = keep[rows, :] + recv[rows, :].astype(jnp.float32)
        if d == 0:
            mine[...] = part
        else:
            sends[d - 1][...] = part.astype(jnp.bfloat16)


def gathered(scores, core, edge):
    return [
        jnp.concatenate([s[pl.ds(pl.multiple_of(c * edge, edge), edge), :] for s in scores], axis=0)
        for c in (core, 1 - core)
    ]


def step_kernel(chips, steps, own, other, *refs):
    scores, mine, sends = refs[:steps], refs[steps], refs[steps + 1 :]
    _, chip, core = place()
    size = mine.shape[0]
    sources = gathered(scores, core, size // CORES)
    for d in [*range(1, chips), 0]:
        rows = pl.ds(pl.multiple_of(lax.rem(chip + d, chips) * size, size), size)
        part = jnp.dot(own[rows, :], sources[0], preferred_element_type=jnp.float32)
        part += jnp.dot(other[rows, :], sources[1], preferred_element_type=jnp.float32)
        if d == 0:
            mine[...] = part
        else:
            sends[d - 1][...] = part.astype(jnp.bfloat16)


def last_kernel(chips, steps, own, other, restart, *refs):
    scores, parts = refs[:steps], refs[steps:]
    _, chip, core = place()
    edge = parts[0].shape[0]
    sources = gathered(scores, core, edge)
    for d in range(chips):
        for e in range(CORES):
            owner = lax.rem(core + e, CORES)
            block = lax.rem(chip + d, chips) * CORES + owner
            rows = pl.ds(pl.multiple_of(block * edge, edge), edge)
            part = jnp.dot(own[rows, :], sources[0], preferred_element_type=jnp.float32)
            part += jnp.dot(other[rows, :], sources[1], preferred_element_type=jnp.float32)
            if d == 0:
                rows = pl.ds(pl.multiple_of(owner * edge, edge), edge)
                part = damping * part + restart[rows, :]
            ref = parts[d * CORES + e]
            ref[...] = part.astype(ref.dtype)


def final_kernel(chips, *refs):
    parts, out = refs[:-1], refs[-1]
    _, _, core = place()
    topics = parts[0].shape[1]
    for e in range(CORES):
        total = sum(parts[d * CORES + e][...].astype(jnp.float32) for d in range(1, chips))
        lanes = pl.ds(pl.multiple_of(lax.rem(core + e, CORES) * topics, topics), topics)
        out[:, lanes] = parts[e][...] + damping * total


def from_col(value, chips, chip_step, core_step):
    route = [
        (x * CORES + c, (x + chip_step) % chips * CORES + (c + core_step) % CORES)
        for x in range(chips)
        for c in range(CORES)
    ]
    return lax.ppermute(value, "col", route)


def from_blk(value, steps, distance):
    return lax.ppermute(value, "blk", [(i, (i + distance) % steps) for i in range(steps)])


def body(tiles, tile_dest, tile_count, topic_seeds):
    slots, edge = tiles.shape[3], tiles.shape[4]
    steps, columns = lax.axis_size("blk"), lax.axis_size("col")
    chips = columns // CORES
    topics, seeds = topic_seeds.shape[0] // CORES, topic_seeds.shape[1]
    dests, sources, pair = columns * edge, steps * edge, CORES * edge
    groups = -(-steps // PACKED)
    scale = steps * columns * edge / seeds
    f32, bf16, i32 = jnp.float32, jnp.bfloat16, jnp.int32

    def shape(dtype, *dims):
        return jax.ShapeDtypeStruct(dims, dtype)

    def call(kernel, in_specs, outs, room, scratch=()):
        return pl.pallas_call(
            kernel,
            in_specs=in_specs,
            out_shape=outs,
            out_specs=[VMEM] * len(outs),
            scratch_shapes=scratch,
            compiler_params=pltpu.CompilerParams(vmem_limit_bytes=room),
        )

    matrix = 2 * dests * sources
    dense, keep, send, seed_rows = call(
        functools.partial(first_kernel, steps, columns, scale),
        [HBM, SMEM, SMEM, HBM],
        [
            shape(bf16, dests, sources),
            shape(f32, dests, topics),
            shape(bf16, dests, topics),
            shape(i32, seeds, topics),
        ],
        6 * MIB + 2 * matrix + 2 * steps * slots * edge * edge,
        [
            pltpu.VMEM((steps, slots, edge, edge), bf16),
            pltpu.VMEM((CORES, topics, seeds), i32),
            pltpu.VMEM((dests, edge), f32),
            pltpu.VMEM((CORES, seeds, topics), i32),
            pltpu.VMEM((CORES, groups, seeds, topics), i32),
            pltpu.SemaphoreType.DMA((steps,)),
            pltpu.SemaphoreType.DMA((CORES,)),
        ],
    )(tiles, tile_dest, tile_count, topic_seeds)
    (restart,) = call(
        functools.partial(restart_kernel, columns, scale),
        [VMEM],
        [shape(f32, pair, topics)],
        4 * MIB,
        [pltpu.VMEM((seeds, topics), i32), pltpu.VMEM((seeds, topics), i32)],
    )(seed_rows)
    recv = from_col(send, chips, 0, 1)
    split = [shape(f32, pair, topics)] + [shape(bf16, pair, topics)] * (chips - 1)
    parts = call(functools.partial(split_kernel, chips), [VMEM] * 2, split, 6 * MIB)(keep, recv)

    other = from_col(dense, chips, 0, 1)
    for iteration in range(ITERS):
        if iteration:
            parts = call(
                functools.partial(step_kernel, chips, steps),
                [VMEM] * (2 + steps),
                split,
                6 * MIB + 2 * matrix,
            )(dense, other, *gather)
        total = parts[0]
        for d in range(1, chips):
            total = total + from_col(parts[d], chips, d, 0).astype(f32)
        sent = (damping * total + restart).astype(bf16)
        gather = [sent] + [from_blk(sent, steps, d) for d in range(1, steps)]
        if iteration == ITERS - 2:
            break
    parts = call(
        functools.partial(last_kernel, chips, steps),
        [VMEM] * (3 + steps),
        [shape(f32, edge, topics)] * CORES + [shape(bf16, edge, topics)] * (CORES * (chips - 1)),
        6 * MIB + 2 * matrix,
    )(dense, other, restart, *gather)
    arrived = [
        part if d == e == 0 else from_col(part, chips, d, e)
        for (d, e), part in zip([(d, e) for d in range(chips) for e in range(CORES)], parts)
    ]
    (out,) = call(
        functools.partial(final_kernel, chips),
        [VMEM] * len(arrived),
        [shape(f32, edge, CORES * topics)],
        4 * MIB,
    )(*arrived)
    return out


def solution(mesh):
    return jax.shard_map(
        body,
        mesh=mesh,
        in_specs=(
            P(("parts", "blk"), "col", None, None, None, None),
            P(("parts", "blk"), "col", None, None),
            P(("parts", "blk"), "col", None),
            P("parts", None),
        ),
        out_specs=P(("parts", "blk", "col"), None),
        check_vma=False,
    )
```

time: 182 us -> 44 us (0.24)
  waiting for transfers between devices: 76.7 us -> 19 us
  local copies, waits for them, and re-layouts: 37.2 us -> 3.58 us
  other arithmetic: 28.3 us -> 0.05 us
  matrix products: 17.7 us -> 0 us
  between operations: 13.3 us -> 0.07 us
  starting transfers between devices: 6.66 us -> 15.5 us
  Pallas kernels: 0 us -> 5.49 us
    reduce_scatter x3 -> x0, waiting for transfers between devices: 53.6 us -> none  [body(): lax.psum_scatter(partial_rows.astype(jnp.bfloat16), 'col', scatter_dimens...]
    dot_general x24 -> x0, matrix products: 17.7 us -> none  [the longest x12 10.9 us: step_terms(): result = jnp.dot(placing.T, products, precision=lax.Precision.HIGHEST)]
    dynamic_slice x19 -> x0, local copies, waits for them, and re-layouts: 16.3 us -> none  [the longest x10 10.7 us: step_terms(): lax.dynamic_index_in_dim(tile_stack, step_index, 0, keepdims=False)]
    add x11 -> x0, other arithmetic: 13.4 us -> none  [the longest x9 11.8 us: cycle_turn(): return (held_block, running + step_terms(held_block, step_index))]
    reshape x24 -> x0, local copies, waits for them, and re-layouts: 9.95 us -> none  [the longest x12 6.75 us: step_terms(): return result.reshape(half_rows, topics)]
    ppermute x9 -> x13, starting transfers between devices: 6.4 us -> 15.5 us  [the longest x6 8.39 us: from_blk(): lax.ppermute(value, 'blk', [(i, (i + distance) % steps) for i in range(st...]
    convert_element_type x6 -> x2, other arithmetic: 7.25 us -> 0.05 us  [body(): sent = (damping * total + restart).astype(bf16)]
    eq x10 -> x0, local copies, waits for them, and re-layouts: 6.92 us -> none  [step_terms(): group_dest[:, None] == block_ids[None, :]]
  transfers between devices with their start and end apart: 12 -> 13, of which waited for: 12 -> 10; matrix products, arithmetic and copies ran while one was open for 15% -> 0% of each run, Pallas kernels for 0% -> 1%
where the time goes in v1:
time: 44 us; the launch traced here: 43.7 us
  waiting for transfers between devices  19 us (43%)
  starting transfers between devices  15.5 us (35%)
  Pallas kernels  5.49 us (12%)
  local copies, waits for them, and re-layouts  3.58 us (8%)
    ppermute x6, waiting for transfers between devices, from_blk(): lax.ppermute(value, 'blk', [(i, (i + distance) % steps) for i in range(st...  9.7 us
    ppermute x7, waiting for transfers between devices, from_col(): return lax.ppermute(value, 'col', route)  9.3 us
    ppermute x6, starting transfers between devices, from_blk(): lax.ppermute(value, 'blk', [(i, (i + distance) % steps) for i in range(st...  8.39 us
    ppermute x7, starting transfers between devices, from_col(): return lax.ppermute(value, 'col', route)  7.15 us
    unnamed x7, local copies, waits for them, and re-layouts  3.58 us
    pallas_call x1, Pallas kernels, body(): call(functools.partial(first_kernel, steps, columns, scale), [HBM, SMEM,...  3.43 us
  transfers between devices with their start and end apart: 13, of which 10 were waited for; matrix products, arithmetic and copies ran while one was open for 0% of the time, Pallas kernels for 1%

profile of v1, /device:TPU:0, one launch (start us, length us, event | category | flops | bytes accessed | tf_op | source)
XLA Modules:
  0.0 43.7 jit_solution(9275383190577744298)
XLA Ops:
  0.0 0.9 %copy.5.seeds = s32[256,64]{1,0:T(8,128)S(1)} copy(s32[256,64]{0,1:T(8,128)} %param.7) | data formatting | bytes 131072 | tf_op args[3]
  0.9 0.0 copy-start
  0.9 1.3 %copy-done = bf16[1,1,4,10,128,128]{5,4,3,2,1,0:T(8,128)(2,1)S(1)} copy-done((bf16[1,1,4,10,128,128]{5,4,3,2,1,0:T(8,128)(2,1)S(1)}, bf16[1,1,4,10,128,128]{5,4,3,2,1,0:T(8,128)(2,1)}, u32[]{:S(2)}) %copy-start) | copy-done | bytes 1310744
  2.3 0.0 copy-start.1
  2.3 0.7 %copy-done.1 = s32[1,1,4,10]{3,2,1,0:T(4,128)S(1)} copy-done((s32[1,1,4,10]{3,2,1,0:T(4,128)S(1)}, s32[1,1,4,10]{3,2,1,0:T(4,128)}, u32[]{:S(2)}) %copy-start.1) | copy-done | bytes 184
  2.9 0.0 copy-start.2
  2.9 0.7 %copy-done.2 = s32[1,1,4]{2,1,0:T(1,128)S(1)} copy-done((s32[1,1,4]{2,1,0:T(1,128)S(1)}, s32[1,1,4]{2,1,0:T(1,128)}, u32[]{:S(2)}) %copy-start.2) | copy-done | bytes 40
  3.6 3.4 %shard_map.46 = (bf16[512,512]{1,0:T(8,128)(2,1)S(1)}, f32[512,128]{1,0:T(8,128)S(1)}, bf16[512,128]{1,0:T(8,128)(2,1)S(1)}, s32[64,128]{1,0:T(8,128)S(1)}) custom-call(bf16[1,1,4,10,128,128]{5,4,3,2,1,0:T(8,128)(2,1)S(1)} %copy-done, s32[1,1,4,10]{3,2,1,0:T(4,128)S(1)} %copy-done.1, s32[1,1,4]{2,1,0:T(1,128)S(1)} %copy-done.2, s32[256,64]{1,0:T(8,128)S(1)} %copy.5.seeds), custom_call_target="tpu_custom_call" | custom-call | tf_op jit(solution)/shard_map/pallas_call | solution.py:217
  7.0 0.4 %collective-permute-start = (bf16[512,512]{1,0:T(8,128)(2,1)S(1)}, bf16[512,512]{1,0:T(8,128)(2,1)S(1)}, u32[]{:S(2)}, u32[]{:S(2)}) collective-permute-start(bf16[512,512]{1,0:T(8,128)(2,1)S(1)} %get-tuple-element.17.own), channel_id=1, source_target_pairs={{0,1},{1,0},{2,3},{3,2},{4,5},{5,4},{6,7},{7,6},{8,9},{9,8},{10,11... | collective-permute-start | bytes 1572872 | tf_op jit(solution)/shard_map/ppermute | solution.py:186
  7.5 0.1 collective-permute-start.1
  7.6 1.6 %collective-permute-done.1.recv = bf16[512,128]{1,0:T(8,128)(2,1)S(1)} collective-permute-done((bf16[512,128]{1,0:T(8,128)(2,1)S(1)}, bf16[512,128]{1,0:T(8,128)(2,1)S(1)}, u32[]{:S(2)}, u32[]{:S(2)}) %collective-permute-start.1) | collective-permute-done | bytes 131104 | tf_op jit(solution)/shard_map/ppermute | solution.py:186
  9.2 3.0 %collective-permute-start.2 = (bf16[256,128]{1,0:T(8,128)(2,1)S(1)}, bf16[256,128]{1,0:T(8,128)(2,1)S(1)}, u32[]{:S(2)}, u32[]{:S(2)}) collective-permute-start(bf16[256,128]{1,0:T(8,128)(2,1)S(1)} %get-tuple-element.22), channel_id=1, source_target_pairs={{0,2},{1,3},{2,0},{3,1},{4,6},{5,7},{6,4},{7,5},{8,10},{9,11},{10,... | collective-permute-start | bytes 196616 | tf_op jit(solution)/shard_map/ppermute | solution.py:186
  12.3 0.5 %shard_map.47.restart = f32[256,128]{1,0:T(8,128)S(1)} custom-call(s32[64,128]{1,0:T(8,128)S(1)} %get-tuple-element.18.seed_rows), custom_call_target="tpu_custom_call" | custom-call | tf_op jit(solution)/shard_map/pallas_call | solution.py:237
  12.8 1.9 %collective-permute-done.2 = bf16[256,128]{1,0:T(8,128)(2,1)S(1)} collective-permute-done((bf16[256,128]{1,0:T(8,128)(2,1)S(1)}, bf16[256,128]{1,0:T(8,128)(2,1)S(1)}, u32[]{:S(2)}, u32[]{:S(2)}) %collective-permute-start.2) | collective-permute-done | bytes 65568 | tf_op jit(solution)/shard_map/ppermute | solution.py:186
  14.7 3.9 %collective-permute-start.5 = (bf16[256,128]{1,0:T(8,128)(2,1)S(1)}, bf16[256,128]{1,0:T(8,128)(2,1)S(1)}, u32[]{:S(2)}, u32[]{:S(2)}) collective-permute-start(bf16[256,128]{1,0:T(8,128)(2,1)S(1)} %add_convert_fusion.1.refs_0_), channel_id=1, source_target_pairs={{0,12},{4,0},{8,4},{12,8},{1,13},{5,1},{9,5},{13,9},{2,14},{6,2},{... | collective-permute-start | bytes 196616 | tf_op jit(solution)/shard_map/ppermute | solution.py:190
  18.6 0.0 collective-permute-start.4
  18.6 1.0 %collective-permute-start.3 = (bf16[256,128]{1,0:T(8,128)(2,1)S(1)}, bf16[256,128]{1,0:T(8,128)(2,1)S(1)}, u32[]{:S(2)}, u32[]{:S(2)}) collective-permute-start(bf16[256,128]{1,0:T(8,128)(2,1)S(1)} %add_convert_fusion.1.refs_0_), channel_id=1, source_target_pairs={{0,4},{4,8},{8,12},{12,0},{1,5},{5,9},{9,13},{13,1},{2,6},{6,10},{... | collective-permute-start | bytes 196616 | tf_op jit(solution)/shard_map/ppermute | solution.py:190
  19.6 0.9 %collective-permute-done.5.refs_3_ = bf16[256,128]{1,0:T(8,128)(2,1)S(1)} collective-permute-done((bf16[256,128]{1,0:T(8,128)(2,1)S(1)}, bf16[256,128]{1,0:T(8,128)(2,1)S(1)}, u32[]{:S(2)}, u32[]{:S(2)}) %collective-permute-start.5) | collective-permute-done | bytes 65568 | tf_op jit(solution)/shard_map/ppermute | solution.py:190
  20.5 3.3 %collective-permute-done.4.refs_2_ = bf16[256,128]{1,0:T(8,128)(2,1)S(1)} collective-permute-done((bf16[256,128]{1,0:T(8,128)(2,1)S(1)}, bf16[256,128]{1,0:T(8,128)(2,1)S(1)}, u32[]{:S(2)}, u32[]{:S(2)}) %collective-permute-start.4) | collective-permute-done | bytes 65568 | tf_op jit(solution)/shard_map/ppermute | solution.py:190
  23.8 0.9 %collective-permute-done.3.refs_1_ = bf16[256,128]{1,0:T(8,128)(2,1)S(1)} collective-permute-done((bf16[256,128]{1,0:T(8,128)(2,1)S(1)}, bf16[256,128]{1,0:T(8,128)(2,1)S(1)}, u32[]{:S(2)}, u32[]{:S(2)}) %collective-permute-start.3) | collective-permute-done | bytes 65568 | tf_op jit(solution)/shard_map/ppermute | solution.py:190
  24.7 0.0 collective-permute-done.other
  24.7 0.4 shard_map.49
  25.1 1.6 %collective-permute-start.6 = (bf16[256,128]{1,0:T(8,128)(2,1)S(1)}, bf16[256,128]{1,0:T(8,128)(2,1)S(1)}, u32[]{:S(2)}, u32[]{:S(2)}) collective-permute-start(bf16[256,128]{1,0:T(8,128)(2,1)S(1)} %get-tuple-element.24), channel_id=1, source_target_pairs={{0,2},{1,3},{2,0},{3,1},{4,6},{5,7},{6,4},{7,5},{8,10},{9,11},{10,... | collective-permute-start | bytes 196616 | tf_op jit(solution)/shard_map/ppermute | solution.py:186
  26.7 2.7 %collective-permute-done.6 = bf16[256,128]{1,0:T(8,128)(2,1)S(1)} collective-permute-done((bf16[256,128]{1,0:T(8,128)(2,1)S(1)}, bf16[256,128]{1,0:T(8,128)(2,1)S(1)}, u32[]{:S(2)}, u32[]{:S(2)}) %collective-permute-start.6) | collective-permute-done | bytes 65568 | tf_op jit(solution)/shard_map/ppermute | solution.py:186
  29.5 1.6 %collective-permute-start.9 = (bf16[256,128]{1,0:T(8,128)(2,1)S(1)}, bf16[256,128]{1,0:T(8,128)(2,1)S(1)}, u32[]{:S(2)}, u32[]{:S(2)}) collective-permute-start(bf16[256,128]{1,0:T(8,128)(2,1)S(1)} %add_convert_fusion.refs_0_), channel_id=1, source_target_pairs={{0,12},{4,0},{8,4},{12,8},{1,13},{5,1},{9,5},{13,9},{2,14},{6,2},{... | collective-permute-start | bytes 196616 | tf_op jit(solution)/shard_map/ppermute | solution.py:190
  31.1 0.0 collective-permute-start.8
  31.1 1.8 %collective-permute-start.7 = (bf16[256,128]{1,0:T(8,128)(2,1)S(1)}, bf16[256,128]{1,0:T(8,128)(2,1)S(1)}, u32[]{:S(2)}, u32[]{:S(2)}) collective-permute-start(bf16[256,128]{1,0:T(8,128)(2,1)S(1)} %add_convert_fusion.refs_0_), channel_id=1, source_target_pairs={{0,4},{4,8},{8,12},{12,0},{1,5},{5,9},{9,13},{13,1},{2,6},{6,10},{... | collective-permute-start | bytes 196616 | tf_op jit(solution)/shard_map/ppermute | solution.py:190
  33.0 1.5 %collective-permute-done.9.refs_3_ = bf16[256,128]{1,0:T(8,128)(2,1)S(1)} collective-permute-done((bf16[256,128]{1,0:T(8,128)(2,1)S(1)}, bf16[256,128]{1,0:T(8,128)(2,1)S(1)}, u32[]{:S(2)}, u32[]{:S(2)}) %collective-permute-start.9) | collective-permute-done | bytes 65568 | tf_op jit(solution)/shard_map/ppermute | solution.py:190
  34.5 3.1 %collective-permute-done.8.refs_2_ = bf16[256,128]{1,0:T(8,128)(2,1)S(1)} collective-permute-done((bf16[256,128]{1,0:T(8,128)(2,1)S(1)}, bf16[256,128]{1,0:T(8,128)(2,1)S(1)}, u32[]{:S(2)}, u32[]{:S(2)}) %collective-permute-start.8) | collective-permute-done | bytes 65568 | tf_op jit(solution)/shard_map/ppermute | solution.py:190
  37.6 0.0 collective-permute-done.7.refs_1_
  37.6 0.4 shard_map.50
  38.0 0.1 collective-permute-start.10
  38.1 1.6 %collective-permute-start.11 = (bf16[128,128]{1,0:T(8,128)(2,1)S(1)}, bf16[128,128]{1,0:T(8,128)(2,1)S(1)}, u32[]{:S(2)}, u32[]{:S(2)}) collective-permute-start(bf16[128,128]{1,0:T(8,128)(2,1)S(1)} %get-tuple-element.27), channel_id=1, source_target_pairs={{0,2},{1,3},{2,0},{3,1},{4,6},{5,7},{6,4},{7,5},{8,10},{9,11},{10,... | collective-permute-start | bytes 98312 | tf_op jit(solution)/shard_map/ppermute | solution.py:186
  39.7 0.3 collective-permute-start.12
  40.0 2.1 %collective-permute-done.11.refs_2_ = bf16[128,128]{1,0:T(8,128)(2,1)S(1)} collective-permute-done((bf16[128,128]{1,0:T(8,128)(2,1)S(1)}, bf16[128,128]{1,0:T(8,128)(2,1)S(1)}, u32[]{:S(2)}, u32[]{:S(2)}) %collective-permute-start.11) | collective-permute-done | bytes 32800 | tf_op jit(solution)/shard_map/ppermute | solution.py:186
  42.1 1.0 %collective-permute-done.12.refs_3_ = bf16[128,128]{1,0:T(8,128)(2,1)S(1)} collective-permute-done((bf16[128,128]{1,0:T(8,128)(2,1)S(1)}, bf16[128,128]{1,0:T(8,128)(2,1)S(1)}, u32[]{:S(2)}, u32[]{:S(2)}) %collective-permute-start.12) | collective-permute-done | bytes 32800 | tf_op jit(solution)/shard_map/ppermute | solution.py:186
  43.0 0.0 collective-permute-done.10.refs_1_
  43.0 0.7 %shard_map.51 = f32[128,256]{1,0:T(8,128)} custom-call(f32[128,128]{1,0:T(8,128)S(1)} %get-tuple-element.25.refs_0_, f32[128,128]{1,0:T(8,128)S(1)} %collective-permute-done.10.refs_1_, bf16[128,128]{1,0:T(8,128)(2,1)S(1)} %collective-permute-done.11.refs_2_, bf16[128,128]{1,0:T(8,128)(2,1)S(1)} %collective-permute-done.12.refs_3_), custom_call_target="tpu_custom_call" | custom-call | tf_op jit(solution)/shard_map/pallas_call | solution.py:274
  (3 shorter events, 0.1 us)
Async XLA Ops:
  0.9 1.3 %copy-start = (bf16[1,1,4,10,128,128]{5,4,3,2,1,0:T(8,128)(2,1)S(1)}, bf16[1,1,4,10,128,128]{5,4,3,2,1,0:T(8,128)(2,1)}, u32[]{:S(2)}) copy-start(bf16[1,1,4,10,128,128]{5,4,3,2,1,0:T(8,128)(2,1)} %tiles.1) | copy-start | bytes 3932164
  2.3 0.7 %copy-start.1 = (s32[1,1,4,10]{3,2,1,0:T(4,128)S(1)}, s32[1,1,4,10]{3,2,1,0:T(4,128)}, u32[]{:S(2)}) copy-start(s32[1,1,4,10]{3,2,1,0:T(4,128)} %dest.1) | copy-start | bytes 484
  2.9 0.7 %copy-start.2 = (s32[1,1,4]{2,1,0:T(1,128)S(1)}, s32[1,1,4]{2,1,0:T(1,128)}, u32[]{:S(2)}) copy-start(s32[1,1,4]{2,1,0:T(1,128)} %count.1) | copy-start | bytes 52
  7.0 17.7 %collective-permute-start = (bf16[512,512]{1,0:T(8,128)(2,1)S(1)}, bf16[512,512]{1,0:T(8,128)(2,1)S(1)}, u32[]{:S(2)}, u32[]{:S(2)}) collective-permute-start(bf16[512,512]{1,0:T(8,128)(2,1)S(1)} %get-tuple-element.17.own), channel_id=1, source_target_pairs={{0,1},{1,0},{2,3},{3,2},{4,5},{5,4},{6,7},{7,6},{8,9},{9,8},{10,11... | collective-permute-start | bytes 1572872 | tf_op jit(solution)/shard_map/ppermute | solution.py:186
  7.5 1.7 %collective-permute-start.1 = (bf16[512,128]{1,0:T(8,128)(2,1)S(1)}, bf16[512,128]{1,0:T(8,128)(2,1)S(1)}, u32[]{:S(2)}, u32[]{:S(2)}) collective-permute-start(bf16[512,128]{1,0:T(8,128)(2,1)S(1)} %get-tuple-element.20), channel_id=1, source_target_pairs={{0,1},{1,0},{2,3},{3,2},{4,5},{5,4},{6,7},{7,6},{8,9},{9,8},{10,11... | collective-permute-start | bytes 393224 | tf_op jit(solution)/shard_map/ppermute | solution.py:186
  9.2 5.4 %collective-permute-start.2 = (bf16[256,128]{1,0:T(8,128)(2,1)S(1)}, bf16[256,128]{1,0:T(8,128)(2,1)S(1)}, u32[]{:S(2)}, u32[]{:S(2)}) collective-permute-start(bf16[256,128]{1,0:T(8,128)(2,1)S(1)} %get-tuple-element.22), channel_id=1, source_target_pairs={{0,2},{1,3},{2,0},{3,1},{4,6},{5,7},{6,4},{7,5},{8,10},{9,11},{10,... | collective-permute-start | bytes 196616 | tf_op jit(solution)/shard_map/ppermute | solution.py:186
  14.7 5.8 %collective-permute-start.5 = (bf16[256,128]{1,0:T(8,128)(2,1)S(1)}, bf16[256,128]{1,0:T(8,128)(2,1)S(1)}, u32[]{:S(2)}, u32[]{:S(2)}) collective-permute-start(bf16[256,128]{1,0:T(8,128)(2,1)S(1)} %add_convert_fusion.1.refs_0_), channel_id=1, source_target_pairs={{0,12},{4,0},{8,4},{12,8},{1,13},{5,1},{9,5},{13,9},{2,14},{6,2},{... | collective-permute-start | bytes 196616 | tf_op jit(solution)/shard_map/ppermute | solution.py:190
  18.6 5.2 %collective-permute-start.4 = (bf16[256,128]{1,0:T(8,128)(2,1)S(1)}, bf16[256,128]{1,0:T(8,128)(2,1)S(1)}, u32[]{:S(2)}, u32[]{:S(2)}) collective-permute-start(bf16[256,128]{1,0:T(8,128)(2,1)S(1)} %add_convert_fusion.1.refs_0_), channel_id=1, source_target_pairs={{0,8},{4,12},{8,0},{12,4},{1,9},{5,13},{9,1},{13,5},{2,10},{6,14},... | collective-permute-start | bytes 196616 | tf_op jit(solution)/shard_map/ppermute | solution.py:190
  18.6 6.1 %collective-permute-start.3 = (bf16[256,128]{1,0:T(8,128)(2,1)S(1)}, bf16[256,128]{1,0:T(8,128)(2,1)S(1)}, u32[]{:S(2)}, u32[]{:S(2)}) collective-permute-start(bf16[256,128]{1,0:T(8,128)(2,1)S(1)} %add_convert_fusion.1.refs_0_), channel_id=1, source_target_pairs={{0,4},{4,8},{8,12},{12,0},{1,5},{5,9},{9,13},{13,1},{2,6},{6,10},{... | collective-permute-start | bytes 196616 | tf_op jit(solution)/shard_map/ppermute | solution.py:190
  25.1 4.3 %collective-permute-start.6 = (bf16[256,128]{1,0:T(8,128)(2,1)S(1)}, bf16[256,128]{1,0:T(8,128)(2,1)S(1)}, u32[]{:S(2)}, u32[]{:S(2)}) collective-permute-start(bf16[256,128]{1,0:T(8,128)(2,1)S(1)} %get-tuple-element.24), channel_id=1, source_target_pairs={{0,2},{1,3},{2,0},{3,1},{4,6},{5,7},{6,4},{7,5},{8,10},{9,11},{10,... | collective-permute-start | bytes 196616 | tf_op jit(solution)/shard_map/ppermute | solution.py:186
  29.5 5.0 %collective-permute-start.9 = (bf16[256,128]{1,0:T(8,128)(2,1)S(1)}, bf16[256,128]{1,0:T(8,128)(2,1)S(1)}, u32[]{:S(2)}, u32[]{:S(2)}) collective-permute-start(bf16[256,128]{1,0:T(8,128)(2,1)S(1)} %add_convert_fusion.refs_0_), channel_id=1, source_target_pairs={{0,12},{4,0},{8,4},{12,8},{1,13},{5,1},{9,5},{13,9},{2,14},{6,2},{... | collective-permute-start | bytes 196616 | tf_op jit(solution)/shard_map/ppermute | solution.py:190
  31.1 6.4 %collective-permute-start.8 = (bf16[256,128]{1,0:T(8,128)(2,1)S(1)}, bf16[256,128]{1,0:T(8,128)(2,1)S(1)}, u32[]{:S(2)}, u32[]{:S(2)}) collective-permute-start(bf16[256,128]{1,0:T(8,128)(2,1)S(1)} %add_convert_fusion.refs_0_), channel_id=1, source_target_pairs={{0,8},{4,12},{8,0},{12,4},{1,9},{5,13},{9,1},{13,5},{2,10},{6,14},... | collective-permute-start | bytes 196616 | tf_op jit(solution)/shard_map/ppermute | solution.py:190
  31.1 6.4 %collective-permute-start.7 = (bf16[256,128]{1,0:T(8,128)(2,1)S(1)}, bf16[256,128]{1,0:T(8,128)(2,1)S(1)}, u32[]{:S(2)}, u32[]{:S(2)}) collective-permute-start(bf16[256,128]{1,0:T(8,128)(2,1)S(1)} %add_convert_fusion.refs_0_), channel_id=1, source_target_pairs={{0,4},{4,8},{8,12},{12,0},{1,5},{5,9},{9,13},{13,1},{2,6},{6,10},{... | collective-permute-start | bytes 196616 | tf_op jit(solution)/shard_map/ppermute | solution.py:190
  38.0 5.0 %collective-permute-start.10 = (f32[128,128]{1,0:T(8,128)S(1)}, f32[128,128]{1,0:T(8,128)S(1)}, u32[]{:S(2)}, u32[]{:S(2)}) collective-permute-start(f32[128,128]{1,0:T(8,128)S(1)} %get-tuple-element.26), channel_id=1, source_target_pairs={{0,1},{1,0},{2,3},{3,2},{4,5},{5,4},{6,7},{7,6},{8,9},{9,8},{10,11... | collective-permute-start | bytes 196616 | tf_op jit(solution)/shard_map/ppermute | solution.py:186
  38.1 4.0 %collective-permute-start.11 = (bf16[128,128]{1,0:T(8,128)(2,1)S(1)}, bf16[128,128]{1,0:T(8,128)(2,1)S(1)}, u32[]{:S(2)}, u32[]{:S(2)}) collective-permute-start(bf16[128,128]{1,0:T(8,128)(2,1)S(1)} %get-tuple-element.27), channel_id=1, source_target_pairs={{0,2},{1,3},{2,0},{3,1},{4,6},{5,7},{6,4},{7,5},{8,10},{9,11},{10,... | collective-permute-start | bytes 98312 | tf_op jit(solution)/shard_map/ppermute | solution.py:186
  39.7 3.3 %collective-permute-start.12 = (bf16[128,128]{1,0:T(8,128)(2,1)S(1)}, bf16[128,128]{1,0:T(8,128)(2,1)S(1)}, u32[]{:S(2)}, u32[]{:S(2)}) collective-permute-start(bf16[128,128]{1,0:T(8,128)(2,1)S(1)} %get-tuple-element.28), channel_id=1, source_target_pairs={{0,3},{1,2},{2,1},{3,0},{4,7},{5,6},{6,5},{7,4},{8,11},{9,10},{10,... | collective-permute-start | bytes 98312 | tf_op jit(solution)/shard_map/ppermute | solution.py:186

commit v2 on v1

--- a/solution.py
+++ b/solution.py
@@ -15,7 +15,6 @@
 damping = 0.85
 
 VMEM = pl.BlockSpec(memory_space=pltpu.VMEM)
-SMEM = pl.BlockSpec(memory_space=pltpu.SMEM)
 HBM = pl.BlockSpec(memory_space=pltpu.HBM)
 MIB = 1 << 20
 
@@ -42,30 +41,30 @@
 
 
 def first_kernel(
-    steps, columns, scale, tiles, dest, count, seeds,
-    dense, keep, send, seed_rows, tile_buf, seed_buf, total, ids, weights, tile_sem, seed_sem,
+    steps, columns, scale, tiles_hbm, dest_hbm, count_hbm, seeds_hbm,
+    dense, keep, send, seed_rows,
+    tiles, dest, count, seeds, total, ids, weights, tile_sem, table_sem,
 ):
-    slots, edge = tile_buf.shape[1], tile_buf.shape[2]
-    topics = seed_buf.shape[1]
+    slots, edge = tiles.shape[1], tiles.shape[2]
+    topics = seeds.shape[1] // CORES
     row, chip, core = place()
     col = chip * CORES + core
-    fetch_seeds = [
-        pltpu.make_async_copy(
-            seeds.at[pl.ds(lax.rem(core + h, CORES) * topics, topics), :], seed_buf.at[h], seed_sem.at[h]
-        )
-        for h in range(CORES)
+    tables = [(seeds_hbm, seeds), (dest_hbm, dest), (count_hbm, count)]
+    fetch_tables = [
+        pltpu.make_async_copy(source, table, table_sem.at[i]) for i, (source, table) in enumerate(tables)
     ]
     fetch_tiles = [
-        pltpu.make_async_copy(tiles.at[0, 0, s], tile_buf.at[s], tile_sem.at[s]) for s in range(steps)
-    ]
-    for fetch in fetch_seeds + fetch_tiles:
+        pltpu.make_async_copy(tiles_hbm.at[0, 0, s], tiles.at[s], tile_sem.at[s]) for s in range(steps)
+    ]
+    for fetch in fetch_tables + fetch_tiles:
         fetch.start()
 
     groups = -(-steps // PACKED)
     counts = []
+    fetch_tables[0].wait()
     for h in range(CORES):
-        fetch_seeds[h].wait()
-        hosts = seed_buf[h].astype(jnp.float32).T.astype(jnp.int32)
+        lanes = pl.ds(pl.multiple_of(lax.rem(core + h, CORES) * topics, topics), topics)
+        hosts = seeds[:, lanes]
         if h == 0:
             seed_rows[...] = hosts
         ids[h] = hosts & (edge - 1)
@@ -83,13 +82,15 @@
         for h in range(CORES)
     ]
 
+    for fetch in fetch_tables[1:]:
+        fetch.wait()
     for s in range(steps):
         fetch_tiles[s].wait()
         total[...] = jnp.zeros_like(total)
 
         def add_tile(t, carry):
             rows = pl.ds(pl.multiple_of(dest[0, 0, s, t] * edge, edge), edge)
-            total[rows, :] += tile_buf[s, t].astype(jnp.float32)
+            total[rows, :] += tiles[s, t].astype(jnp.float32)
             return carry
 
         lax.fori_loop(0, count[0, 0, s], add_tile, 0)
@@ -128,7 +129,7 @@
 
 def gathered(scores, core, edge):
     return [
-        jnp.concatenate([s[pl.ds(pl.multiple_of(c * edge, edge), edge), :] for s in scores], axis=0)
+        jnp.concatenate([s[pl.ds(pl.multiple_of(c * edge, edge), edge), :] for s in scores[::-1]], axis=0)
         for c in (core, 1 - core)
     ]
 
@@ -216,7 +217,7 @@
     matrix = 2 * dests * sources
     dense, keep, send, seed_rows = call(
         functools.partial(first_kernel, steps, columns, scale),
-        [HBM, SMEM, SMEM, HBM],
+        [HBM] * 4,
         [
             shape(bf16, dests, sources),
             shape(f32, dests, topics),
@@ -226,14 +227,16 @@
         6 * MIB + 2 * matrix + 2 * steps * slots * edge * edge,
         [
             pltpu.VMEM((steps, slots, edge, edge), bf16),
-            pltpu.VMEM((CORES, topics, seeds), i32),
+            pltpu.SMEM(tile_dest.shape, i32),
+            pltpu.SMEM(tile_count.shape, i32),
+            pltpu.VMEM((seeds, CORES * topics), i32),
             pltpu.VMEM((dests, edge), f32),
             pltpu.VMEM((CORES, seeds, topics), i32),
             pltpu.VMEM((CORES, groups, seeds, topics), i32),
             pltpu.SemaphoreType.DMA((steps,)),
-            pltpu.SemaphoreType.DMA((CORES,)),
+            pltpu.SemaphoreType.DMA((3,)),
         ],
-    )(tiles, tile_dest, tile_count, topic_seeds)
+    )(*(pltpu.with_memory_space_constraint(a, pltpu.HBM) for a in (tiles, tile_dest, tile_count, topic_seeds.T)))
     (restart,) = call(
         functools.partial(restart_kernel, columns, scale),
         [VMEM],
@@ -258,7 +261,7 @@
         for d in range(1, chips):
             total = total + from_col(parts[d], chips, d, 0).astype(f32)
         sent = (damping * total + restart).astype(bf16)
-        gather = [sent] + [from_blk(sent, steps, d) for d in range(1, steps)]
+        gather = [from_blk(sent, steps, d) for d in range(steps - 1, 0, -1)] + [sent]
         if iteration == ITERS - 2:
             break
     parts = call(

time: 44 us -> 39.1 us (0.89)
  local copies, waits for them, and re-layouts: 3.58 us -> 0 us
  waiting for transfers between devices: 19 us -> 16.8 us
  starting transfers between devices: 15.5 us -> 16.8 us
    unnamed x7 -> x0, local copies, waits for them, and re-layouts: 3.58 us -> none
    ppermute x6, waiting for transfers between devices: 9.7 us -> 7.65 us  [from_blk(): lax.ppermute(value, 'blk', [(i, (i + distance) % steps) for i in range(st...]
    ppermute x6, starting transfers between devices: 8.39 us -> 9.56 us  [from_blk(): lax.ppermute(value, 'blk', [(i, (i + distance) % steps) for i in range(st...]
  transfers between devices with their start and end apart: 13 -> 13, of which waited for: 10 -> 11; matrix products, arithmetic and copies ran while one was open for 0% -> 0% of each run, Pallas kernels for 1% -> 1%
where the time goes in v2:
time: 39.1 us; the launch traced here: 39 us
  starting transfers between devices  16.8 us (43%)
  waiting for transfers between devices  16.8 us (43%)
  Pallas kernels  5.34 us (14%)
    ppermute x6, starting transfers between devices, from_blk(): lax.ppermute(value, 'blk', [(i, (i + distance) % steps) for i in range(st...  9.56 us
    ppermute x7, waiting for transfers between devices, from_col(): return lax.ppermute(value, 'col', route)  9.11 us
    ppermute x6, waiting for transfers between devices, from_blk(): lax.ppermute(value, 'blk', [(i, (i + distance) % steps) for i in range(st...  7.65 us
    ppermute x7, starting transfers between devices, from_col(): return lax.ppermute(value, 'col', route)  7.24 us
    pallas_call x1, Pallas kernels, body(): call(functools.partial(first_kernel, steps, columns, scale), [HBM] * 4, [...  3.28 us
  transfers between devices with their start and end apart: 13, of which 11 were waited for; matrix products, arithmetic and copies ran while one was open for 0% of the time, Pallas kernels for 1%

profile of v2, /device:TPU:0, one launch (start us, length us, event | category | flops | bytes accessed | tf_op | source)
XLA Modules:
  0.0 39.0 jit_solution(17750063720770504980)
XLA Ops:
  0.0 3.3 %shard_map.46 = (bf16[512,512]{1,0:T(8,128)(2,1)S(1)}, f32[512,128]{1,0:T(8,128)S(1)}, bf16[512,128]{1,0:T(8,128)(2,1)S(1)}, s32[64,128]{1,0:T(8,128)S(1)}) custom-call(bf16[1,1,4,10,128,128]{5,4,3,2,1,0:T(8,128)(2,1)} %tiles_hbm.1, s32[1,1,4,10]{3,2,1,0:T(4,128)} %dest_hbm.1, s32[1,1,4]{2,1,0:T(1,128)} %count_hbm.1, s32[64,256]{1,0:T(8,128)} %bitcast.1), custom_call_target="tpu_custom_call" | custom-call | tf_op jit(solution)/shard_map/pallas_call | solution.py:218
  3.3 0.5 %collective-permute-start = (bf16[512,512]{1,0:T(8,128)(2,1)S(1)}, bf16[512,512]{1,0:T(8,128)(2,1)S(1)}, u32[]{:S(2)}, u32[]{:S(2)}) collective-permute-start(bf16[512,512]{1,0:T(8,128)(2,1)S(1)} %get-tuple-element.17.own), channel_id=1, source_target_pairs={{0,1},{1,0},{2,3},{3,2},{4,5},{5,4},{6,7},{7,6},{8,9},{9,8},{10,11... | collective-permute-start | bytes 1572872 | tf_op jit(solution)/shard_map/ppermute | solution.py:187
  3.8 0.1 collective-permute-start.1
  3.9 1.6 %collective-permute-done.1.recv = bf16[512,128]{1,0:T(8,128)(2,1)S(1)} collective-permute-done((bf16[512,128]{1,0:T(8,128)(2,1)S(1)}, bf16[512,128]{1,0:T(8,128)(2,1)S(1)}, u32[]{:S(2)}, u32[]{:S(2)}) %collective-permute-start.1) | collective-permute-done | bytes 131104 | tf_op jit(solution)/shard_map/ppermute | solution.py:187
  5.6 2.9 %collective-permute-start.2 = (bf16[256,128]{1,0:T(8,128)(2,1)S(1)}, bf16[256,128]{1,0:T(8,128)(2,1)S(1)}, u32[]{:S(2)}, u32[]{:S(2)}) collective-permute-start(bf16[256,128]{1,0:T(8,128)(2,1)S(1)} %get-tuple-element.22), channel_id=1, source_target_pairs={{0,2},{1,3},{2,0},{3,1},{4,6},{5,7},{6,4},{7,5},{8,10},{9,11},{10,... | collective-permute-start | bytes 196616 | tf_op jit(solution)/shard_map/ppermute | solution.py:187
  8.5 0.5 %shard_map.47.restart = f32[256,128]{1,0:T(8,128)S(1)} custom-call(s32[64,128]{1,0:T(8,128)S(1)} %get-tuple-element.18.seed_rows), custom_call_target="tpu_custom_call" | custom-call | tf_op jit(solution)/shard_map/pallas_call | solution.py:240
  9.0 1.9 %collective-permute-done.2 = bf16[256,128]{1,0:T(8,128)(2,1)S(1)} collective-permute-done((bf16[256,128]{1,0:T(8,128)(2,1)S(1)}, bf16[256,128]{1,0:T(8,128)(2,1)S(1)}, u32[]{:S(2)}, u32[]{:S(2)}) %collective-permute-start.2) | collective-permute-done | bytes 65568 | tf_op jit(solution)/shard_map/ppermute | solution.py:187
  10.9 1.8 %collective-permute-start.5 = (bf16[256,128]{1,0:T(8,128)(2,1)S(1)}, bf16[256,128]{1,0:T(8,128)(2,1)S(1)}, u32[]{:S(2)}, u32[]{:S(2)}) collective-permute-start(bf16[256,128]{1,0:T(8,128)(2,1)S(1)} %add_convert_fusion.1.refs_3_), channel_id=1, source_target_pairs={{0,4},{4,8},{8,12},{12,0},{1,5},{5,9},{9,13},{13,1},{2,6},{6,10},{... | collective-permute-start | bytes 196616 | tf_op jit(solution)/shard_map/ppermute | solution.py:191
  12.7 2.6 %collective-permute-start.4 = (bf16[256,128]{1,0:T(8,128)(2,1)S(1)}, bf16[256,128]{1,0:T(8,128)(2,1)S(1)}, u32[]{:S(2)}, u32[]{:S(2)}) collective-permute-start(bf16[256,128]{1,0:T(8,128)(2,1)S(1)} %add_convert_fusion.1.refs_3_), channel_id=1, source_target_pairs={{0,8},{4,12},{8,0},{12,4},{1,9},{5,13},{9,1},{13,5},{2,10},{6,14},... | collective-permute-start | bytes 196616 | tf_op jit(solution)/shard_map/ppermute | solution.py:191
  15.3 1.3 %collective-permute-start.3 = (bf16[256,128]{1,0:T(8,128)(2,1)S(1)}, bf16[256,128]{1,0:T(8,128)(2,1)S(1)}, u32[]{:S(2)}, u32[]{:S(2)}) collective-permute-start(bf16[256,128]{1,0:T(8,128)(2,1)S(1)} %add_convert_fusion.1.refs_3_), channel_id=1, source_target_pairs={{0,12},{4,0},{8,4},{12,8},{1,13},{5,1},{9,5},{13,9},{2,14},{6,2},{... | collective-permute-start | bytes 196616 | tf_op jit(solution)/shard_map/ppermute | solution.py:191
  16.6 1.1 %collective-permute-done.5.refs_2_ = bf16[256,128]{1,0:T(8,128)(2,1)S(1)} collective-permute-done((bf16[256,128]{1,0:T(8,128)(2,1)S(1)}, bf16[256,128]{1,0:T(8,128)(2,1)S(1)}, u32[]{:S(2)}, u32[]{:S(2)}) %collective-permute-start.5) | collective-permute-done | bytes 65568 | tf_op jit(solution)/shard_map/ppermute | solution.py:191
  17.7 1.9 %collective-permute-done.4.refs_1_ = bf16[256,128]{1,0:T(8,128)(2,1)S(1)} collective-permute-done((bf16[256,128]{1,0:T(8,128)(2,1)S(1)}, bf16[256,128]{1,0:T(8,128)(2,1)S(1)}, u32[]{:S(2)}, u32[]{:S(2)}) %collective-permute-start.4) | collective-permute-done | bytes 65568 | tf_op jit(solution)/shard_map/ppermute | solution.py:191
  19.6 0.3 collective-permute-done.3.refs_0_
  19.9 0.0 collective-permute-done.other
  19.9 0.4 %shard_map.49 = (f32[256,128]{1,0:T(8,128)S(1)}, bf16[256,128]{1,0:T(8,128)(2,1)S(1)}) custom-call(bf16[512,512]{1,0:T(8,128)(2,1)S(1)} %get-tuple-element.17.own, bf16[512,512]{1,0:T(8,128)(2,1)S(1)} %collective-permute-done.other, bf16[256,128]{1,0:T(8,128)(2,1)S(1)} %collective-permute-done.3.refs_0_, ...), custom_call_target="tpu_custom_call" | custom-call | tf_op jit(solution)/shard_map/pallas_call | solution.py:254
  20.3 1.8 %collective-permute-start.6 = (bf16[256,128]{1,0:T(8,128)(2,1)S(1)}, bf16[256,128]{1,0:T(8,128)(2,1)S(1)}, u32[]{:S(2)}, u32[]{:S(2)}) collective-permute-start(bf16[256,128]{1,0:T(8,128)(2,1)S(1)} %get-tuple-element.24), channel_id=1, source_target_pairs={{0,2},{1,3},{2,0},{3,1},{4,6},{5,7},{6,4},{7,5},{8,10},{9,11},{10,... | collective-permute-start | bytes 196616 | tf_op jit(solution)/shard_map/ppermute | solution.py:187
  22.1 2.5 %collective-permute-done.6 = bf16[256,128]{1,0:T(8,128)(2,1)S(1)} collective-permute-done((bf16[256,128]{1,0:T(8,128)(2,1)S(1)}, bf16[256,128]{1,0:T(8,128)(2,1)S(1)}, u32[]{:S(2)}, u32[]{:S(2)}) %collective-permute-start.6) | collective-permute-done | bytes 65568 | tf_op jit(solution)/shard_map/ppermute | solution.py:187
  24.7 1.3 %collective-permute-start.9 = (bf16[256,128]{1,0:T(8,128)(2,1)S(1)}, bf16[256,128]{1,0:T(8,128)(2,1)S(1)}, u32[]{:S(2)}, u32[]{:S(2)}) collective-permute-start(bf16[256,128]{1,0:T(8,128)(2,1)S(1)} %add_convert_fusion.refs_3_), channel_id=1, source_target_pairs={{0,4},{4,8},{8,12},{12,0},{1,5},{5,9},{9,13},{13,1},{2,6},{6,10},{... | collective-permute-start | bytes 196616 | tf_op jit(solution)/shard_map/ppermute | solution.py:191
  26.0 2.1 %collective-permute-start.8 = (bf16[256,128]{1,0:T(8,128)(2,1)S(1)}, bf16[256,128]{1,0:T(8,128)(2,1)S(1)}, u32[]{:S(2)}, u32[]{:S(2)}) collective-permute-start(bf16[256,128]{1,0:T(8,128)(2,1)S(1)} %add_convert_fusion.refs_3_), channel_id=1, source_target_pairs={{0,8},{4,12},{8,0},{12,4},{1,9},{5,13},{9,1},{13,5},{2,10},{6,14},... | collective-permute-start | bytes 196616 | tf_op jit(solution)/shard_map/ppermute | solution.py:191
  28.1 0.5 %collective-permute-start.7 = (bf16[256,128]{1,0:T(8,128)(2,1)S(1)}, bf16[256,128]{1,0:T(8,128)(2,1)S(1)}, u32[]{:S(2)}, u32[]{:S(2)}) collective-permute-start(bf16[256,128]{1,0:T(8,128)(2,1)S(1)} %add_convert_fusion.refs_3_), channel_id=1, source_target_pairs={{0,12},{4,0},{8,4},{12,8},{1,13},{5,1},{9,5},{13,9},{2,14},{6,2},{... | collective-permute-start | bytes 196616 | tf_op jit(solution)/shard_map/ppermute | solution.py:191
  28.6 2.3 %collective-permute-done.9.refs_2_ = bf16[256,128]{1,0:T(8,128)(2,1)S(1)} collective-permute-done((bf16[256,128]{1,0:T(8,128)(2,1)S(1)}, bf16[256,128]{1,0:T(8,128)(2,1)S(1)}, u32[]{:S(2)}, u32[]{:S(2)}) %collective-permute-start.9) | collective-permute-done | bytes 65568 | tf_op jit(solution)/shard_map/ppermute | solution.py:191
  30.8 1.4 %collective-permute-done.8.refs_1_ = bf16[256,128]{1,0:T(8,128)(2,1)S(1)} collective-permute-done((bf16[256,128]{1,0:T(8,128)(2,1)S(1)}, bf16[256,128]{1,0:T(8,128)(2,1)S(1)}, u32[]{:S(2)}, u32[]{:S(2)}) %collective-permute-start.8) | collective-permute-done | bytes 65568 | tf_op jit(solution)/shard_map/ppermute | solution.py:191
  32.3 0.6 %collective-permute-done.7.refs_0_ = bf16[256,128]{1,0:T(8,128)(2,1)S(1)} collective-permute-done((bf16[256,128]{1,0:T(8,128)(2,1)S(1)}, bf16[256,128]{1,0:T(8,128)(2,1)S(1)}, u32[]{:S(2)}, u32[]{:S(2)}) %collective-permute-start.7) | collective-permute-done | bytes 65568 | tf_op jit(solution)/shard_map/ppermute | solution.py:191
  32.9 0.4 %shard_map.50 = (f32[128,128]{1,0:T(8,128)S(1)}, f32[128,128]{1,0:T(8,128)S(1)}, bf16[128,128]{1,0:T(8,128)(2,1)S(1)}, bf16[128,128]{1,0:T(8,128)(2,1)S(1)}) custom-call(bf16[512,512]{1,0:T(8,128)(2,1)S(1)} %get-tuple-element.17.own, bf16[512,512]{1,0:T(8,128)(2,1)S(1)} %collective-permute-done.other, f32[256,128]{1,0:T(8,128)S(1)} %shard_map.47.restart, ...), custom_call_target="tpu_custom_call" | custom-call | tf_op jit(solution)/shard_map/pallas_call | solution.py:267
  33.3 0.1 collective-permute-start.10
  33.4 1.5 %collective-permute-start.11 = (bf16[128,128]{1,0:T(8,128)(2,1)S(1)}, bf16[128,128]{1,0:T(8,128)(2,1)S(1)}, u32[]{:S(2)}, u32[]{:S(2)}) collective-permute-start(bf16[128,128]{1,0:T(8,128)(2,1)S(1)} %get-tuple-element.27), channel_id=1, source_target_pairs={{0,2},{1,3},{2,0},{3,1},{4,6},{5,7},{6,4},{7,5},{8,10},{9,11},{10,... | collective-permute-start | bytes 98312 | tf_op jit(solution)/shard_map/ppermute | solution.py:187
  35.0 0.3 collective-permute-start.12
  35.3 2.1 %collective-permute-done.11.refs_2_ = bf16[128,128]{1,0:T(8,128)(2,1)S(1)} collective-permute-done((bf16[128,128]{1,0:T(8,128)(2,1)S(1)}, bf16[128,128]{1,0:T(8,128)(2,1)S(1)}, u32[]{:S(2)}, u32[]{:S(2)}) %collective-permute-start.11) | collective-permute-done | bytes 32800 | tf_op jit(solution)/shard_map/ppermute | solution.py:187
  37.4 0.9 %collective-permute-done.12.refs_3_ = bf16[128,128]{1,0:T(8,128)(2,1)S(1)} collective-permute-done((bf16[128,128]{1,0:T(8,128)(2,1)S(1)}, bf16[128,128]{1,0:T(8,128)(2,1)S(1)}, u32[]{:S(2)}, u32[]{:S(2)}) %collective-permute-start.12) | collective-permute-done | bytes 32800 | tf_op jit(solution)/shard_map/ppermute | solution.py:187
  38.3 0.0 collective-permute-done.10.refs_1_
  38.3 0.7 %shard_map.51 = f32[128,256]{1,0:T(8,128)} custom-call(f32[128,128]{1,0:T(8,128)S(1)} %get-tuple-element.25.refs_0_, f32[128,128]{1,0:T(8,128)S(1)} %collective-permute-done.10.refs_1_, bf16[128,128]{1,0:T(8,128)(2,1)S(1)} %collective-permute-done.11.refs_2_, bf16[128,128]{1,0:T(8,128)(2,1)S(1)} %collective-permute-done.12.refs_3_), custom_call_target="tpu_custom_call" | custom-call | tf_op jit(solution)/shard_map/pallas_call | solution.py:277
  (3 shorter events, 0.1 us)
Async XLA Ops:
  3.3 16.6 %collective-permute-start = (bf16[512,512]{1,0:T(8,128)(2,1)S(1)}, bf16[512,512]{1,0:T(8,128)(2,1)S(1)}, u32[]{:S(2)}, u32[]{:S(2)}) collective-permute-start(bf16[512,512]{1,0:T(8,128)(2,1)S(1)} %get-tuple-element.17.own), channel_id=1, source_target_pairs={{0,1},{1,0},{2,3},{3,2},{4,5},{5,4},{6,7},{7,6},{8,9},{9,8},{10,11... | collective-permute-start | bytes 1572872 | tf_op jit(solution)/shard_map/ppermute | solution.py:187
  3.8 1.7 %collective-permute-start.1 = (bf16[512,128]{1,0:T(8,128)(2,1)S(1)}, bf16[512,128]{1,0:T(8,128)(2,1)S(1)}, u32[]{:S(2)}, u32[]{:S(2)}) collective-permute-start(bf16[512,128]{1,0:T(8,128)(2,1)S(1)} %get-tuple-element.20), channel_id=1, source_target_pairs={{0,1},{1,0},{2,3},{3,2},{4,5},{5,4},{6,7},{7,6},{8,9},{9,8},{10,11... | collective-permute-start | bytes 393224 | tf_op jit(solution)/shard_map/ppermute | solution.py:187
  5.6 5.3 %collective-permute-start.2 = (bf16[256,128]{1,0:T(8,128)(2,1)S(1)}, bf16[256,128]{1,0:T(8,128)(2,1)S(1)}, u32[]{:S(2)}, u32[]{:S(2)}) collective-permute-start(bf16[256,128]{1,0:T(8,128)(2,1)S(1)} %get-tuple-element.22), channel_id=1, source_target_pairs={{0,2},{1,3},{2,0},{3,1},{4,6},{5,7},{6,4},{7,5},{8,10},{9,11},{10,... | collective-permute-start | bytes 196616 | tf_op jit(solution)/shard_map/ppermute | solution.py:187
  10.9 6.8 %collective-permute-start.5 = (bf16[256,128]{1,0:T(8,128)(2,1)S(1)}, bf16[256,128]{1,0:T(8,128)(2,1)S(1)}, u32[]{:S(2)}, u32[]{:S(2)}) collective-permute-start(bf16[256,128]{1,0:T(8,128)(2,1)S(1)} %add_convert_fusion.1.refs_3_), channel_id=1, source_target_pairs={{0,4},{4,8},{8,12},{12,0},{1,5},{5,9},{9,13},{13,1},{2,6},{6,10},{... | collective-permute-start | bytes 196616 | tf_op jit(solution)/shard_map/ppermute | solution.py:191
  12.7 6.9 %collective-permute-start.4 = (bf16[256,128]{1,0:T(8,128)(2,1)S(1)}, bf16[256,128]{1,0:T(8,128)(2,1)S(1)}, u32[]{:S(2)}, u32[]{:S(2)}) collective-permute-start(bf16[256,128]{1,0:T(8,128)(2,1)S(1)} %add_convert_fusion.1.refs_3_), channel_id=1, source_target_pairs={{0,8},{4,12},{8,0},{12,4},{1,9},{5,13},{9,1},{13,5},{2,10},{6,14},... | collective-permute-start | bytes 196616 | tf_op jit(solution)/shard_map/ppermute | solution.py:191
  15.3 4.6 %collective-permute-start.3 = (bf16[256,128]{1,0:T(8,128)(2,1)S(1)}, bf16[256,128]{1,0:T(8,128)(2,1)S(1)}, u32[]{:S(2)}, u32[]{:S(2)}) collective-permute-start(bf16[256,128]{1,0:T(8,128)(2,1)S(1)} %add_convert_fusion.1.refs_3_), channel_id=1, source_target_pairs={{0,12},{4,0},{8,4},{12,8},{1,13},{5,1},{9,5},{13,9},{2,14},{6,2},{... | collective-permute-start | bytes 196616 | tf_op jit(solution)/shard_map/ppermute | solution.py:191
  20.3 4.3 %collective-permute-start.6 = (bf16[256,128]{1,0:T(8,128)(2,1)S(1)}, bf16[256,128]{1,0:T(8,128)(2,1)S(1)}, u32[]{:S(2)}, u32[]{:S(2)}) collective-permute-start(bf16[256,128]{1,0:T(8,128)(2,1)S(1)} %get-tuple-element.24), channel_id=1, source_target_pairs={{0,2},{1,3},{2,0},{3,1},{4,6},{5,7},{6,4},{7,5},{8,10},{9,11},{10,... | collective-permute-start | bytes 196616 | tf_op jit(solution)/shard_map/ppermute | solution.py:187
  24.7 6.2 %collective-permute-start.9 = (bf16[256,128]{1,0:T(8,128)(2,1)S(1)}, bf16[256,128]{1,0:T(8,128)(2,1)S(1)}, u32[]{:S(2)}, u32[]{:S(2)}) collective-permute-start(bf16[256,128]{1,0:T(8,128)(2,1)S(1)} %add_convert_fusion.refs_3_), channel_id=1, source_target_pairs={{0,4},{4,8},{8,12},{12,0},{1,5},{5,9},{9,13},{13,1},{2,6},{6,10},{... | collective-permute-start | bytes 196616 | tf_op jit(solution)/shard_map/ppermute | solution.py:191
  26.0 6.3 %collective-permute-start.8 = (bf16[256,128]{1,0:T(8,128)(2,1)S(1)}, bf16[256,128]{1,0:T(8,128)(2,1)S(1)}, u32[]{:S(2)}, u32[]{:S(2)}) collective-permute-start(bf16[256,128]{1,0:T(8,128)(2,1)S(1)} %add_convert_fusion.refs_3_), channel_id=1, source_target_pairs={{0,8},{4,12},{8,0},{12,4},{1,9},{5,13},{9,1},{13,5},{2,10},{6,14},... | collective-permute-start | bytes 196616 | tf_op jit(solution)/shard_map/ppermute | solution.py:191
  28.1 4.8 %collective-permute-start.7 = (bf16[256,128]{1,0:T(8,128)(2,1)S(1)}, bf16[256,128]{1,0:T(8,128)(2,1)S(1)}, u32[]{:S(2)}, u32[]{:S(2)}) collective-permute-start(bf16[256,128]{1,0:T(8,128)(2,1)S(1)} %add_convert_fusion.refs_3_), channel_id=1, source_target_pairs={{0,12},{4,0},{8,4},{12,8},{1,13},{5,1},{9,5},{13,9},{2,14},{6,2},{... | collective-permute-start | bytes 196616 | tf_op jit(solution)/shard_map/ppermute | solution.py:191
  33.3 5.0 %collective-permute-start.10 = (f32[128,128]{1,0:T(8,128)S(1)}, f32[128,128]{1,0:T(8,128)S(1)}, u32[]{:S(2)}, u32[]{:S(2)}) collective-permute-start(f32[128,128]{1,0:T(8,128)S(1)} %get-tuple-element.26), channel_id=1, source_target_pairs={{0,1},{1,0},{2,3},{3,2},{4,5},{5,4},{6,7},{7,6},{8,9},{9,8},{10,11... | collective-permute-start | bytes 196616 | tf_op jit(solution)/shard_map/ppermute | solution.py:187
  33.4 4.0 %collective-permute-start.11 = (bf16[128,128]{1,0:T(8,128)(2,1)S(1)}, bf16[128,128]{1,0:T(8,128)(2,1)S(1)}, u32[]{:S(2)}, u32[]{:S(2)}) collective-permute-start(bf16[128,128]{1,0:T(8,128)(2,1)S(1)} %get-tuple-element.27), channel_id=1, source_target_pairs={{0,2},{1,3},{2,0},{3,1},{4,6},{5,7},{6,4},{7,5},{8,10},{9,11},{10,... | collective-permute-start | bytes 98312 | tf_op jit(solution)/shard_map/ppermute | solution.py:187
  35.0 3.3 %collective-permute-start.12 = (bf16[128,128]{1,0:T(8,128)(2,1)S(1)}, bf16[128,128]{1,0:T(8,128)(2,1)S(1)}, u32[]{:S(2)}, u32[]{:S(2)}) collective-permute-start(bf16[128,128]{1,0:T(8,128)(2,1)S(1)} %get-tuple-element.28), channel_id=1, source_target_pairs={{0,3},{1,2},{2,1},{3,0},{4,7},{5,6},{6,5},{7,4},{8,11},{9,10},{10,... | collective-permute-start | bytes 98312 | tf_op jit(solution)/shard_map/ppermute | solution.py:187

commit v3 on v2

v3 whole, which is shorter than its diff:
```python
import functools

import jax
import jax.numpy as jnp
from jax import lax
from jax.experimental import pallas as pl
from jax.experimental.pallas import tpu as pltpu
from jax.sharding import PartitionSpec as P

ITERS = 3
CORES = 2
FIELD = 8
PACKED = 4

damping = 0.85

VMEM = pl.BlockSpec(memory_space=pltpu.VMEM)
HBM = pl.BlockSpec(memory_space=pltpu.HBM)
MIB = 1 << 20


def place():
    col = lax.axis_index("col")
    return lax.axis_index("blk"), col // CORES, col % CORES


def add_seeds(counts, ids, weights, first, last):
    rows = lax.broadcasted_iota(jnp.int32, counts[0].shape, 0)
    for j in range(first, last):
        hit = rows == ids[j : j + 1, :]
        counts = [c + jnp.where(hit, weights[g, j : j + 1, :], 0) for g, c in enumerate(counts)]
    return counts


def field(packed, index):
    return ((packed >> (FIELD * index)) & ((1 << FIELD) - 1)).astype(jnp.float32)


def source_weights(hosts, edge, steps, columns, row, col, weights):
    block = hosts >> (edge.bit_length() - 1)
    step = lax.rem(row - block // columns + steps, steps)
    mine = lax.rem(block, columns) == col
    one = 1 << (FIELD * lax.rem(step, PACKED))
    for g in range(-(-steps // PACKED)):
        weights[g] = jnp.where(mine & (step // PACKED == g), one, 0)
    return block


def source_rows(counts, scale, steps):
    parts = [scale * field(counts[s // PACKED], s % PACKED) for s in range(steps)]
    return jnp.concatenate(parts, axis=0).astype(jnp.bfloat16)


def first_kernel(
    steps, columns, scale, tiles_hbm, dest_hbm, count_hbm, seeds_hbm,
    dense, send, seed_rows,
    tiles, dest, count, seeds, total, ids, weights, tile_sem, table_sem,
):
    slots, edge = tiles.shape[1], tiles.shape[2]
    topics = seeds.shape[1] // CORES
    row, chip, core = place()
    tables = [(seeds_hbm, seeds), (dest_hbm, dest), (count_hbm, count)]
    fetch_tables = [
        pltpu.make_async_copy(source, table, table_sem.at[i]) for i, (source, table) in enumerate(tables)
    ]
    fetch_tiles = [
        pltpu.make_async_copy(tiles_hbm.at[0, 0, s], tiles.at[s], tile_sem.at[s]) for s in range(steps)
    ]
    for fetch in fetch_tables + fetch_tiles:
        fetch.start()

    fetch_tables[0].wait()
    own, other = (
        seeds[:, pl.ds(pl.multiple_of(c * topics, topics), topics)] for c in (core, 1 - core)
    )
    seed_rows[...] = own
    ids[...] = other & (edge - 1)
    source_weights(other, edge, steps, columns, row, chip * CORES + core, weights)
    groups = weights.shape[0]
    counts = [jnp.zeros((edge, topics), jnp.int32)] * groups
    number, done = ids.shape[0], 0

    for fetch in fetch_tables[1:]:
        fetch.wait()
    for s in range(steps):
        upto = number * (steps + 1 + s) // (2 * steps)
        counts = add_seeds(counts, ids, weights, done, upto)
        done = upto
        fetch_tiles[s].wait()
        slot = s % total.shape[0]
        total[slot] = jnp.zeros(total.shape[1:], jnp.float32)
        for t in range(slots):
            block = jnp.where(t < count[0, 0, s], dest[0, 0, s, t], columns)
            rows = pl.ds(pl.multiple_of(block * edge, edge), edge)
            total[slot, rows, :] += tiles[s, t].astype(jnp.float32)
        dense[:, s * edge : (s + 1) * edge] = total[slot, : columns * edge, :].astype(jnp.bfloat16)

    restart = source_rows(counts, scale, steps)
    send[...] = jnp.dot(dense[...], restart, preferred_element_type=jnp.float32).astype(jnp.bfloat16)


def keep_kernel(steps, columns, scale, dense, seed_rows, keep, restart, restart_behind, ids, weights):
    edge = restart.shape[0] // CORES
    row, chip, core = place()
    hosts = seed_rows[...]
    ids[...] = hosts & (edge - 1)
    block = source_weights(hosts, edge, steps, columns, row, chip * CORES + core, weights)
    groups = weights.shape[0] - 1
    weights[groups] = jnp.zeros_like(hosts)
    for d in range(2):
        offset = block - lax.rem(row - d + steps, steps) * columns - chip * CORES
        for c in range(CORES):
            weights[groups] += jnp.where(offset == c, 1 << (FIELD * (d * CORES + c)), 0)
    counts = [jnp.zeros((edge, hosts.shape[1]), jnp.int32)] * (groups + 1)
    counts = add_seeds(counts, ids, weights, 0, ids.shape[0])
    for d, term in enumerate((restart, restart_behind)):
        for c in range(CORES):
            term[c * edge : (c + 1) * edge, :] = (1.0 - damping) * (
                scale * field(counts[groups], d * CORES + c)
            )
    rows = source_rows(counts, scale, steps)
    keep[...] = jnp.dot(dense[...], rows, preferred_element_type=jnp.float32)


def split_kernel(chips, keep, recv, mine, *sends):
    _, chip, _ = place()
    size = mine.shape[0]
    for d in range(chips):
        rows = pl.ds(pl.multiple_of(lax.rem(chip + d, chips) * size, size), size)
        part = keep[rows, :] + recv[rows, :].astype(jnp.float32)
        if d == 0:
            mine[...] = part
        sends[d][...] = part.astype(jnp.bfloat16)


def gathered(scores, core, edge):
    return [
        jnp.concatenate([s[pl.ds(pl.multiple_of(c * edge, edge), edge), :] for s in scores[::-1]], axis=0)
        for c in (core, 1 - core)
    ]


def product(matrices, sources, rows, first):
    lanes = pl.ds(first, sources[0].shape[0])
    return jnp.dot(
        jnp.concatenate([m[rows, lanes] for m in matrices], axis=1),
        jnp.concatenate(sources, axis=0),
        preferred_element_type=jnp.float32,
    )


def near_kernel(own, other, *refs):
    scores, out = refs[:-1], refs[-1]
    _, _, core = place()
    sources = gathered(scores, core, scores[0].shape[0] // CORES)
    out[...] = product((own, other), sources, slice(None), 0)


def step_kernel(chips, first, own, other, near, *refs):
    scores, mine, sends = refs[: -chips - 1], refs[-chips - 1], refs[-chips:]
    _, chip, core = place()
    size = mine.shape[0]
    sources = gathered(scores, core, size // CORES)
    for d in [*range(1, chips), 0]:
        rows = pl.ds(pl.multiple_of(lax.rem(chip + d, chips) * size, size), size)
        part = near[rows, :] + product((own, other), sources, rows, first)
        if d == 0:
            mine[...] = part
        sends[d][...] = part.astype(jnp.bfloat16)


def last_kernel(chips, first, own, other, near, restart, *refs):
    scores, parts = refs[: -chips * CORES], refs[-chips * CORES :]
    _, chip, core = place()
    edge = parts[0].shape[0]
    sources = gathered(scores, core, edge)
    for d in range(chips):
        for e in range(CORES):
            owner = lax.rem(core + e, CORES)
            block = lax.rem(chip + d, chips) * CORES + owner
            rows = pl.ds(pl.multiple_of(block * edge, edge), edge)
            part = near[rows, :] + product((own, other), sources, rows, first)
            if d == 0:
                rows = pl.ds(pl.multiple_of(owner * edge, edge), edge)
                part = damping * part + restart[rows, :]
            ref = parts[d * CORES + e]
            ref[...] = part.astype(ref.dtype)


def final_kernel(chips, *refs):
    parts, out = refs[:-1], refs[-1]
    _, _, core = place()
    topics = parts[0].shape[1]
    for e in range(CORES):
        total = sum(parts[d * CORES + e][...].astype(jnp.float32) for d in range(1, chips))
        lanes = pl.ds(pl.multiple_of(lax.rem(core + e, CORES) * topics, topics), topics)
        out[:, lanes] = parts[e][...] + damping * total


def from_col(value, chips, chip_step, core_step):
    route = [
        (x * CORES + c, (x + chip_step) % chips * CORES + (c + core_step) % CORES)
        for x in range(chips)
        for c in range(CORES)
    ]
    return lax.ppermute(value, "col", route)


def from_behind(value, steps, distance, chips=1, chip_step=0):
    if not chip_step:
        return lax.ppermute(value, "blk", [(i, (i + distance) % steps) for i in range(steps)])
    columns = chips * CORES
    route = [
        (i * columns + x * CORES + c, (i + distance) % steps * columns + (x + chip_step) % chips * CORES + c)
        for i in range(steps)
        for x in range(chips)
        for c in range(CORES)
    ]
    return lax.ppermute(value, ("blk", "col"), route)


def body(tiles, tile_dest, tile_count, topic_seeds):
    slots, edge = tiles.shape[3], tiles.shape[4]
    steps, columns = lax.axis_size("blk"), lax.axis_size("col")
    chips = columns // CORES
    topics, seeds = topic_seeds.shape[0] // CORES, topic_seeds.shape[1]
    dests, sources, pair = columns * edge, steps * edge, CORES * edge
    groups = -(-steps // PACKED)
    scale = steps * columns * edge / seeds
    f32, bf16, i32 = jnp.float32, jnp.bfloat16, jnp.int32

    def shape(dtype, *dims):
        return jax.ShapeDtypeStruct(dims, dtype)

    def call(kernel, in_specs, outs, room, scratch=()):
        return pl.pallas_call(
            kernel,
            in_specs=in_specs,
            out_shape=outs,
            out_specs=[VMEM] * len(outs),
            scratch_shapes=scratch,
            compiler_params=pltpu.CompilerParams(vmem_limit_bytes=room),
        )

    matrix = 2 * dests * sources
    dense, send, seed_rows = call(
        functools.partial(first_kernel, steps, columns, scale),
        [HBM] * 4,
        [shape(bf16, dests, sources), shape(bf16, dests, topics), shape(i32, seeds, topics)],
        6 * MIB + 2 * matrix + 2 * steps * slots * edge * edge,
        [
            pltpu.VMEM((steps, slots, edge, edge), bf16),
            pltpu.SMEM(tile_dest.shape, i32),
            pltpu.SMEM(tile_count.shape, i32),
            pltpu.VMEM((seeds, CORES * topics), i32),
            pltpu.VMEM((2, dests + edge, edge), f32),
            pltpu.VMEM((seeds, topics), i32),
            pltpu.VMEM((groups, seeds, topics), i32),
            pltpu.SemaphoreType.DMA((steps,)),
            pltpu.SemaphoreType.DMA((3,)),
        ],
    )(*(pltpu.with_memory_space_constraint(a, pltpu.HBM) for a in (tiles, tile_dest, tile_count, topic_seeds.T)))
    recv = from_col(send, chips, 0, 1)
    keep, restart, restart_behind = call(
        functools.partial(keep_kernel, steps, columns, scale),
        [VMEM] * 2,
        [shape(f32, dests, topics)] + [shape(f32, pair, topics)] * 2,
        6 * MIB + 2 * matrix,
        [pltpu.VMEM((seeds, topics), i32), pltpu.VMEM((groups + 1, seeds, topics), i32)],
    )(dense, seed_rows)
    split = [shape(f32, pair, topics)] + [shape(bf16, pair, topics)] * chips
    parts = call(functools.partial(split_kernel, chips), [VMEM] * 2, split, 6 * MIB)(keep, recv)

    parts = list(parts)
    parts[0], tied = lax.optimization_barrier((parts[0], dense))
    other = from_col(tied, chips, 0, 1)
    far = steps - 2
    first = 2 * edge
    room = 6 * MIB + 2 * matrix
    for iteration in range(1, ITERS):
        mine, *sends = parts
        total = mine
        for d in range(1, chips):
            total = total + from_col(sends[d], chips, d, 0).astype(f32)
        behind = sum(from_behind(sends[d], steps, 1, chips, d).astype(f32) for d in range(chips))
        sent = (damping * total + restart).astype(bf16)
        sent_behind = (damping * behind + restart_behind).astype(bf16)
        arriving = [from_behind(sent, steps, d) for d in range(steps - 1, 1, -1)]
        (near,) = call(near_kernel, [VMEM] * 4, [shape(f32, dests, topics)], room)(
            dense, other, sent_behind, sent
        )
        if iteration < ITERS - 1:
            parts = call(
                functools.partial(step_kernel, chips, first), [VMEM] * (3 + far), split, room
            )(dense, other, near, *arriving)
        else:
            parts = call(
                functools.partial(last_kernel, chips, first),
                [VMEM] * (4 + far),
                [shape(f32, edge, topics)] * CORES + [shape(bf16, edge, topics)] * (CORES * (chips - 1)),
                room,
            )(dense, other, near, restart, *arriving)
    arrived = [
        part if d == e == 0 else from_col(part, chips, d, e)
        for (d, e), part in zip([(d, e) for d in range(chips) for e in range(CORES)], parts)
    ]
    (out,) = call(
        functools.partial(final_kernel, chips),
        [VMEM] * len(arrived),
        [shape(f32, edge, CORES * topics)],
        4 * MIB,
    )(*arrived)
    return out


def solution(mesh):
    return jax.shard_map(
        body,
        mesh=mesh,
        in_specs=(
            P(("parts", "blk"), "col", None, None, None, None),
            P(("parts", "blk"), "col", None, None),
            P(("parts", "blk"), "col", None),
            P("parts", None),
        ),
        out_specs=P(("parts", "blk", "col"), None),
        check_vma=False,
    )
```

time: 39.1 us -> 35.7 us (0.913)
  waiting for transfers between devices: 16.8 us -> 10.2 us
  starting transfers between devices: 16.8 us -> 19.9 us
    ppermute x7, waiting for transfers between devices: 9.11 us -> 3.96 us  [from_col(): return lax.ppermute(value, 'col', route)]
    ppermute x6 -> x8, starting transfers between devices: 9.56 us -> 13.2 us  [the longest x6 9.81 us: from_behind(): lax.ppermute(value, 'blk', [(i, (i + distance) % steps) for i in range(st...]
    ppermute x6 -> x8, waiting for transfers between devices: 7.65 us -> 6.25 us  [the longest x6 6.25 us: from_behind(): lax.ppermute(value, 'blk', [(i, (i + distance) % steps) for i in range(st...]
    pallas_call x1, Pallas kernels: 3.28 us -> 2.25 us  [body(): call(functools.partial(first_kernel, steps, columns, scale), [HBM] * 4, [...]
    pallas_call x3 -> x5, Pallas kernels: 1.36 us -> 2.27 us  [the longest x1 1.08 us: body(): call(functools.partial(keep_kernel, steps, columns, scale), [VMEM] * 2, [...]
    ppermute x7, starting transfers between devices: 7.24 us -> 6.7 us  [from_col(): return lax.ppermute(value, 'col', route)]
  transfers between devices with their start and end apart: 13 -> 15, of which waited for: 11 -> 8; matrix products, arithmetic and copies ran while one was open for 0% -> 0% of each run, Pallas kernels for 1% -> 5%
where the time goes in v3:
time: 35.7 us; the launch traced here: 35.6 us
  starting transfers between devices  19.9 us (56%)
  waiting for transfers between devices  10.2 us (29%)
  Pallas kernels  5.25 us (15%)
    ppermute x6, starting transfers between devices, from_behind(): lax.ppermute(value, 'blk', [(i, (i + distance) % steps) for i in range(st...  9.81 us
    ppermute x7, starting transfers between devices, from_col(): return lax.ppermute(value, 'col', route)  6.7 us
    ppermute x6, waiting for transfers between devices, from_behind(): lax.ppermute(value, 'blk', [(i, (i + distance) % steps) for i in range(st...  6.25 us
    ppermute x7, waiting for transfers between devices, from_col(): return lax.ppermute(value, 'col', route)  3.96 us
    ppermute x2, starting transfers between devices, from_behind(): return lax.ppermute(value, ('blk', 'col'), route)  3.42 us
    pallas_call x1, Pallas kernels, body(): call(functools.partial(first_kernel, steps, columns, scale), [HBM] * 4, [...  2.25 us
    pallas_call x1, Pallas kernels, body(): call(functools.partial(keep_kernel, steps, columns, scale), [VMEM] * 2, [...  1.08 us
  transfers between devices with their start and end apart: 15, of which 8 were waited for; matrix products, arithmetic and copies ran while one was open for 0% of the time, Pallas kernels for 5%

profile of v3, /device:TPU:0, one launch (start us, length us, event | category | flops | bytes accessed | tf_op | source)
XLA Modules:
  0.0 35.6 jit_solution(1387667260501908920)
XLA Ops:
  0.0 2.3 %shard_map.46 = (bf16[512,512]{1,0:T(8,128)(2,1)S(1)}, bf16[512,128]{1,0:T(8,128)(2,1)S(1)}, s32[64,128]{1,0:T(8,128)S(1)}) custom-call(bf16[1,1,4,10,128,128]{5,4,3,2,1,0:T(8,128)(2,1)} %tiles_hbm.1, s32[1,1,4,10]{3,2,1,0:T(4,128)} %dest_hbm.1, s32[1,1,4]{2,1,0:T(1,128)} %count_hbm.1, s32[64,256]{1,0:T(8,128)} %bitcast.1), custom_call_target="tpu_custom_call" | custom-call | tf_op jit(solution)/shard_map/pallas_call | solution.py:246
  2.3 0.5 %collective-permute-start = (bf16[512,128]{1,0:T(8,128)(2,1)S(1)}, bf16[512,128]{1,0:T(8,128)(2,1)S(1)}, u32[]{:S(2)}, u32[]{:S(2)}) collective-permute-start(bf16[512,128]{1,0:T(8,128)(2,1)S(1)} %get-tuple-element.26), channel_id=1, source_target_pairs={{0,1},{1,0},{2,3},{3,2},{4,5},{5,4},{6,7},{7,6},{8,9},{9,8},{10,11... | collective-permute-start | bytes 393224 | tf_op jit(solution)/shard_map/ppermute | solution.py:206
  2.8 1.1 %shard_map.47 = (f32[512,128]{1,0:T(8,128)S(1)}, f32[256,128]{1,0:T(8,128)S(1)}, f32[256,128]{1,0:T(8,128)S(1)}) custom-call(bf16[512,512]{1,0:T(8,128)(2,1)S(1)} %get-tuple-element.28.dense.own, s32[64,128]{1,0:T(8,128)S(1)} %get-tuple-element.24.seed_rows), custom_call_target="tpu_custom_call" | custom-call | tf_op jit(solution)/shard_map/pallas_call | solution.py:264
  3.9 0.0 collective-permute-done.recv
  3.9 0.1 shard_map.48
  3.9 2.8 %collective-permute-start.4 = (bf16[256,128]{1,0:T(8,128)(2,1)S(1)}, bf16[256,128]{1,0:T(8,128)(2,1)S(1)}, u32[]{:S(2)}, u32[]{:S(2)}) collective-permute-start(bf16[256,128]{1,0:T(8,128)(2,1)S(1)} %get-tuple-element.30), channel_id=1, source_target_pairs={{0,2},{1,3},{2,0},{3,1},{4,6},{5,7},{6,4},{7,5},{8,10},{9,11},{10,... | collective-permute-start | bytes 196616 | tf_op jit(solution)/shard_map/ppermute | solution.py:206
  6.7 0.0 collective-permute-start.1
  6.7 1.6 %collective-permute-start.3 = (bf16[256,128]{1,0:T(8,128)(2,1)S(1)}, bf16[256,128]{1,0:T(8,128)(2,1)S(1)}, u32[]{:S(2)}, u32[]{:S(2)}) collective-permute-start(bf16[256,128]{1,0:T(8,128)(2,1)S(1)} %get-tuple-element.30), channel_id=1, source_target_pairs={{0,6},{1,7},{2,4},{3,5},{4,10},{5,11},{6,8},{7,9},{8,14},{9,15},{1... | collective-permute-start | bytes 196616 | tf_op jit(solution)/shard_map/ppermute | solution.py:219
  8.3 1.6 %collective-permute-start.2 = (bf16[256,128]{1,0:T(8,128)(2,1)S(1)}, bf16[256,128]{1,0:T(8,128)(2,1)S(1)}, u32[]{:S(2)}, u32[]{:S(2)}) collective-permute-start(bf16[256,128]{1,0:T(8,128)(2,1)S(1)} %get-tuple-element.29), channel_id=1, source_target_pairs={{0,4},{4,8},{8,12},{12,0},{1,5},{5,9},{9,13},{13,1},{2,6},{6,10},{... | collective-permute-start | bytes 196616 | tf_op jit(solution)/shard_map/ppermute | solution.py:211
  9.8 0.0 collective-permute-done.4
  9.9 2.3 %collective-permute-start.6 = (bf16[256,128]{1,0:T(8,128)(2,1)S(1)}, bf16[256,128]{1,0:T(8,128)(2,1)S(1)}, u32[]{:S(2)}, u32[]{:S(2)}) collective-permute-start(bf16[256,128]{1,0:T(8,128)(2,1)S(1)} %add_convert_fusion.2.refs_1_), channel_id=1, source_target_pairs={{0,8},{4,12},{8,0},{12,4},{1,9},{5,13},{9,1},{13,5},{2,10},{6,14},... | collective-permute-start | bytes 196616 | tf_op jit(solution)/shard_map/ppermute | solution.py:211
  12.2 1.7 %collective-permute-start.5 = (bf16[256,128]{1,0:T(8,128)(2,1)S(1)}, bf16[256,128]{1,0:T(8,128)(2,1)S(1)}, u32[]{:S(2)}, u32[]{:S(2)}) collective-permute-start(bf16[256,128]{1,0:T(8,128)(2,1)S(1)} %add_convert_fusion.2.refs_1_), channel_id=1, source_target_pairs={{0,12},{4,0},{8,4},{12,8},{1,13},{5,1},{9,5},{13,9},{2,14},{6,2},{... | collective-permute-start | bytes 196616 | tf_op jit(solution)/shard_map/ppermute | solution.py:211
  13.9 0.8 %collective-permute-done.2 = bf16[256,128]{1,0:T(8,128)(2,1)S(1)} collective-permute-done((bf16[256,128]{1,0:T(8,128)(2,1)S(1)}, bf16[256,128]{1,0:T(8,128)(2,1)S(1)}, u32[]{:S(2)}, u32[]{:S(2)}) %collective-permute-start.2) | collective-permute-done | bytes 65568 | tf_op jit(solution)/shard_map/ppermute | solution.py:211
  14.7 0.0 collective-permute-done.3
  14.7 0.0 collective-permute-done.1.other
  14.7 0.3 shard_map.49.near
  15.1 2.3 %collective-permute-done.6.refs_1_ = bf16[256,128]{1,0:T(8,128)(2,1)S(1)} collective-permute-done((bf16[256,128]{1,0:T(8,128)(2,1)S(1)}, bf16[256,128]{1,0:T(8,128)(2,1)S(1)}, u32[]{:S(2)}, u32[]{:S(2)}) %collective-permute-start.6) | collective-permute-done | bytes 65568 | tf_op jit(solution)/shard_map/ppermute | solution.py:211
  17.4 0.1 collective-permute-done.5.refs_0_
  17.5 0.3 shard_map.50
  17.8 1.5 %collective-permute-start.9 = (bf16[256,128]{1,0:T(8,128)(2,1)S(1)}, bf16[256,128]{1,0:T(8,128)(2,1)S(1)}, u32[]{:S(2)}, u32[]{:S(2)}) collective-permute-start(bf16[256,128]{1,0:T(8,128)(2,1)S(1)} %get-tuple-element.35), channel_id=1, source_target_pairs={{0,2},{1,3},{2,0},{3,1},{4,6},{5,7},{6,4},{7,5},{8,10},{9,11},{10,... | collective-permute-start | bytes 196616 | tf_op jit(solution)/shard_map/ppermute | solution.py:206
  19.2 1.9 %collective-permute-start.8 = (bf16[256,128]{1,0:T(8,128)(2,1)S(1)}, bf16[256,128]{1,0:T(8,128)(2,1)S(1)}, u32[]{:S(2)}, u32[]{:S(2)}) collective-permute-start(bf16[256,128]{1,0:T(8,128)(2,1)S(1)} %get-tuple-element.35), channel_id=1, source_target_pairs={{0,6},{1,7},{2,4},{3,5},{4,10},{5,11},{6,8},{7,9},{8,14},{9,15},{1... | collective-permute-start | bytes 196616 | tf_op jit(solution)/shard_map/ppermute | solution.py:219
  21.1 0.0 collective-permute-start.7
  21.1 1.0 %collective-permute-done.9 = bf16[256,128]{1,0:T(8,128)(2,1)S(1)} collective-permute-done((bf16[256,128]{1,0:T(8,128)(2,1)S(1)}, bf16[256,128]{1,0:T(8,128)(2,1)S(1)}, u32[]{:S(2)}, u32[]{:S(2)}) %collective-permute-start.9) | collective-permute-done | bytes 65568 | tf_op jit(solution)/shard_map/ppermute | solution.py:206
  22.1 1.7 %collective-permute-start.11 = (bf16[256,128]{1,0:T(8,128)(2,1)S(1)}, bf16[256,128]{1,0:T(8,128)(2,1)S(1)}, u32[]{:S(2)}, u32[]{:S(2)}) collective-permute-start(bf16[256,128]{1,0:T(8,128)(2,1)S(1)} %add_convert_fusion.refs_1_), channel_id=1, source_target_pairs={{0,8},{4,12},{8,0},{12,4},{1,9},{5,13},{9,1},{13,5},{2,10},{6,14},... | collective-permute-start | bytes 196616 | tf_op jit(solution)/shard_map/ppermute | solution.py:211
  23.8 2.6 %collective-permute-start.10 = (bf16[256,128]{1,0:T(8,128)(2,1)S(1)}, bf16[256,128]{1,0:T(8,128)(2,1)S(1)}, u32[]{:S(2)}, u32[]{:S(2)}) collective-permute-start(bf16[256,128]{1,0:T(8,128)(2,1)S(1)} %add_convert_fusion.refs_1_), channel_id=1, source_target_pairs={{0,12},{4,0},{8,4},{12,8},{1,13},{5,1},{9,5},{13,9},{2,14},{6,2},{... | collective-permute-start | bytes 196616 | tf_op jit(solution)/shard_map/ppermute | solution.py:211
  26.3 1.6 %collective-permute-done.7 = bf16[256,128]{1,0:T(8,128)(2,1)S(1)} collective-permute-done((bf16[256,128]{1,0:T(8,128)(2,1)S(1)}, bf16[256,128]{1,0:T(8,128)(2,1)S(1)}, u32[]{:S(2)}, u32[]{:S(2)}) %collective-permute-start.7) | collective-permute-done | bytes 65568 | tf_op jit(solution)/shard_map/ppermute | solution.py:211
  27.9 0.0 collective-permute-done.8
  28.0 0.3 shard_map.51.near
  28.3 1.4 %collective-permute-done.11.refs_1_ = bf16[256,128]{1,0:T(8,128)(2,1)S(1)} collective-permute-done((bf16[256,128]{1,0:T(8,128)(2,1)S(1)}, bf16[256,128]{1,0:T(8,128)(2,1)S(1)}, u32[]{:S(2)}, u32[]{:S(2)}) %collective-permute-start.11) | collective-permute-done | bytes 65568 | tf_op jit(solution)/shard_map/ppermute | solution.py:211
  29.7 0.0 collective-permute-done.10.refs_0_
  29.7 0.3 shard_map.52
  30.0 0.1 collective-permute-start.12
  30.1 1.5 %collective-permute-start.13 = (bf16[128,128]{1,0:T(8,128)(2,1)S(1)}, bf16[128,128]{1,0:T(8,128)(2,1)S(1)}, u32[]{:S(2)}, u32[]{:S(2)}) collective-permute-start(bf16[128,128]{1,0:T(8,128)(2,1)S(1)} %get-tuple-element.39), channel_id=1, source_target_pairs={{0,2},{1,3},{2,0},{3,1},{4,6},{5,7},{6,4},{7,5},{8,10},{9,11},{10,... | collective-permute-start | bytes 98312 | tf_op jit(solution)/shard_map/ppermute | solution.py:206
  31.6 0.4 %collective-permute-start.14 = (bf16[128,128]{1,0:T(8,128)(2,1)S(1)}, bf16[128,128]{1,0:T(8,128)(2,1)S(1)}, u32[]{:S(2)}, u32[]{:S(2)}) collective-permute-start(bf16[128,128]{1,0:T(8,128)(2,1)S(1)} %get-tuple-element.40), channel_id=1, source_target_pairs={{0,3},{1,2},{2,1},{3,0},{4,7},{5,6},{6,5},{7,4},{8,11},{9,10},{10,... | collective-permute-start | bytes 98312 | tf_op jit(solution)/shard_map/ppermute | solution.py:206
  32.0 2.1 %collective-permute-done.13.refs_2_ = bf16[128,128]{1,0:T(8,128)(2,1)S(1)} collective-permute-done((bf16[128,128]{1,0:T(8,128)(2,1)S(1)}, bf16[128,128]{1,0:T(8,128)(2,1)S(1)}, u32[]{:S(2)}, u32[]{:S(2)}) %collective-permute-start.13) | collective-permute-done | bytes 32800 | tf_op jit(solution)/shard_map/ppermute | solution.py:206
  34.1 0.8 %collective-permute-done.14.refs_3_ = bf16[128,128]{1,0:T(8,128)(2,1)S(1)} collective-permute-done((bf16[128,128]{1,0:T(8,128)(2,1)S(1)}, bf16[128,128]{1,0:T(8,128)(2,1)S(1)}, u32[]{:S(2)}, u32[]{:S(2)}) %collective-permute-start.14) | collective-permute-done | bytes 32800 | tf_op jit(solution)/shard_map/ppermute | solution.py:206
  34.9 0.0 collective-permute-done.12.refs_1_
  34.9 0.7 %shard_map.53 = f32[128,256]{1,0:T(8,128)} custom-call(f32[128,128]{1,0:T(8,128)S(1)} %get-tuple-element.37.refs_0_, f32[128,128]{1,0:T(8,128)S(1)} %collective-permute-done.12.refs_1_, bf16[128,128]{1,0:T(8,128)(2,1)S(1)} %collective-permute-done.13.refs_2_, bf16[128,128]{1,0:T(8,128)(2,1)S(1)} %collective-permute-done.14.refs_3_), custom_call_target="tpu_custom_call" | custom-call | tf_op jit(solution)/shard_map/pallas_call | solution.py:307
  (4 shorter events, 0.1 us)
Async XLA Ops:
  2.3 1.6 %collective-permute-start = (bf16[512,128]{1,0:T(8,128)(2,1)S(1)}, bf16[512,128]{1,0:T(8,128)(2,1)S(1)}, u32[]{:S(2)}, u32[]{:S(2)}) collective-permute-start(bf16[512,128]{1,0:T(8,128)(2,1)S(1)} %get-tuple-element.26), channel_id=1, source_target_pairs={{0,1},{1,0},{2,3},{3,2},{4,5},{5,4},{6,7},{7,6},{8,9},{9,8},{10,11... | collective-permute-start | bytes 393224 | tf_op jit(solution)/shard_map/ppermute | solution.py:206
  3.9 5.9 %collective-permute-start.4 = (bf16[256,128]{1,0:T(8,128)(2,1)S(1)}, bf16[256,128]{1,0:T(8,128)(2,1)S(1)}, u32[]{:S(2)}, u32[]{:S(2)}) collective-permute-start(bf16[256,128]{1,0:T(8,128)(2,1)S(1)} %get-tuple-element.30), channel_id=1, source_target_pairs={{0,2},{1,3},{2,0},{3,1},{4,6},{5,7},{6,4},{7,5},{8,10},{9,11},{10,... | collective-permute-start | bytes 196616 | tf_op jit(solution)/shard_map/ppermute | solution.py:206
  6.7 8.0 %collective-permute-start.1 = (bf16[512,512]{1,0:T(8,128)(2,1)S(1)}, bf16[512,512]{1,0:T(8,128)(2,1)S(1)}, u32[]{:S(2)}, u32[]{:S(2)}) collective-permute-start(bf16[512,512]{1,0:T(8,128)(2,1)S(1)} %get-tuple-element.28.dense.own), channel_id=1, source_target_pairs={{0,1},{1,0},{2,3},{3,2},{4,5},{5,4},{6,7},{7,6},{8,9},{9,8},{10,11... | collective-permute-start | bytes 1572872 | tf_op jit(solution)/shard_map/ppermute | solution.py:206
  6.7 8.0 %collective-permute-start.3 = (bf16[256,128]{1,0:T(8,128)(2,1)S(1)}, bf16[256,128]{1,0:T(8,128)(2,1)S(1)}, u32[]{:S(2)}, u32[]{:S(2)}) collective-permute-start(bf16[256,128]{1,0:T(8,128)(2,1)S(1)} %get-tuple-element.30), channel_id=1, source_target_pairs={{0,6},{1,7},{2,4},{3,5},{4,10},{5,11},{6,8},{7,9},{8,14},{9,15},{1... | collective-permute-start | bytes 196616 | tf_op jit(solution)/shard_map/ppermute | solution.py:219
  8.3 6.4 %collective-permute-start.2 = (bf16[256,128]{1,0:T(8,128)(2,1)S(1)}, bf16[256,128]{1,0:T(8,128)(2,1)S(1)}, u32[]{:S(2)}, u32[]{:S(2)}) collective-permute-start(bf16[256,128]{1,0:T(8,128)(2,1)S(1)} %get-tuple-element.29), channel_id=1, source_target_pairs={{0,4},{4,8},{8,12},{12,0},{1,5},{5,9},{9,13},{13,1},{2,6},{6,10},{... | collective-permute-start | bytes 196616 | tf_op jit(solution)/shard_map/ppermute | solution.py:211
  9.9 7.5 %collective-permute-start.6 = (bf16[256,128]{1,0:T(8,128)(2,1)S(1)}, bf16[256,128]{1,0:T(8,128)(2,1)S(1)}, u32[]{:S(2)}, u32[]{:S(2)}) collective-permute-start(bf16[256,128]{1,0:T(8,128)(2,1)S(1)} %add_convert_fusion.2.refs_1_), channel_id=1, source_target_pairs={{0,8},{4,12},{8,0},{12,4},{1,9},{5,13},{9,1},{13,5},{2,10},{6,14},... | collective-permute-start | bytes 196616 | tf_op jit(solution)/shard_map/ppermute | solution.py:211
  12.2 5.3 %collective-permute-start.5 = (bf16[256,128]{1,0:T(8,128)(2,1)S(1)}, bf16[256,128]{1,0:T(8,128)(2,1)S(1)}, u32[]{:S(2)}, u32[]{:S(2)}) collective-permute-start(bf16[256,128]{1,0:T(8,128)(2,1)S(1)} %add_convert_fusion.2.refs_1_), channel_id=1, source_target_pairs={{0,12},{4,0},{8,4},{12,8},{1,13},{5,1},{9,5},{13,9},{2,14},{6,2},{... | collective-permute-start | bytes 196616 | tf_op jit(solution)/shard_map/ppermute | solution.py:211
  17.8 4.3 %collective-permute-start.9 = (bf16[256,128]{1,0:T(8,128)(2,1)S(1)}, bf16[256,128]{1,0:T(8,128)(2,1)S(1)}, u32[]{:S(2)}, u32[]{:S(2)}) collective-permute-start(bf16[256,128]{1,0:T(8,128)(2,1)S(1)} %get-tuple-element.35), channel_id=1, source_target_pairs={{0,2},{1,3},{2,0},{3,1},{4,6},{5,7},{6,4},{7,5},{8,10},{9,11},{10,... | collective-permute-start | bytes 196616 | tf_op jit(solution)/shard_map/ppermute | solution.py:206
  19.2 8.7 %collective-permute-start.8 = (bf16[256,128]{1,0:T(8,128)(2,1)S(1)}, bf16[256,128]{1,0:T(8,128)(2,1)S(1)}, u32[]{:S(2)}, u32[]{:S(2)}) collective-permute-start(bf16[256,128]{1,0:T(8,128)(2,1)S(1)} %get-tuple-element.35), channel_id=1, source_target_pairs={{0,6},{1,7},{2,4},{3,5},{4,10},{5,11},{6,8},{7,9},{8,14},{9,15},{1... | collective-permute-start | bytes 196616 | tf_op jit(solution)/shard_map/ppermute | solution.py:219
  21.1 6.9 %collective-permute-start.7 = (bf16[256,128]{1,0:T(8,128)(2,1)S(1)}, bf16[256,128]{1,0:T(8,128)(2,1)S(1)}, u32[]{:S(2)}, u32[]{:S(2)}) collective-permute-start(bf16[256,128]{1,0:T(8,128)(2,1)S(1)} %get-tuple-element.34), channel_id=1, source_target_pairs={{0,4},{4,8},{8,12},{12,0},{1,5},{5,9},{9,13},{13,1},{2,6},{6,10},{... | collective-permute-start | bytes 196616 | tf_op jit(solution)/shard_map/ppermute | solution.py:211
  22.1 7.6 %collective-permute-start.11 = (bf16[256,128]{1,0:T(8,128)(2,1)S(1)}, bf16[256,128]{1,0:T(8,128)(2,1)S(1)}, u32[]{:S(2)}, u32[]{:S(2)}) collective-permute-start(bf16[256,128]{1,0:T(8,128)(2,1)S(1)} %add_convert_fusion.refs_1_), channel_id=1, source_target_pairs={{0,8},{4,12},{8,0},{12,4},{1,9},{5,13},{9,1},{13,5},{2,10},{6,14},... | collective-permute-start | bytes 196616 | tf_op jit(solution)/shard_map/ppermute | solution.py:211
  23.8 6.0 %collective-permute-start.10 = (bf16[256,128]{1,0:T(8,128)(2,1)S(1)}, bf16[256,128]{1,0:T(8,128)(2,1)S(1)}, u32[]{:S(2)}, u32[]{:S(2)}) collective-permute-start(bf16[256,128]{1,0:T(8,128)(2,1)S(1)} %add_convert_fusion.refs_1_), channel_id=1, source_target_pairs={{0,12},{4,0},{8,4},{12,8},{1,13},{5,1},{9,5},{13,9},{2,14},{6,2},{... | collective-permute-start | bytes 196616 | tf_op jit(solution)/shard_map/ppermute | solution.py:211
  30.0 4.9 %collective-permute-start.12 = (f32[128,128]{1,0:T(8,128)S(1)}, f32[128,128]{1,0:T(8,128)S(1)}, u32[]{:S(2)}, u32[]{:S(2)}) collective-permute-start(f32[128,128]{1,0:T(8,128)S(1)} %get-tuple-element.38), channel_id=1, source_target_pairs={{0,1},{1,0},{2,3},{3,2},{4,5},{5,4},{6,7},{7,6},{8,9},{9,8},{10,11... | collective-permute-start | bytes 196616 | tf_op jit(solution)/shard_map/ppermute | solution.py:206
  30.1 4.0 %collective-permute-start.13 = (bf16[128,128]{1,0:T(8,128)(2,1)S(1)}, bf16[128,128]{1,0:T(8,128)(2,1)S(1)}, u32[]{:S(2)}, u32[]{:S(2)}) collective-permute-start(bf16[128,128]{1,0:T(8,128)(2,1)S(1)} %get-tuple-element.39), channel_id=1, source_target_pairs={{0,2},{1,3},{2,0},{3,1},{4,6},{5,7},{6,4},{7,5},{8,10},{9,11},{10,... | collective-permute-start | bytes 98312 | tf_op jit(solution)/shard_map/ppermute | solution.py:206
  31.6 3.3 %collective-permute-start.14 = (bf16[128,128]{1,0:T(8,128)(2,1)S(1)}, bf16[128,128]{1,0:T(8,128)(2,1)S(1)}, u32[]{:S(2)}, u32[]{:S(2)}) collective-permute-start(bf16[128,128]{1,0:T(8,128)(2,1)S(1)} %get-tuple-element.40), channel_id=1, source_target_pairs={{0,3},{1,2},{2,1},{3,0},{4,7},{5,6},{6,5},{7,4},{8,11},{9,10},{10,... | collective-permute-start | bytes 98312 | tf_op jit(solution)/shard_map/ppermute | solution.py:206

commit v4 on v3

--- a/solution.py
+++ b/solution.py
@@ -22,6 +22,17 @@
 def place():
     col = lax.axis_index("col")
     return lax.axis_index("blk"), col // CORES, col % CORES
+
+
+def cycle(core, steps):
+    return list(range(steps)) if core == 0 else [0, *range(1, steps, 2), *range((steps - 1) // 2 * 2, 0, -2)]
+
+
+def row_behind(row, core, steps, distance):
+    place_out = jnp.where(row % 2 == 1, (row + 1) // 2, lax.rem(steps - row // 2, steps))
+    at = lax.rem(jnp.where(core == 0, row, place_out) - distance + steps, steps)
+    row_out = jnp.where(at <= steps // 2, jnp.maximum(2 * at - 1, 0), 2 * (steps - at))
+    return jnp.where(core == 0, at, row_out)
 
 
 def add_seeds(counts, ids, weights, first, last):
@@ -108,7 +119,7 @@
     groups = weights.shape[0] - 1
     weights[groups] = jnp.zeros_like(hosts)
     for d in range(2):
-        offset = block - lax.rem(row - d + steps, steps) * columns - chip * CORES
+        offset = block - row_behind(row, core, steps, d) * columns - chip * CORES
         for c in range(CORES):
             weights[groups] += jnp.where(offset == c, 1 << (FIELD * (d * CORES + c)), 0)
     counts = [jnp.zeros((edge, hosts.shape[1]), jnp.int32)] * (groups + 1)
@@ -133,53 +144,47 @@
         sends[d][...] = part.astype(jnp.bfloat16)
 
 
-def gathered(scores, core, edge):
-    return [
-        jnp.concatenate([s[pl.ds(pl.multiple_of(c * edge, edge), edge), :] for s in scores[::-1]], axis=0)
-        for c in (core, 1 - core)
-    ]
-
-
-def product(matrices, sources, rows, first):
-    lanes = pl.ds(first, sources[0].shape[0])
+def product(matrices, scores, rows, first, steps):
+    row, _, core = place()
+    edge = scores[0].shape[0] // CORES
+    left, right = [], []
+    for distance, score in enumerate(scores[::-1], first):
+        step = lax.rem(row - row_behind(row, core, steps, distance) + steps, steps)
+        for matrix, c in zip(matrices, (core, 1 - core)):
+            left.append(matrix[rows, pl.ds(pl.multiple_of(step * edge, edge), edge)])
+            right.append(score[pl.ds(pl.multiple_of(c * edge, edge), edge), :])
     return jnp.dot(
-        jnp.concatenate([m[rows, lanes] for m in matrices], axis=1),
-        jnp.concatenate(sources, axis=0),
-        preferred_element_type=jnp.float32,
+        jnp.concatenate(left, axis=1), jnp.concatenate(right, axis=0), preferred_element_type=jnp.float32
     )
 
 
-def near_kernel(own, other, *refs):
+def near_kernel(steps, own, other, *refs):
     scores, out = refs[:-1], refs[-1]
-    _, _, core = place()
-    sources = gathered(scores, core, scores[0].shape[0] // CORES)
-    out[...] = product((own, other), sources, slice(None), 0)
-
-
-def step_kernel(chips, first, own, other, near, *refs):
+    out[...] = product((own, other), scores, slice(None), 0, steps)
+
+
+def step_kernel(steps, chips, own, other, near, *refs):
     scores, mine, sends = refs[: -chips - 1], refs[-chips - 1], refs[-chips:]
-    _, chip, core = place()
+    _, chip, _ = place()
     size = mine.shape[0]
-    sources = gathered(scores, core, size // CORES)
     for d in [*range(1, chips), 0]:
         rows = pl.ds(pl.multiple_of(lax.rem(chip + d, chips) * size, size), size)
-        part = near[rows, :] + product((own, other), sources, rows, first)
+        part = near[rows, :] + product((own, other), scores, rows, steps - len(scores), steps)
         if d == 0:
             mine[...] = part
         sends[d][...] = part.astype(jnp.bfloat16)
 
 
-def last_kernel(chips, first, own, other, near, restart, *refs):
+def last_kernel(steps, chips, own, other, near, restart, *refs):
     scores, parts = refs[: -chips * CORES], refs[-chips * CORES :]
     _, chip, core = place()
     edge = parts[0].shape[0]
-    sources = gathered(scores, core, edge)
     for d in range(chips):
         for e in range(CORES):
             owner = lax.rem(core + e, CORES)
             block = lax.rem(chip + d, chips) * CORES + owner
             rows = pl.ds(pl.multiple_of(block * edge, edge), edge)
-            part = near[rows, :] + product((own, other), sources, rows, first)
+            part = near[rows, :] + product((own, other), scores, rows, steps - len(scores), steps)
             if d == 0:
                 rows = pl.ds(pl.multiple_of(owner * edge, edge), edge)
                 part = damping * part + restart[rows, :]
@@ -206,16 +211,15 @@
     return lax.ppermute(value, "col", route)
 
 
-def from_behind(value, steps, distance, chips=1, chip_step=0):
-    if not chip_step:
-        return lax.ppermute(value, "blk", [(i, (i + distance) % steps) for i in range(steps)])
+def from_behind(value, steps, chips, distance, chip_step=0):
     columns = chips * CORES
-    route = [
-        (i * columns + x * CORES + c, (i + distance) % steps * columns + (x + chip_step) % chips * CORES + c)
-        for i in range(steps)
-        for x in range(chips)
-        for c in range(CORES)
-    ]
+    route = []
+    for c in range(CORES):
+        rows = cycle(c, steps)
+        for i in range(steps):
+            for x in range(chips):
+                target = rows[(i + distance) % steps] * columns + (x + chip_step) % chips * CORES + c
+                route.append((rows[i] * columns + x * CORES + c, target))
     return lax.ppermute(value, ("blk", "col"), route)
 
 
@@ -275,27 +279,26 @@
     parts[0], tied = lax.optimization_barrier((parts[0], dense))
     other = from_col(tied, chips, 0, 1)
     far = steps - 2
-    first = 2 * edge
     room = 6 * MIB + 2 * matrix
     for iteration in range(1, ITERS):
         mine, *sends = parts
         total = mine
         for d in range(1, chips):
             total = total + from_col(sends[d], chips, d, 0).astype(f32)
-        behind = sum(from_behind(sends[d], steps, 1, chips, d).astype(f32) for d in range(chips))
+        behind = sum(from_behind(sends[d], steps, chips, 1, d).astype(f32) for d in range(chips))
         sent = (damping * total + restart).astype(bf16)
         sent_behind = (damping * behind + restart_behind).astype(bf16)
-        arriving = [from_behind(sent, steps, d) for d in range(steps - 1, 1, -1)]
-        (near,) = call(near_kernel, [VMEM] * 4, [shape(f32, dests, topics)], room)(
+        arriving = [from_behind(sent, steps, chips, d) for d in range(steps - 1, 1, -1)]
+        (near,) = call(functools.partial(near_kernel, steps), [VMEM] * 4, [shape(f32, dests, topics)], room)(
             dense, other, sent_behind, sent
         )
         if iteration < ITERS - 1:
             parts = call(
-                functools.partial(step_kernel, chips, first), [VMEM] * (3 + far), split, room
+                functools.partial(step_kernel, steps, chips), [VMEM] * (3 + far), split, room
             )(dense, other, near, *arriving)
         else:
             parts = call(
-                functools.partial(last_kernel, chips, first),
+                functools.partial(last_kernel, steps, chips),
                 [VMEM] * (4 + far),
                 [shape(f32, edge, topics)] * CORES + [shape(bf16, edge, topics)] * (CORES * (chips - 1)),
                 room,

time: 35.7 us -> 35.2 us (0.986)
  starting transfers between devices: 19.9 us -> 19.5 us
    ppermute x6 -> x0, starting transfers between devices: 9.81 us -> none  [from_behind(): lax.ppermute(value, 'blk', [(i, (i + distance) % steps) for i in range(st...]
    ppermute x2 -> x8, starting transfers between devices: 3.42 us -> 12.7 us  [from_behind(): return lax.ppermute(value, ('blk', 'col'), route)]
    ppermute x6 -> x0, waiting for transfers between devices: 6.25 us -> none  [from_behind(): lax.ppermute(value, 'blk', [(i, (i + distance) % steps) for i in range(st...]
    ppermute x2 -> x8, waiting for transfers between devices: 0.01 us -> 5.97 us  [from_behind(): return lax.ppermute(value, ('blk', 'col'), route)]
where the time goes in v4:
time: 35.2 us; the launch traced here: 35.1 us
  starting transfers between devices  19.5 us (55%)
  waiting for transfers between devices  10.1 us (29%)
  Pallas kernels  5.33 us (15%)
    ppermute x8, starting transfers between devices, from_behind(): return lax.ppermute(value, ('blk', 'col'), route)  12.7 us
    ppermute x7, starting transfers between devices, from_col(): return lax.ppermute(value, 'col', route)  6.83 us
    ppermute x8, waiting for transfers between devices, from_behind(): return lax.ppermute(value, ('blk', 'col'), route)  5.97 us
    ppermute x7, waiting for transfers between devices, from_col(): return lax.ppermute(value, 'col', route)  4.09 us
    pallas_call x1, Pallas kernels, body(): call(functools.partial(first_kernel, steps, columns, scale), [HBM] * 4, [...  2.25 us
    pallas_call x1, Pallas kernels, body(): call(functools.partial(keep_kernel, steps, columns, scale), [VMEM] * 2, [...  1.08 us
  transfers between devices with their start and end apart: 15, of which 8 were waited for; matrix products, arithmetic and copies ran while one was open for 0% of the time, Pallas kernels for 5%

profile of v4, /device:TPU:0, one launch (start us, length us, event | category | flops | bytes accessed | tf_op | source)
XLA Modules:
  0.0 35.1 jit_solution(3882135040318220290)
XLA Ops:
  0.0 2.3 %shard_map.46 = (bf16[512,512]{1,0:T(8,128)(2,1)S(1)}, bf16[512,128]{1,0:T(8,128)(2,1)S(1)}, s32[64,128]{1,0:T(8,128)S(1)}) custom-call(bf16[1,1,4,10,128,128]{5,4,3,2,1,0:T(8,128)(2,1)} %tiles_hbm.1, s32[1,1,4,10]{3,2,1,0:T(4,128)} %dest_hbm.1, s32[1,1,4]{2,1,0:T(1,128)} %count_hbm.1, s32[64,256]{1,0:T(8,128)} %bitcast.1), custom_call_target="tpu_custom_call" | custom-call | tf_op jit(solution)/shard_map/pallas_call | solution.py:250
  2.3 0.5 %collective-permute-start = (bf16[512,128]{1,0:T(8,128)(2,1)S(1)}, bf16[512,128]{1,0:T(8,128)(2,1)S(1)}, u32[]{:S(2)}, u32[]{:S(2)}) collective-permute-start(bf16[512,128]{1,0:T(8,128)(2,1)S(1)} %get-tuple-element.26), channel_id=1, source_target_pairs={{0,1},{1,0},{2,3},{3,2},{4,5},{5,4},{6,7},{7,6},{8,9},{9,8},{10,11... | collective-permute-start | bytes 393224 | tf_op jit(solution)/shard_map/ppermute | solution.py:211
  2.8 1.1 %shard_map.47 = (f32[512,128]{1,0:T(8,128)S(1)}, f32[256,128]{1,0:T(8,128)S(1)}, f32[256,128]{1,0:T(8,128)S(1)}) custom-call(bf16[512,512]{1,0:T(8,128)(2,1)S(1)} %get-tuple-element.28.dense.own, s32[64,128]{1,0:T(8,128)S(1)} %get-tuple-element.24.seed_rows), custom_call_target="tpu_custom_call" | custom-call | tf_op jit(solution)/shard_map/pallas_call | solution.py:268
  3.9 0.0 collective-permute-done.recv
  3.9 0.1 shard_map.48
  3.9 2.8 %collective-permute-start.4 = (bf16[256,128]{1,0:T(8,128)(2,1)S(1)}, bf16[256,128]{1,0:T(8,128)(2,1)S(1)}, u32[]{:S(2)}, u32[]{:S(2)}) collective-permute-start(bf16[256,128]{1,0:T(8,128)(2,1)S(1)} %get-tuple-element.30), channel_id=1, source_target_pairs={{0,2},{1,3},{2,0},{3,1},{4,6},{5,7},{6,4},{7,5},{8,10},{9,11},{10,... | collective-permute-start | bytes 196616 | tf_op jit(solution)/shard_map/ppermute | solution.py:211
  6.7 0.0 collective-permute-start.1
  6.7 1.5 %collective-permute-start.3 = (bf16[256,128]{1,0:T(8,128)(2,1)S(1)}, bf16[256,128]{1,0:T(8,128)(2,1)S(1)}, u32[]{:S(2)}, u32[]{:S(2)}) collective-permute-start(bf16[256,128]{1,0:T(8,128)(2,1)S(1)} %get-tuple-element.30), channel_id=1, source_target_pairs={{0,6},{2,4},{4,10},{6,8},{8,14},{10,12},{12,2},{14,0},{1,7},{3,5},... | collective-permute-start | bytes 196616 | tf_op jit(solution)/shard_map/ppermute | solution.py:223
  8.3 1.6 %collective-permute-start.2 = (bf16[256,128]{1,0:T(8,128)(2,1)S(1)}, bf16[256,128]{1,0:T(8,128)(2,1)S(1)}, u32[]{:S(2)}, u32[]{:S(2)}) collective-permute-start(bf16[256,128]{1,0:T(8,128)(2,1)S(1)} %get-tuple-element.29), channel_id=1, source_target_pairs={{0,4},{2,6},{4,8},{6,10},{8,12},{10,14},{12,0},{14,2},{1,5},{3,7},... | collective-permute-start | bytes 196616 | tf_op jit(solution)/shard_map/ppermute | solution.py:223
  9.8 0.0 collective-permute-done.4
  9.9 2.3 %collective-permute-start.6 = (bf16[256,128]{1,0:T(8,128)(2,1)S(1)}, bf16[256,128]{1,0:T(8,128)(2,1)S(1)}, u32[]{:S(2)}, u32[]{:S(2)}) collective-permute-start(bf16[256,128]{1,0:T(8,128)(2,1)S(1)} %add_convert_fusion.2.refs_1_), channel_id=1, source_target_pairs={{0,8},{2,10},{4,12},{6,14},{8,0},{10,2},{12,4},{14,6},{1,13},{3,15... | collective-permute-start | bytes 196616 | tf_op jit(solution)/shard_map/ppermute | solution.py:223
  12.2 1.7 %collective-permute-start.5 = (bf16[256,128]{1,0:T(8,128)(2,1)S(1)}, bf16[256,128]{1,0:T(8,128)(2,1)S(1)}, u32[]{:S(2)}, u32[]{:S(2)}) collective-permute-start(bf16[256,128]{1,0:T(8,128)(2,1)S(1)} %add_convert_fusion.2.refs_1_), channel_id=1, source_target_pairs={{0,12},{2,14},{4,0},{6,2},{8,4},{10,6},{12,8},{14,10},{1,9},{3,11}... | collective-permute-start | bytes 196616 | tf_op jit(solution)/shard_map/ppermute | solution.py:223
  13.9 0.8 %collective-permute-done.2 = bf16[256,128]{1,0:T(8,128)(2,1)S(1)} collective-permute-done((bf16[256,128]{1,0:T(8,128)(2,1)S(1)}, bf16[256,128]{1,0:T(8,128)(2,1)S(1)}, u32[]{:S(2)}, u32[]{:S(2)}) %collective-permute-start.2) | collective-permute-done | bytes 65568 | tf_op jit(solution)/shard_map/ppermute | solution.py:223
  14.7 0.0 collective-permute-done.3
  14.8 0.0 collective-permute-done.1.other
  14.8 0.3 shard_map.49.near
  15.1 2.1 %collective-permute-done.6.refs_1_ = bf16[256,128]{1,0:T(8,128)(2,1)S(1)} collective-permute-done((bf16[256,128]{1,0:T(8,128)(2,1)S(1)}, bf16[256,128]{1,0:T(8,128)(2,1)S(1)}, u32[]{:S(2)}, u32[]{:S(2)}) %collective-permute-start.6) | collective-permute-done | bytes 65568 | tf_op jit(solution)/shard_map/ppermute | solution.py:223
  17.2 0.4 %collective-permute-done.5.refs_0_ = bf16[256,128]{1,0:T(8,128)(2,1)S(1)} collective-permute-done((bf16[256,128]{1,0:T(8,128)(2,1)S(1)}, bf16[256,128]{1,0:T(8,128)(2,1)S(1)}, u32[]{:S(2)}, u32[]{:S(2)}) %collective-permute-start.5) | collective-permute-done | bytes 65568 | tf_op jit(solution)/shard_map/ppermute | solution.py:223
  17.6 0.3 shard_map.50
  17.9 1.6 %collective-permute-start.9 = (bf16[256,128]{1,0:T(8,128)(2,1)S(1)}, bf16[256,128]{1,0:T(8,128)(2,1)S(1)}, u32[]{:S(2)}, u32[]{:S(2)}) collective-permute-start(bf16[256,128]{1,0:T(8,128)(2,1)S(1)} %get-tuple-element.35), channel_id=1, source_target_pairs={{0,2},{1,3},{2,0},{3,1},{4,6},{5,7},{6,4},{7,5},{8,10},{9,11},{10,... | collective-permute-start | bytes 196616 | tf_op jit(solution)/shard_map/ppermute | solution.py:211
  19.5 1.2 %collective-permute-start.8 = (bf16[256,128]{1,0:T(8,128)(2,1)S(1)}, bf16[256,128]{1,0:T(8,128)(2,1)S(1)}, u32[]{:S(2)}, u32[]{:S(2)}) collective-permute-start(bf16[256,128]{1,0:T(8,128)(2,1)S(1)} %get-tuple-element.35), channel_id=1, source_target_pairs={{0,6},{2,4},{4,10},{6,8},{8,14},{10,12},{12,2},{14,0},{1,7},{3,5},... | collective-permute-start | bytes 196616 | tf_op jit(solution)/shard_map/ppermute | solution.py:223
  20.7 0.4 %collective-permute-start.7 = (bf16[256,128]{1,0:T(8,128)(2,1)S(1)}, bf16[256,128]{1,0:T(8,128)(2,1)S(1)}, u32[]{:S(2)}, u32[]{:S(2)}) collective-permute-start(bf16[256,128]{1,0:T(8,128)(2,1)S(1)} %get-tuple-element.34), channel_id=1, source_target_pairs={{0,4},{2,6},{4,8},{6,10},{8,12},{10,14},{12,0},{14,2},{1,5},{3,7},... | collective-permute-start | bytes 196616 | tf_op jit(solution)/shard_map/ppermute | solution.py:223
  21.1 1.1 %collective-permute-done.9 = bf16[256,128]{1,0:T(8,128)(2,1)S(1)} collective-permute-done((bf16[256,128]{1,0:T(8,128)(2,1)S(1)}, bf16[256,128]{1,0:T(8,128)(2,1)S(1)}, u32[]{:S(2)}, u32[]{:S(2)}) %collective-permute-start.9) | collective-permute-done | bytes 65568 | tf_op jit(solution)/shard_map/ppermute | solution.py:211
  22.3 1.7 %collective-permute-start.11 = (bf16[256,128]{1,0:T(8,128)(2,1)S(1)}, bf16[256,128]{1,0:T(8,128)(2,1)S(1)}, u32[]{:S(2)}, u32[]{:S(2)}) collective-permute-start(bf16[256,128]{1,0:T(8,128)(2,1)S(1)} %add_convert_fusion.refs_1_), channel_id=1, source_target_pairs={{0,8},{2,10},{4,12},{6,14},{8,0},{10,2},{12,4},{14,6},{1,13},{3,15... | collective-permute-start | bytes 196616 | tf_op jit(solution)/shard_map/ppermute | solution.py:223
  23.9 2.3 %collective-permute-start.10 = (bf16[256,128]{1,0:T(8,128)(2,1)S(1)}, bf16[256,128]{1,0:T(8,128)(2,1)S(1)}, u32[]{:S(2)}, u32[]{:S(2)}) collective-permute-start(bf16[256,128]{1,0:T(8,128)(2,1)S(1)} %add_convert_fusion.refs_1_), channel_id=1, source_target_pairs={{0,12},{2,14},{4,0},{6,2},{8,4},{10,6},{12,8},{14,10},{1,9},{3,11}... | collective-permute-start | bytes 196616 | tf_op jit(solution)/shard_map/ppermute | solution.py:223
  26.2 1.2 %collective-permute-done.7 = bf16[256,128]{1,0:T(8,128)(2,1)S(1)} collective-permute-done((bf16[256,128]{1,0:T(8,128)(2,1)S(1)}, bf16[256,128]{1,0:T(8,128)(2,1)S(1)}, u32[]{:S(2)}, u32[]{:S(2)}) %collective-permute-start.7) | collective-permute-done | bytes 65568 | tf_op jit(solution)/shard_map/ppermute | solution.py:223
  27.4 0.0 collective-permute-done.8
  27.4 0.3 shard_map.51.near
  27.8 1.4 %collective-permute-done.11.refs_1_ = bf16[256,128]{1,0:T(8,128)(2,1)S(1)} collective-permute-done((bf16[256,128]{1,0:T(8,128)(2,1)S(1)}, bf16[256,128]{1,0:T(8,128)(2,1)S(1)}, u32[]{:S(2)}, u32[]{:S(2)}) %collective-permute-start.11) | collective-permute-done | bytes 65568 | tf_op jit(solution)/shard_map/ppermute | solution.py:223
  29.2 0.0 collective-permute-done.10.refs_0_
  29.2 0.3 shard_map.52
  29.5 0.1 collective-permute-start.12
  29.6 1.5 %collective-permute-start.13 = (bf16[128,128]{1,0:T(8,128)(2,1)S(1)}, bf16[128,128]{1,0:T(8,128)(2,1)S(1)}, u32[]{:S(2)}, u32[]{:S(2)}) collective-permute-start(bf16[128,128]{1,0:T(8,128)(2,1)S(1)} %get-tuple-element.39), channel_id=1, source_target_pairs={{0,2},{1,3},{2,0},{3,1},{4,6},{5,7},{6,4},{7,5},{8,10},{9,11},{10,... | collective-permute-start | bytes 98312 | tf_op jit(solution)/shard_map/ppermute | solution.py:211
  31.1 0.4 %collective-permute-start.14 = (bf16[128,128]{1,0:T(8,128)(2,1)S(1)}, bf16[128,128]{1,0:T(8,128)(2,1)S(1)}, u32[]{:S(2)}, u32[]{:S(2)}) collective-permute-start(bf16[128,128]{1,0:T(8,128)(2,1)S(1)} %get-tuple-element.40), channel_id=1, source_target_pairs={{0,3},{1,2},{2,1},{3,0},{4,7},{5,6},{6,5},{7,4},{8,11},{9,10},{10,... | collective-permute-start | bytes 98312 | tf_op jit(solution)/shard_map/ppermute | solution.py:211
  31.5 2.1 %collective-permute-done.13.refs_2_ = bf16[128,128]{1,0:T(8,128)(2,1)S(1)} collective-permute-done((bf16[128,128]{1,0:T(8,128)(2,1)S(1)}, bf16[128,128]{1,0:T(8,128)(2,1)S(1)}, u32[]{:S(2)}, u32[]{:S(2)}) %collective-permute-start.13) | collective-permute-done | bytes 32800 | tf_op jit(solution)/shard_map/ppermute | solution.py:211
  33.6 0.8 %collective-permute-done.14.refs_3_ = bf16[128,128]{1,0:T(8,128)(2,1)S(1)} collective-permute-done((bf16[128,128]{1,0:T(8,128)(2,1)S(1)}, bf16[128,128]{1,0:T(8,128)(2,1)S(1)}, u32[]{:S(2)}, u32[]{:S(2)}) %collective-permute-start.14) | collective-permute-done | bytes 32800 | tf_op jit(solution)/shard_map/ppermute | solution.py:211
  34.4 0.0 collective-permute-done.12.refs_1_
  34.4 0.7 %shard_map.53 = f32[128,256]{1,0:T(8,128)} custom-call(f32[128,128]{1,0:T(8,128)S(1)} %get-tuple-element.37.refs_0_, f32[128,128]{1,0:T(8,128)S(1)} %collective-permute-done.12.refs_1_, bf16[128,128]{1,0:T(8,128)(2,1)S(1)} %collective-permute-done.13.refs_2_, bf16[128,128]{1,0:T(8,128)(2,1)S(1)} %collective-permute-done.14.refs_3_), custom_call_target="tpu_custom_call" | custom-call | tf_op jit(solution)/shard_map/pallas_call | solution.py:310
  (4 shorter events, 0.1 us)
Async XLA Ops:
  2.3 1.6 %collective-permute-start = (bf16[512,128]{1,0:T(8,128)(2,1)S(1)}, bf16[512,128]{1,0:T(8,128)(2,1)S(1)}, u32[]{:S(2)}, u32[]{:S(2)}) collective-permute-start(bf16[512,128]{1,0:T(8,128)(2,1)S(1)} %get-tuple-element.26), channel_id=1, source_target_pairs={{0,1},{1,0},{2,3},{3,2},{4,5},{5,4},{6,7},{7,6},{8,9},{9,8},{10,11... | collective-permute-start | bytes 393224 | tf_op jit(solution)/shard_map/ppermute | solution.py:211
  3.9 5.9 %collective-permute-start.4 = (bf16[256,128]{1,0:T(8,128)(2,1)S(1)}, bf16[256,128]{1,0:T(8,128)(2,1)S(1)}, u32[]{:S(2)}, u32[]{:S(2)}) collective-permute-start(bf16[256,128]{1,0:T(8,128)(2,1)S(1)} %get-tuple-element.30), channel_id=1, source_target_pairs={{0,2},{1,3},{2,0},{3,1},{4,6},{5,7},{6,4},{7,5},{8,10},{9,11},{10,... | collective-permute-start | bytes 196616 | tf_op jit(solution)/shard_map/ppermute | solution.py:211
  6.7 8.1 %collective-permute-start.1 = (bf16[512,512]{1,0:T(8,128)(2,1)S(1)}, bf16[512,512]{1,0:T(8,128)(2,1)S(1)}, u32[]{:S(2)}, u32[]{:S(2)}) collective-permute-start(bf16[512,512]{1,0:T(8,128)(2,1)S(1)} %get-tuple-element.28.dense.own), channel_id=1, source_target_pairs={{0,1},{1,0},{2,3},{3,2},{4,5},{5,4},{6,7},{7,6},{8,9},{9,8},{10,11... | collective-permute-start | bytes 1572872 | tf_op jit(solution)/shard_map/ppermute | solution.py:211
  6.7 8.0 %collective-permute-start.3 = (bf16[256,128]{1,0:T(8,128)(2,1)S(1)}, bf16[256,128]{1,0:T(8,128)(2,1)S(1)}, u32[]{:S(2)}, u32[]{:S(2)}) collective-permute-start(bf16[256,128]{1,0:T(8,128)(2,1)S(1)} %get-tuple-element.30), channel_id=1, source_target_pairs={{0,6},{2,4},{4,10},{6,8},{8,14},{10,12},{12,2},{14,0},{1,7},{3,5},... | collective-permute-start | bytes 196616 | tf_op jit(solution)/shard_map/ppermute | solution.py:223
  8.3 6.5 %collective-permute-start.2 = (bf16[256,128]{1,0:T(8,128)(2,1)S(1)}, bf16[256,128]{1,0:T(8,128)(2,1)S(1)}, u32[]{:S(2)}, u32[]{:S(2)}) collective-permute-start(bf16[256,128]{1,0:T(8,128)(2,1)S(1)} %get-tuple-element.29), channel_id=1, source_target_pairs={{0,4},{2,6},{4,8},{6,10},{8,12},{10,14},{12,0},{14,2},{1,5},{3,7},... | collective-permute-start | bytes 196616 | tf_op jit(solution)/shard_map/ppermute | solution.py:223
  9.9 7.3 %collective-permute-start.6 = (bf16[256,128]{1,0:T(8,128)(2,1)S(1)}, bf16[256,128]{1,0:T(8,128)(2,1)S(1)}, u32[]{:S(2)}, u32[]{:S(2)}) collective-permute-start(bf16[256,128]{1,0:T(8,128)(2,1)S(1)} %add_convert_fusion.2.refs_1_), channel_id=1, source_target_pairs={{0,8},{2,10},{4,12},{6,14},{8,0},{10,2},{12,4},{14,6},{1,13},{3,15... | collective-permute-start | bytes 196616 | tf_op jit(solution)/shard_map/ppermute | solution.py:223
  12.2 5.4 %collective-permute-start.5 = (bf16[256,128]{1,0:T(8,128)(2,1)S(1)}, bf16[256,128]{1,0:T(8,128)(2,1)S(1)}, u32[]{:S(2)}, u32[]{:S(2)}) collective-permute-start(bf16[256,128]{1,0:T(8,128)(2,1)S(1)} %add_convert_fusion.2.refs_1_), channel_id=1, source_target_pairs={{0,12},{2,14},{4,0},{6,2},{8,4},{10,6},{12,8},{14,10},{1,9},{3,11}... | collective-permute-start | bytes 196616 | tf_op jit(solution)/shard_map/ppermute | solution.py:223
  17.9 4.3 %collective-permute-start.9 = (bf16[256,128]{1,0:T(8,128)(2,1)S(1)}, bf16[256,128]{1,0:T(8,128)(2,1)S(1)}, u32[]{:S(2)}, u32[]{:S(2)}) collective-permute-start(bf16[256,128]{1,0:T(8,128)(2,1)S(1)} %get-tuple-element.35), channel_id=1, source_target_pairs={{0,2},{1,3},{2,0},{3,1},{4,6},{5,7},{6,4},{7,5},{8,10},{9,11},{10,... | collective-permute-start | bytes 196616 | tf_op jit(solution)/shard_map/ppermute | solution.py:211
  19.5 7.9 %collective-permute-start.8 = (bf16[256,128]{1,0:T(8,128)(2,1)S(1)}, bf16[256,128]{1,0:T(8,128)(2,1)S(1)}, u32[]{:S(2)}, u32[]{:S(2)}) collective-permute-start(bf16[256,128]{1,0:T(8,128)(2,1)S(1)} %get-tuple-element.35), channel_id=1, source_target_pairs={{0,6},{2,4},{4,10},{6,8},{8,14},{10,12},{12,2},{14,0},{1,7},{3,5},... | collective-permute-start | bytes 196616 | tf_op jit(solution)/shard_map/ppermute | solution.py:223
  20.7 6.7 %collective-permute-start.7 = (bf16[256,128]{1,0:T(8,128)(2,1)S(1)}, bf16[256,128]{1,0:T(8,128)(2,1)S(1)}, u32[]{:S(2)}, u32[]{:S(2)}) collective-permute-start(bf16[256,128]{1,0:T(8,128)(2,1)S(1)} %get-tuple-element.34), channel_id=1, source_target_pairs={{0,4},{2,6},{4,8},{6,10},{8,12},{10,14},{12,0},{14,2},{1,5},{3,7},... | collective-permute-start | bytes 196616 | tf_op jit(solution)/shard_map/ppermute | solution.py:223
  22.3 6.9 %collective-permute-start.11 = (bf16[256,128]{1,0:T(8,128)(2,1)S(1)}, bf16[256,128]{1,0:T(8,128)(2,1)S(1)}, u32[]{:S(2)}, u32[]{:S(2)}) collective-permute-start(bf16[256,128]{1,0:T(8,128)(2,1)S(1)} %add_convert_fusion.refs_1_), channel_id=1, source_target_pairs={{0,8},{2,10},{4,12},{6,14},{8,0},{10,2},{12,4},{14,6},{1,13},{3,15... | collective-permute-start | bytes 196616 | tf_op jit(solution)/shard_map/ppermute | solution.py:223
  23.9 5.3 %collective-permute-start.10 = (bf16[256,128]{1,0:T(8,128)(2,1)S(1)}, bf16[256,128]{1,0:T(8,128)(2,1)S(1)}, u32[]{:S(2)}, u32[]{:S(2)}) collective-permute-start(bf16[256,128]{1,0:T(8,128)(2,1)S(1)} %add_convert_fusion.refs_1_), channel_id=1, source_target_pairs={{0,12},{2,14},{4,0},{6,2},{8,4},{10,6},{12,8},{14,10},{1,9},{3,11}... | collective-permute-start | bytes 196616 | tf_op jit(solution)/shard_map/ppermute | solution.py:223
  29.5 4.9 %collective-permute-start.12 = (f32[128,128]{1,0:T(8,128)S(1)}, f32[128,128]{1,0:T(8,128)S(1)}, u32[]{:S(2)}, u32[]{:S(2)}) collective-permute-start(f32[128,128]{1,0:T(8,128)S(1)} %get-tuple-element.38), channel_id=1, source_target_pairs={{0,1},{1,0},{2,3},{3,2},{4,5},{5,4},{6,7},{7,6},{8,9},{9,8},{10,11... | collective-permute-start | bytes 196616 | tf_op jit(solution)/shard_map/ppermute | solution.py:211
  29.6 4.0 %collective-permute-start.13 = (bf16[128,128]{1,0:T(8,128)(2,1)S(1)}, bf16[128,128]{1,0:T(8,128)(2,1)S(1)}, u32[]{:S(2)}, u32[]{:S(2)}) collective-permute-start(bf16[128,128]{1,0:T(8,128)(2,1)S(1)} %get-tuple-element.39), channel_id=1, source_target_pairs={{0,2},{1,3},{2,0},{3,1},{4,6},{5,7},{6,4},{7,5},{8,10},{9,11},{10,... | collective-permute-start | bytes 98312 | tf_op jit(solution)/shard_map/ppermute | solution.py:211
  31.1 3.3 %collective-permute-start.14 = (bf16[128,128]{1,0:T(8,128)(2,1)S(1)}, bf16[128,128]{1,0:T(8,128)(2,1)S(1)}, u32[]{:S(2)}, u32[]{:S(2)}) collective-permute-start(bf16[128,128]{1,0:T(8,128)(2,1)S(1)} %get-tuple-element.40), channel_id=1, source_target_pairs={{0,3},{1,2},{2,1},{3,0},{4,7},{5,6},{6,5},{7,4},{8,11},{9,10},{10,... | collective-permute-start | bytes 98312 | tf_op jit(solution)/shard_map/ppermute | solution.py:211

commit v5 on v4

--- a/solution.py
+++ b/solution.py
@@ -64,7 +64,7 @@
 
 def first_kernel(
     steps, columns, scale, tiles_hbm, dest_hbm, count_hbm, seeds_hbm,
-    dense, send, seed_rows,
+    dense, send, seed_rows, restart_other,
     tiles, dest, count, seeds, total, ids, weights, tile_sem, table_sem,
 ):
     slots, edge = tiles.shape[1], tiles.shape[2]
@@ -106,6 +106,7 @@
             total[slot, rows, :] += tiles[s, t].astype(jnp.float32)
         dense[:, s * edge : (s + 1) * edge] = total[slot, : columns * edge, :].astype(jnp.bfloat16)
 
+    restart_other[...] = (1.0 - damping) * (scale * field(counts[0], 0))
     restart = source_rows(counts, scale, steps)
     send[...] = jnp.dot(dense[...], restart, preferred_element_type=jnp.float32).astype(jnp.bfloat16)
 
@@ -185,21 +186,21 @@
             block = lax.rem(chip + d, chips) * CORES + owner
             rows = pl.ds(pl.multiple_of(block * edge, edge), edge)
             part = near[rows, :] + product((own, other), scores, rows, steps - len(scores), steps)
-            if d == 0:
-                rows = pl.ds(pl.multiple_of(owner * edge, edge), edge)
+            if d == e == 0:
+                rows = pl.ds(pl.multiple_of(core * edge, edge), edge)
                 part = damping * part + restart[rows, :]
             ref = parts[d * CORES + e]
             ref[...] = part.astype(ref.dtype)
 
 
-def final_kernel(chips, *refs):
+def final_kernel(chips, own, restart, *refs):
     parts, out = refs[:-1], refs[-1]
     _, _, core = place()
-    topics = parts[0].shape[1]
+    topics = own.shape[1]
     for e in range(CORES):
-        total = sum(parts[d * CORES + e][...].astype(jnp.float32) for d in range(1, chips))
-        lanes = pl.ds(pl.multiple_of(lax.rem(core + e, CORES) * topics, topics), topics)
-        out[:, lanes] = parts[e][...] + damping * total
+        total = sum(ref[...].astype(jnp.float32) for ref in parts[e::CORES])
+        lanes = pl.ds(pl.multiple_of(lax.rem(core + 1 - e, CORES) * topics, topics), topics)
+        out[:, lanes] = (restart if e == 0 else own)[...] + damping * total
 
 
 def from_col(value, chips, chip_step, core_step):
@@ -247,10 +248,15 @@
         )
 
     matrix = 2 * dests * sources
-    dense, send, seed_rows = call(
+    dense, send, seed_rows, restart_other = call(
         functools.partial(first_kernel, steps, columns, scale),
         [HBM] * 4,
-        [shape(bf16, dests, sources), shape(bf16, dests, topics), shape(i32, seeds, topics)],
+        [
+            shape(bf16, dests, sources),
+            shape(bf16, dests, topics),
+            shape(i32, seeds, topics),
+            shape(f32, edge, topics),
+        ],
         6 * MIB + 2 * matrix + 2 * steps * slots * edge * edge,
         [
             pltpu.VMEM((steps, slots, edge, edge), bf16),
@@ -300,19 +306,18 @@
             parts = call(
                 functools.partial(last_kernel, steps, chips),
                 [VMEM] * (4 + far),
-                [shape(f32, edge, topics)] * CORES + [shape(bf16, edge, topics)] * (CORES * (chips - 1)),
+                [shape(f32, edge, topics)] + [shape(bf16, edge, topics)] * (CORES * chips - 1),
                 room,
             )(dense, other, near, restart, *arriving)
-    arrived = [
-        part if d == e == 0 else from_col(part, chips, d, e)
-        for (d, e), part in zip([(d, e) for d in range(chips) for e in range(CORES)], parts)
-    ]
+    own, core, *away = parts
+    moved = [from_col(core, chips, 0, 1)]
+    moved += [from_col(part, chips, 1 + i // CORES, i % CORES) for i, part in enumerate(away)]
     (out,) = call(
         functools.partial(final_kernel, chips),
-        [VMEM] * len(arrived),
+        [VMEM] * (2 + len(moved)),
         [shape(f32, edge, CORES * topics)],
         4 * MIB,
-    )(*arrived)
+    )(own, restart_other, *moved[:0:-1], moved[0])
     return out
 
 

time: 35.2 us -> 34.4 us (0.977)
  waiting for transfers between devices: 10.1 us -> 9.26 us
    ppermute x7, waiting for transfers between devices: 4.09 us -> 3.29 us  [from_col(): return lax.ppermute(value, 'col', route)]
where the time goes in v5:
time: 34.4 us; the launch traced here: 34.3 us
  starting transfers between devices  19.5 us (57%)
  waiting for transfers between devices  9.26 us (27%)
  Pallas kernels  5.33 us (15%)
    ppermute x8, starting transfers between devices, from_behind(): return lax.ppermute(value, ('blk', 'col'), route)  12.7 us
    ppermute x7, starting transfers between devices, from_col(): return lax.ppermute(value, 'col', route)  6.81 us
    ppermute x8, waiting for transfers between devices, from_behind(): return lax.ppermute(value, ('blk', 'col'), route)  5.97 us
    ppermute x7, waiting for transfers between devices, from_col(): return lax.ppermute(value, 'col', route)  3.29 us
    pallas_call x1, Pallas kernels, body(): call(functools.partial(first_kernel, steps, columns, scale), [HBM] * 4, [...  2.25 us
    pallas_call x1, Pallas kernels, body(): call(functools.partial(keep_kernel, steps, columns, scale), [VMEM] * 2, [...  1.08 us
  transfers between devices with their start and end apart: 15, of which 8 were waited for; matrix products, arithmetic and copies ran while one was open for 0% of the time, Pallas kernels for 5%

profile of v5, /device:TPU:0, one launch (start us, length us, event | category | flops | bytes accessed | tf_op | source)
XLA Modules:
  0.0 34.3 jit_solution(8045489571321745541)
XLA Ops:
  0.0 2.2 %shard_map.46 = (bf16[512,512]{1,0:T(8,128)(2,1)S(1)}, bf16[512,128]{1,0:T(8,128)(2,1)S(1)}, s32[64,128]{1,0:T(8,128)S(1)}, f32[128,128]{1,0:T(8,128)S(1)}) custom-call(bf16[1,1,4,10,128,128]{5,4,3,2,1,0:T(8,128)(2,1)} %tiles_hbm.1, s32[1,1,4,10]{3,2,1,0:T(4,128)} %dest_hbm.1, s32[1,1,4]{2,1,0:T(1,128)} %count_hbm.1, s32[64,256]{1,0:T(8,128)} %bitcast.1), custom_call_target="tpu_custom_call" | custom-call | tf_op jit(solution)/shard_map/pallas_call | solution.py:251
  2.3 0.5 %collective-permute-start = (bf16[512,128]{1,0:T(8,128)(2,1)S(1)}, bf16[512,128]{1,0:T(8,128)(2,1)S(1)}, u32[]{:S(2)}, u32[]{:S(2)}) collective-permute-start(bf16[512,128]{1,0:T(8,128)(2,1)S(1)} %get-tuple-element.27), channel_id=1, source_target_pairs={{0,1},{1,0},{2,3},{3,2},{4,5},{5,4},{6,7},{7,6},{8,9},{9,8},{10,11... | collective-permute-start | bytes 393224 | tf_op jit(solution)/shard_map/ppermute | solution.py:212
  2.8 1.1 %shard_map.47 = (f32[512,128]{1,0:T(8,128)S(1)}, f32[256,128]{1,0:T(8,128)S(1)}, f32[256,128]{1,0:T(8,128)S(1)}) custom-call(bf16[512,512]{1,0:T(8,128)(2,1)S(1)} %get-tuple-element.29.dense.own, s32[64,128]{1,0:T(8,128)S(1)} %get-tuple-element.25.seed_rows), custom_call_target="tpu_custom_call" | custom-call | tf_op jit(solution)/shard_map/pallas_call | solution.py:274
  3.9 0.0 collective-permute-done.recv
  3.9 0.1 shard_map.48
  3.9 2.8 %collective-permute-start.4 = (bf16[256,128]{1,0:T(8,128)(2,1)S(1)}, bf16[256,128]{1,0:T(8,128)(2,1)S(1)}, u32[]{:S(2)}, u32[]{:S(2)}) collective-permute-start(bf16[256,128]{1,0:T(8,128)(2,1)S(1)} %get-tuple-element.31), channel_id=1, source_target_pairs={{0,2},{1,3},{2,0},{3,1},{4,6},{5,7},{6,4},{7,5},{8,10},{9,11},{10,... | collective-permute-start | bytes 196616 | tf_op jit(solution)/shard_map/ppermute | solution.py:212
  6.7 0.0 collective-permute-start.1
  6.7 1.5 %collective-permute-start.3 = (bf16[256,128]{1,0:T(8,128)(2,1)S(1)}, bf16[256,128]{1,0:T(8,128)(2,1)S(1)}, u32[]{:S(2)}, u32[]{:S(2)}) collective-permute-start(bf16[256,128]{1,0:T(8,128)(2,1)S(1)} %get-tuple-element.31), channel_id=1, source_target_pairs={{0,6},{2,4},{4,10},{6,8},{8,14},{10,12},{12,2},{14,0},{1,7},{3,5},... | collective-permute-start | bytes 196616 | tf_op jit(solution)/shard_map/ppermute | solution.py:224
  8.3 1.6 %collective-permute-start.2 = (bf16[256,128]{1,0:T(8,128)(2,1)S(1)}, bf16[256,128]{1,0:T(8,128)(2,1)S(1)}, u32[]{:S(2)}, u32[]{:S(2)}) collective-permute-start(bf16[256,128]{1,0:T(8,128)(2,1)S(1)} %get-tuple-element.30), channel_id=1, source_target_pairs={{0,4},{2,6},{4,8},{6,10},{8,12},{10,14},{12,0},{14,2},{1,5},{3,7},... | collective-permute-start | bytes 196616 | tf_op jit(solution)/shard_map/ppermute | solution.py:224
  9.8 0.0 collective-permute-done.4
  9.9 2.3 %collective-permute-start.6 = (bf16[256,128]{1,0:T(8,128)(2,1)S(1)}, bf16[256,128]{1,0:T(8,128)(2,1)S(1)}, u32[]{:S(2)}, u32[]{:S(2)}) collective-permute-start(bf16[256,128]{1,0:T(8,128)(2,1)S(1)} %add_convert_fusion.2.refs_1_), channel_id=1, source_target_pairs={{0,8},{2,10},{4,12},{6,14},{8,0},{10,2},{12,4},{14,6},{1,13},{3,15... | collective-permute-start | bytes 196616 | tf_op jit(solution)/shard_map/ppermute | solution.py:224
  12.2 1.7 %collective-permute-start.5 = (bf16[256,128]{1,0:T(8,128)(2,1)S(1)}, bf16[256,128]{1,0:T(8,128)(2,1)S(1)}, u32[]{:S(2)}, u32[]{:S(2)}) collective-permute-start(bf16[256,128]{1,0:T(8,128)(2,1)S(1)} %add_convert_fusion.2.refs_1_), channel_id=1, source_target_pairs={{0,12},{2,14},{4,0},{6,2},{8,4},{10,6},{12,8},{14,10},{1,9},{3,11}... | collective-permute-start | bytes 196616 | tf_op jit(solution)/shard_map/ppermute | solution.py:224
  13.9 0.8 %collective-permute-done.2 = bf16[256,128]{1,0:T(8,128)(2,1)S(1)} collective-permute-done((bf16[256,128]{1,0:T(8,128)(2,1)S(1)}, bf16[256,128]{1,0:T(8,128)(2,1)S(1)}, u32[]{:S(2)}, u32[]{:S(2)}) %collective-permute-start.2) | collective-permute-done | bytes 65568 | tf_op jit(solution)/shard_map/ppermute | solution.py:224
  14.7 0.0 collective-permute-done.3
  14.8 0.0 collective-permute-done.1.other
  14.8 0.3 shard_map.49.near
  15.1 2.1 %collective-permute-done.6.refs_1_ = bf16[256,128]{1,0:T(8,128)(2,1)S(1)} collective-permute-done((bf16[256,128]{1,0:T(8,128)(2,1)S(1)}, bf16[256,128]{1,0:T(8,128)(2,1)S(1)}, u32[]{:S(2)}, u32[]{:S(2)}) %collective-permute-start.6) | collective-permute-done | bytes 65568 | tf_op jit(solution)/shard_map/ppermute | solution.py:224
  17.2 0.4 %collective-permute-done.5.refs_0_ = bf16[256,128]{1,0:T(8,128)(2,1)S(1)} collective-permute-done((bf16[256,128]{1,0:T(8,128)(2,1)S(1)}, bf16[256,128]{1,0:T(8,128)(2,1)S(1)}, u32[]{:S(2)}, u32[]{:S(2)}) %collective-permute-start.5) | collective-permute-done | bytes 65568 | tf_op jit(solution)/shard_map/ppermute | solution.py:224
  17.6 0.3 shard_map.50
  17.9 1.6 %collective-permute-start.9 = (bf16[256,128]{1,0:T(8,128)(2,1)S(1)}, bf16[256,128]{1,0:T(8,128)(2,1)S(1)}, u32[]{:S(2)}, u32[]{:S(2)}) collective-permute-start(bf16[256,128]{1,0:T(8,128)(2,1)S(1)} %get-tuple-element.36), channel_id=1, source_target_pairs={{0,2},{1,3},{2,0},{3,1},{4,6},{5,7},{6,4},{7,5},{8,10},{9,11},{10,... | collective-permute-start | bytes 196616 | tf_op jit(solution)/shard_map/ppermute | solution.py:212
  19.5 1.2 %collective-permute-start.8 = (bf16[256,128]{1,0:T(8,128)(2,1)S(1)}, bf16[256,128]{1,0:T(8,128)(2,1)S(1)}, u32[]{:S(2)}, u32[]{:S(2)}) collective-permute-start(bf16[256,128]{1,0:T(8,128)(2,1)S(1)} %get-tuple-element.36), channel_id=1, source_target_pairs={{0,6},{2,4},{4,10},{6,8},{8,14},{10,12},{12,2},{14,0},{1,7},{3,5},... | collective-permute-start | bytes 196616 | tf_op jit(solution)/shard_map/ppermute | solution.py:224
  20.7 0.4 %collective-permute-start.7 = (bf16[256,128]{1,0:T(8,128)(2,1)S(1)}, bf16[256,128]{1,0:T(8,128)(2,1)S(1)}, u32[]{:S(2)}, u32[]{:S(2)}) collective-permute-start(bf16[256,128]{1,0:T(8,128)(2,1)S(1)} %get-tuple-element.35), channel_id=1, source_target_pairs={{0,4},{2,6},{4,8},{6,10},{8,12},{10,14},{12,0},{14,2},{1,5},{3,7},... | collective-permute-start | bytes 196616 | tf_op jit(solution)/shard_map/ppermute | solution.py:224
  21.1 1.1 %collective-permute-done.9 = bf16[256,128]{1,0:T(8,128)(2,1)S(1)} collective-permute-done((bf16[256,128]{1,0:T(8,128)(2,1)S(1)}, bf16[256,128]{1,0:T(8,128)(2,1)S(1)}, u32[]{:S(2)}, u32[]{:S(2)}) %collective-permute-start.9) | collective-permute-done | bytes 65568 | tf_op jit(solution)/shard_map/ppermute | solution.py:212
  22.3 1.7 %collective-permute-start.11 = (bf16[256,128]{1,0:T(8,128)(2,1)S(1)}, bf16[256,128]{1,0:T(8,128)(2,1)S(1)}, u32[]{:S(2)}, u32[]{:S(2)}) collective-permute-start(bf16[256,128]{1,0:T(8,128)(2,1)S(1)} %add_convert_fusion.refs_1_), channel_id=1, source_target_pairs={{0,8},{2,10},{4,12},{6,14},{8,0},{10,2},{12,4},{14,6},{1,13},{3,15... | collective-permute-start | bytes 196616 | tf_op jit(solution)/shard_map/ppermute | solution.py:224
  23.9 2.3 %collective-permute-start.10 = (bf16[256,128]{1,0:T(8,128)(2,1)S(1)}, bf16[256,128]{1,0:T(8,128)(2,1)S(1)}, u32[]{:S(2)}, u32[]{:S(2)}) collective-permute-start(bf16[256,128]{1,0:T(8,128)(2,1)S(1)} %add_convert_fusion.refs_1_), channel_id=1, source_target_pairs={{0,12},{2,14},{4,0},{6,2},{8,4},{10,6},{12,8},{14,10},{1,9},{3,11}... | collective-permute-start | bytes 196616 | tf_op jit(solution)/shard_map/ppermute | solution.py:224
  26.2 1.2 %collective-permute-done.7 = bf16[256,128]{1,0:T(8,128)(2,1)S(1)} collective-permute-done((bf16[256,128]{1,0:T(8,128)(2,1)S(1)}, bf16[256,128]{1,0:T(8,128)(2,1)S(1)}, u32[]{:S(2)}, u32[]{:S(2)}) %collective-permute-start.7) | collective-permute-done | bytes 65568 | tf_op jit(solution)/shard_map/ppermute | solution.py:224
  27.4 0.0 collective-permute-done.8
  27.4 0.3 shard_map.51.near
  27.8 1.4 %collective-permute-done.11.refs_1_ = bf16[256,128]{1,0:T(8,128)(2,1)S(1)} collective-permute-done((bf16[256,128]{1,0:T(8,128)(2,1)S(1)}, bf16[256,128]{1,0:T(8,128)(2,1)S(1)}, u32[]{:S(2)}, u32[]{:S(2)}) %collective-permute-start.11) | collective-permute-done | bytes 65568 | tf_op jit(solution)/shard_map/ppermute | solution.py:224
  29.2 0.0 collective-permute-done.10.refs_0_
  29.2 0.3 shard_map.52
  29.5 0.1 collective-permute-start.12
  29.6 1.5 %collective-permute-start.13 = (bf16[128,128]{1,0:T(8,128)(2,1)S(1)}, bf16[128,128]{1,0:T(8,128)(2,1)S(1)}, u32[]{:S(2)}, u32[]{:S(2)}) collective-permute-start(bf16[128,128]{1,0:T(8,128)(2,1)S(1)} %get-tuple-element.41), channel_id=1, source_target_pairs={{0,2},{1,3},{2,0},{3,1},{4,6},{5,7},{6,4},{7,5},{8,10},{9,11},{10,... | collective-permute-start | bytes 98312 | tf_op jit(solution)/shard_map/ppermute | solution.py:212
  31.1 0.4 %collective-permute-start.14 = (bf16[128,128]{1,0:T(8,128)(2,1)S(1)}, bf16[128,128]{1,0:T(8,128)(2,1)S(1)}, u32[]{:S(2)}, u32[]{:S(2)}) collective-permute-start(bf16[128,128]{1,0:T(8,128)(2,1)S(1)} %get-tuple-element.42), channel_id=1, source_target_pairs={{0,1},{1,0},{2,3},{3,2},{4,5},{5,4},{6,7},{7,6},{8,9},{9,8},{10,11... | collective-permute-start | bytes 98312 | tf_op jit(solution)/shard_map/ppermute | solution.py:212
  31.4 1.8 %collective-permute-done.12.refs_0_ = bf16[128,128]{1,0:T(8,128)(2,1)S(1)} collective-permute-done((bf16[128,128]{1,0:T(8,128)(2,1)S(1)}, bf16[128,128]{1,0:T(8,128)(2,1)S(1)}, u32[]{:S(2)}, u32[]{:S(2)}) %collective-permute-start.12) | collective-permute-done | bytes 32800 | tf_op jit(solution)/shard_map/ppermute | solution.py:212
  33.2 0.3 collective-permute-done.13.refs_1_
  33.6 0.0 collective-permute-done.14.refs_2_
  33.6 0.7 %shard_map.53 = f32[128,256]{1,0:T(8,128)} custom-call(f32[128,128]{1,0:T(8,128)S(1)} %get-tuple-element.38.own, f32[128,128]{1,0:T(8,128)S(1)} %get-tuple-element.39.restart, bf16[128,128]{1,0:T(8,128)(2,1)S(1)} %collective-permute-done.12.refs_0_, bf16[128,128]{1,0:T(8,128)(2,1)S(1)} %collective-permute-done.13.refs_1_, ...), custom_call_target="tpu_custom_call" | custom-call | tf_op jit(solution)/shard_map/pallas_call | solution.py:315
  (4 shorter events, 0.1 us)
Async XLA Ops:
  2.3 1.6 %collective-permute-start = (bf16[512,128]{1,0:T(8,128)(2,1)S(1)}, bf16[512,128]{1,0:T(8,128)(2,1)S(1)}, u32[]{:S(2)}, u32[]{:S(2)}) collective-permute-start(bf16[512,128]{1,0:T(8,128)(2,1)S(1)} %get-tuple-element.27), channel_id=1, source_target_pairs={{0,1},{1,0},{2,3},{3,2},{4,5},{5,4},{6,7},{7,6},{8,9},{9,8},{10,11... | collective-permute-start | bytes 393224 | tf_op jit(solution)/shard_map/ppermute | solution.py:212
  3.9 5.9 %collective-permute-start.4 = (bf16[256,128]{1,0:T(8,128)(2,1)S(1)}, bf16[256,128]{1,0:T(8,128)(2,1)S(1)}, u32[]{:S(2)}, u32[]{:S(2)}) collective-permute-start(bf16[256,128]{1,0:T(8,128)(2,1)S(1)} %get-tuple-element.31), channel_id=1, source_target_pairs={{0,2},{1,3},{2,0},{3,1},{4,6},{5,7},{6,4},{7,5},{8,10},{9,11},{10,... | collective-permute-start | bytes 196616 | tf_op jit(solution)/shard_map/ppermute | solution.py:212
  6.7 8.1 %collective-permute-start.1 = (bf16[512,512]{1,0:T(8,128)(2,1)S(1)}, bf16[512,512]{1,0:T(8,128)(2,1)S(1)}, u32[]{:S(2)}, u32[]{:S(2)}) collective-permute-start(bf16[512,512]{1,0:T(8,128)(2,1)S(1)} %get-tuple-element.29.dense.own), channel_id=1, source_target_pairs={{0,1},{1,0},{2,3},{3,2},{4,5},{5,4},{6,7},{7,6},{8,9},{9,8},{10,11... | collective-permute-start | bytes 1572872 | tf_op jit(solution)/shard_map/ppermute | solution.py:212
  6.7 8.0 %collective-permute-start.3 = (bf16[256,128]{1,0:T(8,128)(2,1)S(1)}, bf16[256,128]{1,0:T(8,128)(2,1)S(1)}, u32[]{:S(2)}, u32[]{:S(2)}) collective-permute-start(bf16[256,128]{1,0:T(8,128)(2,1)S(1)} %get-tuple-element.31), channel_id=1, source_target_pairs={{0,6},{2,4},{4,10},{6,8},{8,14},{10,12},{12,2},{14,0},{1,7},{3,5},... | collective-permute-start | bytes 196616 | tf_op jit(solution)/shard_map/ppermute | solution.py:224
  8.3 6.5 %collective-permute-start.2 = (bf16[256,128]{1,0:T(8,128)(2,1)S(1)}, bf16[256,128]{1,0:T(8,128)(2,1)S(1)}, u32[]{:S(2)}, u32[]{:S(2)}) collective-permute-start(bf16[256,128]{1,0:T(8,128)(2,1)S(1)} %get-tuple-element.30), channel_id=1, source_target_pairs={{0,4},{2,6},{4,8},{6,10},{8,12},{10,14},{12,0},{14,2},{1,5},{3,7},... | collective-permute-start | bytes 196616 | tf_op jit(solution)/shard_map/ppermute | solution.py:224
  9.9 7.3 %collective-permute-start.6 = (bf16[256,128]{1,0:T(8,128)(2,1)S(1)}, bf16[256,128]{1,0:T(8,128)(2,1)S(1)}, u32[]{:S(2)}, u32[]{:S(2)}) collective-permute-start(bf16[256,128]{1,0:T(8,128)(2,1)S(1)} %add_convert_fusion.2.refs_1_), channel_id=1, source_target_pairs={{0,8},{2,10},{4,12},{6,14},{8,0},{10,2},{12,4},{14,6},{1,13},{3,15... | collective-permute-start | bytes 196616 | tf_op jit(solution)/shard_map/ppermute | solution.py:224
  12.2 5.4 %collective-permute-start.5 = (bf16[256,128]{1,0:T(8,128)(2,1)S(1)}, bf16[256,128]{1,0:T(8,128)(2,1)S(1)}, u32[]{:S(2)}, u32[]{:S(2)}) collective-permute-start(bf16[256,128]{1,0:T(8,128)(2,1)S(1)} %add_convert_fusion.2.refs_1_), channel_id=1, source_target_pairs={{0,12},{2,14},{4,0},{6,2},{8,4},{10,6},{12,8},{14,10},{1,9},{3,11}... | collective-permute-start | bytes 196616 | tf_op jit(solution)/shard_map/ppermute | solution.py:224
  17.9 4.3 %collective-permute-start.9 = (bf16[256,128]{1,0:T(8,128)(2,1)S(1)}, bf16[256,128]{1,0:T(8,128)(2,1)S(1)}, u32[]{:S(2)}, u32[]{:S(2)}) collective-permute-start(bf16[256,128]{1,0:T(8,128)(2,1)S(1)} %get-tuple-element.36), channel_id=1, source_target_pairs={{0,2},{1,3},{2,0},{3,1},{4,6},{5,7},{6,4},{7,5},{8,10},{9,11},{10,... | collective-permute-start | bytes 196616 | tf_op jit(solution)/shard_map/ppermute | solution.py:212
  19.5 7.9 %collective-permute-start.8 = (bf16[256,128]{1,0:T(8,128)(2,1)S(1)}, bf16[256,128]{1,0:T(8,128)(2,1)S(1)}, u32[]{:S(2)}, u32[]{:S(2)}) collective-permute-start(bf16[256,128]{1,0:T(8,128)(2,1)S(1)} %get-tuple-element.36), channel_id=1, source_target_pairs={{0,6},{2,4},{4,10},{6,8},{8,14},{10,12},{12,2},{14,0},{1,7},{3,5},... | collective-permute-start | bytes 196616 | tf_op jit(solution)/shard_map/ppermute | solution.py:224
  20.7 6.7 %collective-permute-start.7 = (bf16[256,128]{1,0:T(8,128)(2,1)S(1)}, bf16[256,128]{1,0:T(8,128)(2,1)S(1)}, u32[]{:S(2)}, u32[]{:S(2)}) collective-permute-start(bf16[256,128]{1,0:T(8,128)(2,1)S(1)} %get-tuple-element.35), channel_id=1, source_target_pairs={{0,4},{2,6},{4,8},{6,10},{8,12},{10,14},{12,0},{14,2},{1,5},{3,7},... | collective-permute-start | bytes 196616 | tf_op jit(solution)/shard_map/ppermute | solution.py:224
  22.3 6.9 %collective-permute-start.11 = (bf16[256,128]{1,0:T(8,128)(2,1)S(1)}, bf16[256,128]{1,0:T(8,128)(2,1)S(1)}, u32[]{:S(2)}, u32[]{:S(2)}) collective-permute-start(bf16[256,128]{1,0:T(8,128)(2,1)S(1)} %add_convert_fusion.refs_1_), channel_id=1, source_target_pairs={{0,8},{2,10},{4,12},{6,14},{8,0},{10,2},{12,4},{14,6},{1,13},{3,15... | collective-permute-start | bytes 196616 | tf_op jit(solution)/shard_map/ppermute | solution.py:224
  23.9 5.3 %collective-permute-start.10 = (bf16[256,128]{1,0:T(8,128)(2,1)S(1)}, bf16[256,128]{1,0:T(8,128)(2,1)S(1)}, u32[]{:S(2)}, u32[]{:S(2)}) collective-permute-start(bf16[256,128]{1,0:T(8,128)(2,1)S(1)} %add_convert_fusion.refs_1_), channel_id=1, source_target_pairs={{0,12},{2,14},{4,0},{6,2},{8,4},{10,6},{12,8},{14,10},{1,9},{3,11}... | collective-permute-start | bytes 196616 | tf_op jit(solution)/shard_map/ppermute | solution.py:224
  29.5 3.7 %collective-permute-start.12 = (bf16[128,128]{1,0:T(8,128)(2,1)S(1)}, bf16[128,128]{1,0:T(8,128)(2,1)S(1)}, u32[]{:S(2)}, u32[]{:S(2)}) collective-permute-start(bf16[128,128]{1,0:T(8,128)(2,1)S(1)} %get-tuple-element.40), channel_id=1, source_target_pairs={{0,3},{1,2},{2,1},{3,0},{4,7},{5,6},{6,5},{7,4},{8,11},{9,10},{10,... | collective-permute-start | bytes 98312 | tf_op jit(solution)/shard_map/ppermute | solution.py:212
  29.6 4.0 %collective-permute-start.13 = (bf16[128,128]{1,0:T(8,128)(2,1)S(1)}, bf16[128,128]{1,0:T(8,128)(2,1)S(1)}, u32[]{:S(2)}, u32[]{:S(2)}) collective-permute-start(bf16[128,128]{1,0:T(8,128)(2,1)S(1)} %get-tuple-element.41), channel_id=1, source_target_pairs={{0,2},{1,3},{2,0},{3,1},{4,6},{5,7},{6,4},{7,5},{8,10},{9,11},{10,... | collective-permute-start | bytes 98312 | tf_op jit(solution)/shard_map/ppermute | solution.py:212
  31.1 2.5 %collective-permute-start.14 = (bf16[128,128]{1,0:T(8,128)(2,1)S(1)}, bf16[128,128]{1,0:T(8,128)(2,1)S(1)}, u32[]{:S(2)}, u32[]{:S(2)}) collective-permute-start(bf16[128,128]{1,0:T(8,128)(2,1)S(1)} %get-tuple-element.42), channel_id=1, source_target_pairs={{0,1},{1,0},{2,3},{3,2},{4,5},{5,4},{6,7},{7,6},{8,9},{9,8},{10,11... | collective-permute-start | bytes 98312 | tf_op jit(solution)/shard_map/ppermute | solution.py:212

commit v6 on v5

--- a/solution.py
+++ b/solution.py
@@ -11,6 +11,7 @@
 CORES = 2
 FIELD = 8
 PACKED = 4
+LOW = 32
 
 damping = 0.85
 
@@ -65,7 +66,7 @@
 def first_kernel(
     steps, columns, scale, tiles_hbm, dest_hbm, count_hbm, seeds_hbm,
     dense, send, seed_rows, restart_other,
-    tiles, dest, count, seeds, total, ids, weights, tile_sem, table_sem,
+    tiles, dest, count, seeds, total, ids, weights, split, tile_sem, table_sem,
 ):
     slots, edge = tiles.shape[1], tiles.shape[2]
     topics = seeds.shape[1] // CORES
@@ -85,17 +86,21 @@
         seeds[:, pl.ds(pl.multiple_of(c * topics, topics), topics)] for c in (core, 1 - core)
     )
     seed_rows[...] = own
-    ids[...] = other & (edge - 1)
+    ids[...] = other & (LOW - 1)
     source_weights(other, edge, steps, columns, row, chip * CORES + core, weights)
-    groups = weights.shape[0]
-    counts = [jnp.zeros((edge, topics), jnp.int32)] * groups
+    high = (other & (edge - 1)) // LOW
+    parts = edge // LOW
+    for g in range(weights.shape[0]):
+        for h in range(parts):
+            split[g * parts + h] = jnp.where(high == h, weights[g], 0)
+    counts = [jnp.zeros((LOW, topics), jnp.int32)] * split.shape[0]
     number, done = ids.shape[0], 0
 
     for fetch in fetch_tables[1:]:
         fetch.wait()
     for s in range(steps):
         upto = number * (steps + 1 + s) // (2 * steps)
-        counts = add_seeds(counts, ids, weights, done, upto)
+        counts = add_seeds(counts, ids, split, done, upto)
         done = upto
         fetch_tiles[s].wait()
         slot = s % total.shape[0]
@@ -106,6 +111,7 @@
             total[slot, rows, :] += tiles[s, t].astype(jnp.float32)
         dense[:, s * edge : (s + 1) * edge] = total[slot, : columns * edge, :].astype(jnp.bfloat16)
 
+    counts = [jnp.concatenate(counts[g : g + parts], axis=0) for g in range(0, len(counts), parts)]
     restart_other[...] = (1.0 - damping) * (scale * field(counts[0], 0))
     restart = source_rows(counts, scale, steps)
     send[...] = jnp.dot(dense[...], restart, preferred_element_type=jnp.float32).astype(jnp.bfloat16)
@@ -176,21 +182,19 @@
         sends[d][...] = part.astype(jnp.bfloat16)
 
 
-def last_kernel(steps, chips, own, other, near, restart, *refs):
-    scores, parts = refs[: -chips * CORES], refs[-chips * CORES :]
+def last_kernel(steps, chips, first, own, other, near, restart, *refs):
+    scores, parts = refs[: steps - 2], refs[steps - 2 :]
     _, chip, core = place()
     edge = parts[0].shape[0]
-    for d in range(chips):
-        for e in range(CORES):
-            owner = lax.rem(core + e, CORES)
-            block = lax.rem(chip + d, chips) * CORES + owner
-            rows = pl.ds(pl.multiple_of(block * edge, edge), edge)
-            part = near[rows, :] + product((own, other), scores, rows, steps - len(scores), steps)
-            if d == e == 0:
-                rows = pl.ds(pl.multiple_of(core * edge, edge), edge)
-                part = damping * part + restart[rows, :]
-            ref = parts[d * CORES + e]
-            ref[...] = part.astype(ref.dtype)
+    for i, ref in enumerate(parts):
+        d, e = first + i // CORES, i % CORES
+        block = lax.rem(chip + d, chips) * CORES + lax.rem(core + e, CORES)
+        rows = pl.ds(pl.multiple_of(block * edge, edge), edge)
+        part = near[rows, :] + product((own, other), scores, rows, steps - len(scores), steps)
+        if d == e == 0:
+            rows = pl.ds(pl.multiple_of(core * edge, edge), edge)
+            part = damping * part + restart[rows, :]
+        ref[...] = part.astype(ref.dtype)
 
 
 def final_kernel(chips, own, restart, *refs):
@@ -266,6 +270,7 @@
             pltpu.VMEM((2, dests + edge, edge), f32),
             pltpu.VMEM((seeds, topics), i32),
             pltpu.VMEM((groups, seeds, topics), i32),
+            pltpu.VMEM((groups * edge // LOW, seeds, topics), i32),
             pltpu.SemaphoreType.DMA((steps,)),
             pltpu.SemaphoreType.DMA((3,)),
         ],
@@ -303,12 +308,19 @@
                 functools.partial(step_kernel, steps, chips), [VMEM] * (3 + far), split, room
             )(dense, other, near, *arriving)
         else:
-            parts = call(
-                functools.partial(last_kernel, steps, chips),
+            away = call(
+                functools.partial(last_kernel, steps, chips, 1),
                 [VMEM] * (4 + far),
-                [shape(f32, edge, topics)] + [shape(bf16, edge, topics)] * (CORES * chips - 1),
+                [shape(bf16, edge, topics)] * (CORES * (chips - 1)),
                 room,
             )(dense, other, near, restart, *arriving)
+            home = call(
+                functools.partial(last_kernel, steps, chips, 0),
+                [VMEM] * (4 + far),
+                [shape(f32, edge, topics), shape(bf16, edge, topics)],
+                room,
+            )(dense, other, near, restart, *arriving)
+            parts = [*home, *away]
     own, core, *away = parts
     moved = [from_col(core, chips, 0, 1)]
     moved += [from_col(part, chips, 1 + i // CORES, i % CORES) for i, part in enumerate(away)]

time: 34.4 us -> 34.2 us (level)
  transfers between devices with their start and end apart: 15 -> 15, of which waited for: 8 -> 8; matrix products, arithmetic and copies ran while one was open for 0% -> 0% of each run, Pallas kernels for 5% -> 6%
where the time goes in v6:
time: 34.2 us; the launch traced here: 34.1 us
  starting transfers between devices  19.5 us (57%)
  waiting for transfers between devices  8.96 us (26%)
  Pallas kernels  5.38 us (16%)
    ppermute x8, starting transfers between devices, from_behind(): return lax.ppermute(value, ('blk', 'col'), route)  12.7 us
    ppermute x7, starting transfers between devices, from_col(): return lax.ppermute(value, 'col', route)  6.88 us
    ppermute x8, waiting for transfers between devices, from_behind(): return lax.ppermute(value, ('blk', 'col'), route)  5.98 us
    ppermute x7, waiting for transfers between devices, from_col(): return lax.ppermute(value, 'col', route)  2.98 us
    pallas_call x1, Pallas kernels, body(): call(functools.partial(first_kernel, steps, columns, scale), [HBM] * 4, [...  2.15 us
    pallas_call x1, Pallas kernels, body(): call(functools.partial(keep_kernel, steps, columns, scale), [VMEM] * 2, [...  1.08 us
  transfers between devices with their start and end apart: 15, of which 8 were waited for; matrix products, arithmetic and copies ran while one was open for 0% of the time, Pallas kernels for 6%

profile of v6, /device:TPU:0, one launch (start us, length us, event | category | flops | bytes accessed | tf_op | source)
XLA Modules:
  0.0 34.1 jit_solution(38832838284657099)
XLA Ops:
  0.0 2.2 %shard_map.46 = (bf16[512,512]{1,0:T(8,128)(2,1)S(1)}, bf16[512,128]{1,0:T(8,128)(2,1)S(1)}, s32[64,128]{1,0:T(8,128)S(1)}, f32[128,128]{1,0:T(8,128)S(1)}) custom-call(bf16[1,1,4,10,128,128]{5,4,3,2,1,0:T(8,128)(2,1)} %tiles_hbm.1, s32[1,1,4,10]{3,2,1,0:T(4,128)} %dest_hbm.1, s32[1,1,4]{2,1,0:T(1,128)} %count_hbm.1, s32[64,256]{1,0:T(8,128)} %bitcast.1), custom_call_target="tpu_custom_call" | custom-call | tf_op jit(solution)/shard_map/pallas_call | solution.py:255
  2.2 0.5 %collective-permute-start = (bf16[512,128]{1,0:T(8,128)(2,1)S(1)}, bf16[512,128]{1,0:T(8,128)(2,1)S(1)}, u32[]{:S(2)}, u32[]{:S(2)}) collective-permute-start(bf16[512,128]{1,0:T(8,128)(2,1)S(1)} %get-tuple-element.27), channel_id=1, source_target_pairs={{0,1},{1,0},{2,3},{3,2},{4,5},{5,4},{6,7},{7,6},{8,9},{9,8},{10,11... | collective-permute-start | bytes 393224 | tf_op jit(solution)/shard_map/ppermute | solution.py:216
  2.7 1.1 %shard_map.47 = (f32[512,128]{1,0:T(8,128)S(1)}, f32[256,128]{1,0:T(8,128)S(1)}, f32[256,128]{1,0:T(8,128)S(1)}) custom-call(bf16[512,512]{1,0:T(8,128)(2,1)S(1)} %get-tuple-element.29.dense.own, s32[64,128]{1,0:T(8,128)S(1)} %get-tuple-element.25.seed_rows), custom_call_target="tpu_custom_call" | custom-call | tf_op jit(solution)/shard_map/pallas_call | solution.py:279
  3.8 0.0 collective-permute-done.recv
  3.8 0.1 shard_map.48
  3.8 2.8 %collective-permute-start.4 = (bf16[256,128]{1,0:T(8,128)(2,1)S(1)}, bf16[256,128]{1,0:T(8,128)(2,1)S(1)}, u32[]{:S(2)}, u32[]{:S(2)}) collective-permute-start(bf16[256,128]{1,0:T(8,128)(2,1)S(1)} %get-tuple-element.31), channel_id=1, source_target_pairs={{0,2},{1,3},{2,0},{3,1},{4,6},{5,7},{6,4},{7,5},{8,10},{9,11},{10,... | collective-permute-start | bytes 196616 | tf_op jit(solution)/shard_map/ppermute | solution.py:216
  6.6 0.0 collective-permute-start.1
  6.6 1.6 %collective-permute-start.3 = (bf16[256,128]{1,0:T(8,128)(2,1)S(1)}, bf16[256,128]{1,0:T(8,128)(2,1)S(1)}, u32[]{:S(2)}, u32[]{:S(2)}) collective-permute-start(bf16[256,128]{1,0:T(8,128)(2,1)S(1)} %get-tuple-element.31), channel_id=1, source_target_pairs={{0,6},{2,4},{4,10},{6,8},{8,14},{10,12},{12,2},{14,0},{1,7},{3,5},... | collective-permute-start | bytes 196616 | tf_op jit(solution)/shard_map/ppermute | solution.py:228
  8.2 1.6 %collective-permute-start.2 = (bf16[256,128]{1,0:T(8,128)(2,1)S(1)}, bf16[256,128]{1,0:T(8,128)(2,1)S(1)}, u32[]{:S(2)}, u32[]{:S(2)}) collective-permute-start(bf16[256,128]{1,0:T(8,128)(2,1)S(1)} %get-tuple-element.30), channel_id=1, source_target_pairs={{0,4},{2,6},{4,8},{6,10},{8,12},{10,14},{12,0},{14,2},{1,5},{3,7},... | collective-permute-start | bytes 196616 | tf_op jit(solution)/shard_map/ppermute | solution.py:228
  9.7 0.0 collective-permute-done.4
  9.8 2.3 %collective-permute-start.6 = (bf16[256,128]{1,0:T(8,128)(2,1)S(1)}, bf16[256,128]{1,0:T(8,128)(2,1)S(1)}, u32[]{:S(2)}, u32[]{:S(2)}) collective-permute-start(bf16[256,128]{1,0:T(8,128)(2,1)S(1)} %add_convert_fusion.2.refs_1_), channel_id=1, source_target_pairs={{0,8},{2,10},{4,12},{6,14},{8,0},{10,2},{12,4},{14,6},{1,13},{3,15... | collective-permute-start | bytes 196616 | tf_op jit(solution)/shard_map/ppermute | solution.py:228
  12.1 1.7 %collective-permute-start.5 = (bf16[256,128]{1,0:T(8,128)(2,1)S(1)}, bf16[256,128]{1,0:T(8,128)(2,1)S(1)}, u32[]{:S(2)}, u32[]{:S(2)}) collective-permute-start(bf16[256,128]{1,0:T(8,128)(2,1)S(1)} %add_convert_fusion.2.refs_1_), channel_id=1, source_target_pairs={{0,12},{2,14},{4,0},{6,2},{8,4},{10,6},{12,8},{14,10},{1,9},{3,11}... | collective-permute-start | bytes 196616 | tf_op jit(solution)/shard_map/ppermute | solution.py:228
  13.8 0.8 %collective-permute-done.2 = bf16[256,128]{1,0:T(8,128)(2,1)S(1)} collective-permute-done((bf16[256,128]{1,0:T(8,128)(2,1)S(1)}, bf16[256,128]{1,0:T(8,128)(2,1)S(1)}, u32[]{:S(2)}, u32[]{:S(2)}) %collective-permute-start.2) | collective-permute-done | bytes 65568 | tf_op jit(solution)/shard_map/ppermute | solution.py:228
  14.6 0.0 collective-permute-done.3
  14.7 0.0 collective-permute-done.1.other
  14.7 0.3 shard_map.49.near
  15.0 2.1 %collective-permute-done.6.refs_1_ = bf16[256,128]{1,0:T(8,128)(2,1)S(1)} collective-permute-done((bf16[256,128]{1,0:T(8,128)(2,1)S(1)}, bf16[256,128]{1,0:T(8,128)(2,1)S(1)}, u32[]{:S(2)}, u32[]{:S(2)}) %collective-permute-start.6) | collective-permute-done | bytes 65568 | tf_op jit(solution)/shard_map/ppermute | solution.py:228
  17.1 0.4 %collective-permute-done.5.refs_0_ = bf16[256,128]{1,0:T(8,128)(2,1)S(1)} collective-permute-done((bf16[256,128]{1,0:T(8,128)(2,1)S(1)}, bf16[256,128]{1,0:T(8,128)(2,1)S(1)}, u32[]{:S(2)}, u32[]{:S(2)}) %collective-permute-start.5) | collective-permute-done | bytes 65568 | tf_op jit(solution)/shard_map/ppermute | solution.py:228
  17.5 0.3 shard_map.50
  17.8 1.6 %collective-permute-start.9 = (bf16[256,128]{1,0:T(8,128)(2,1)S(1)}, bf16[256,128]{1,0:T(8,128)(2,1)S(1)}, u32[]{:S(2)}, u32[]{:S(2)}) collective-permute-start(bf16[256,128]{1,0:T(8,128)(2,1)S(1)} %get-tuple-element.36), channel_id=1, source_target_pairs={{0,2},{1,3},{2,0},{3,1},{4,6},{5,7},{6,4},{7,5},{8,10},{9,11},{10,... | collective-permute-start | bytes 196616 | tf_op jit(solution)/shard_map/ppermute | solution.py:216
  19.4 1.2 %collective-permute-start.8 = (bf16[256,128]{1,0:T(8,128)(2,1)S(1)}, bf16[256,128]{1,0:T(8,128)(2,1)S(1)}, u32[]{:S(2)}, u32[]{:S(2)}) collective-permute-start(bf16[256,128]{1,0:T(8,128)(2,1)S(1)} %get-tuple-element.36), channel_id=1, source_target_pairs={{0,6},{2,4},{4,10},{6,8},{8,14},{10,12},{12,2},{14,0},{1,7},{3,5},... | collective-permute-start | bytes 196616 | tf_op jit(solution)/shard_map/ppermute | solution.py:228
  20.6 0.4 %collective-permute-start.7 = (bf16[256,128]{1,0:T(8,128)(2,1)S(1)}, bf16[256,128]{1,0:T(8,128)(2,1)S(1)}, u32[]{:S(2)}, u32[]{:S(2)}) collective-permute-start(bf16[256,128]{1,0:T(8,128)(2,1)S(1)} %get-tuple-element.35), channel_id=1, source_target_pairs={{0,4},{2,6},{4,8},{6,10},{8,12},{10,14},{12,0},{14,2},{1,5},{3,7},... | collective-permute-start | bytes 196616 | tf_op jit(solution)/shard_map/ppermute | solution.py:228
  21.0 1.1 %collective-permute-done.9 = bf16[256,128]{1,0:T(8,128)(2,1)S(1)} collective-permute-done((bf16[256,128]{1,0:T(8,128)(2,1)S(1)}, bf16[256,128]{1,0:T(8,128)(2,1)S(1)}, u32[]{:S(2)}, u32[]{:S(2)}) %collective-permute-start.9) | collective-permute-done | bytes 65568 | tf_op jit(solution)/shard_map/ppermute | solution.py:216
  22.1 1.7 %collective-permute-start.11 = (bf16[256,128]{1,0:T(8,128)(2,1)S(1)}, bf16[256,128]{1,0:T(8,128)(2,1)S(1)}, u32[]{:S(2)}, u32[]{:S(2)}) collective-permute-start(bf16[256,128]{1,0:T(8,128)(2,1)S(1)} %add_convert_fusion.refs_1_), channel_id=1, source_target_pairs={{0,8},{2,10},{4,12},{6,14},{8,0},{10,2},{12,4},{14,6},{1,13},{3,15... | collective-permute-start | bytes 196616 | tf_op jit(solution)/shard_map/ppermute | solution.py:228
  23.8 2.3 %collective-permute-start.10 = (bf16[256,128]{1,0:T(8,128)(2,1)S(1)}, bf16[256,128]{1,0:T(8,128)(2,1)S(1)}, u32[]{:S(2)}, u32[]{:S(2)}) collective-permute-start(bf16[256,128]{1,0:T(8,128)(2,1)S(1)} %add_convert_fusion.refs_1_), channel_id=1, source_target_pairs={{0,12},{2,14},{4,0},{6,2},{8,4},{10,6},{12,8},{14,10},{1,9},{3,11}... | collective-permute-start | bytes 196616 | tf_op jit(solution)/shard_map/ppermute | solution.py:228
  26.1 1.2 %collective-permute-done.7 = bf16[256,128]{1,0:T(8,128)(2,1)S(1)} collective-permute-done((bf16[256,128]{1,0:T(8,128)(2,1)S(1)}, bf16[256,128]{1,0:T(8,128)(2,1)S(1)}, u32[]{:S(2)}, u32[]{:S(2)}) %collective-permute-start.7) | collective-permute-done | bytes 65568 | tf_op jit(solution)/shard_map/ppermute | solution.py:228
  27.3 0.0 collective-permute-done.8
  27.3 0.3 shard_map.51.near
  27.7 1.4 %collective-permute-done.11.refs_1_ = bf16[256,128]{1,0:T(8,128)(2,1)S(1)} collective-permute-done((bf16[256,128]{1,0:T(8,128)(2,1)S(1)}, bf16[256,128]{1,0:T(8,128)(2,1)S(1)}, u32[]{:S(2)}, u32[]{:S(2)}) %collective-permute-start.11) | collective-permute-done | bytes 65568 | tf_op jit(solution)/shard_map/ppermute | solution.py:228
  29.1 0.0 collective-permute-done.10.refs_0_
  29.1 0.2 shard_map.53
  29.3 0.1 collective-permute-start.12
  29.4 1.5 %collective-permute-start.13 = (bf16[128,128]{1,0:T(8,128)(2,1)S(1)}, bf16[128,128]{1,0:T(8,128)(2,1)S(1)}, u32[]{:S(2)}, u32[]{:S(2)}) collective-permute-start(bf16[128,128]{1,0:T(8,128)(2,1)S(1)} %get-tuple-element.41), channel_id=1, source_target_pairs={{0,2},{1,3},{2,0},{3,1},{4,6},{5,7},{6,4},{7,5},{8,10},{9,11},{10,... | collective-permute-start | bytes 98312 | tf_op jit(solution)/shard_map/ppermute | solution.py:216
  30.9 0.2 shard_map.52
  31.1 0.4 %collective-permute-start.14 = (bf16[128,128]{1,0:T(8,128)(2,1)S(1)}, bf16[128,128]{1,0:T(8,128)(2,1)S(1)}, u32[]{:S(2)}, u32[]{:S(2)}) collective-permute-start(bf16[128,128]{1,0:T(8,128)(2,1)S(1)} %get-tuple-element.42), channel_id=1, source_target_pairs={{0,1},{1,0},{2,3},{3,2},{4,5},{5,4},{6,7},{7,6},{8,9},{9,8},{10,11... | collective-permute-start | bytes 98312 | tf_op jit(solution)/shard_map/ppermute | solution.py:216
  31.6 1.5 %collective-permute-done.12.refs_0_ = bf16[128,128]{1,0:T(8,128)(2,1)S(1)} collective-permute-done((bf16[128,128]{1,0:T(8,128)(2,1)S(1)}, bf16[128,128]{1,0:T(8,128)(2,1)S(1)}, u32[]{:S(2)}, u32[]{:S(2)}) %collective-permute-start.12) | collective-permute-done | bytes 32800 | tf_op jit(solution)/shard_map/ppermute | solution.py:216
  33.1 0.3 collective-permute-done.13.refs_1_
  33.4 0.0 collective-permute-done.14.refs_2_
  33.4 0.7 %shard_map.54 = f32[128,256]{1,0:T(8,128)} custom-call(f32[128,128]{1,0:T(8,128)S(1)} %get-tuple-element.38.own, f32[128,128]{1,0:T(8,128)S(1)} %get-tuple-element.39.restart, bf16[128,128]{1,0:T(8,128)(2,1)S(1)} %collective-permute-done.12.refs_0_, bf16[128,128]{1,0:T(8,128)(2,1)S(1)} %collective-permute-done.13.refs_1_, ...), custom_call_target="tpu_custom_call" | custom-call | tf_op jit(solution)/shard_map/pallas_call | solution.py:327
  (4 shorter events, 0.1 us)
Async XLA Ops:
  2.2 1.6 %collective-permute-start = (bf16[512,128]{1,0:T(8,128)(2,1)S(1)}, bf16[512,128]{1,0:T(8,128)(2,1)S(1)}, u32[]{:S(2)}, u32[]{:S(2)}) collective-permute-start(bf16[512,128]{1,0:T(8,128)(2,1)S(1)} %get-tuple-element.27), channel_id=1, source_target_pairs={{0,1},{1,0},{2,3},{3,2},{4,5},{5,4},{6,7},{7,6},{8,9},{9,8},{10,11... | collective-permute-start | bytes 393224 | tf_op jit(solution)/shard_map/ppermute | solution.py:216
  3.8 5.9 %collective-permute-start.4 = (bf16[256,128]{1,0:T(8,128)(2,1)S(1)}, bf16[256,128]{1,0:T(8,128)(2,1)S(1)}, u32[]{:S(2)}, u32[]{:S(2)}) collective-permute-start(bf16[256,128]{1,0:T(8,128)(2,1)S(1)} %get-tuple-element.31), channel_id=1, source_target_pairs={{0,2},{1,3},{2,0},{3,1},{4,6},{5,7},{6,4},{7,5},{8,10},{9,11},{10,... | collective-permute-start | bytes 196616 | tf_op jit(solution)/shard_map/ppermute | solution.py:216
  6.6 8.0 %collective-permute-start.1 = (bf16[512,512]{1,0:T(8,128)(2,1)S(1)}, bf16[512,512]{1,0:T(8,128)(2,1)S(1)}, u32[]{:S(2)}, u32[]{:S(2)}) collective-permute-start(bf16[512,512]{1,0:T(8,128)(2,1)S(1)} %get-tuple-element.29.dense.own), channel_id=1, source_target_pairs={{0,1},{1,0},{2,3},{3,2},{4,5},{5,4},{6,7},{7,6},{8,9},{9,8},{10,11... | collective-permute-start | bytes 1572872 | tf_op jit(solution)/shard_map/ppermute | solution.py:216
  6.6 8.0 %collective-permute-start.3 = (bf16[256,128]{1,0:T(8,128)(2,1)S(1)}, bf16[256,128]{1,0:T(8,128)(2,1)S(1)}, u32[]{:S(2)}, u32[]{:S(2)}) collective-permute-start(bf16[256,128]{1,0:T(8,128)(2,1)S(1)} %get-tuple-element.31), channel_id=1, source_target_pairs={{0,6},{2,4},{4,10},{6,8},{8,14},{10,12},{12,2},{14,0},{1,7},{3,5},... | collective-permute-start | bytes 196616 | tf_op jit(solution)/shard_map/ppermute | solution.py:228
  8.2 6.5 %collective-permute-start.2 = (bf16[256,128]{1,0:T(8,128)(2,1)S(1)}, bf16[256,128]{1,0:T(8,128)(2,1)S(1)}, u32[]{:S(2)}, u32[]{:S(2)}) collective-permute-start(bf16[256,128]{1,0:T(8,128)(2,1)S(1)} %get-tuple-element.30), channel_id=1, source_target_pairs={{0,4},{2,6},{4,8},{6,10},{8,12},{10,14},{12,0},{14,2},{1,5},{3,7},... | collective-permute-start | bytes 196616 | tf_op jit(solution)/shard_map/ppermute | solution.py:228
  9.8 7.3 %collective-permute-start.6 = (bf16[256,128]{1,0:T(8,128)(2,1)S(1)}, bf16[256,128]{1,0:T(8,128)(2,1)S(1)}, u32[]{:S(2)}, u32[]{:S(2)}) collective-permute-start(bf16[256,128]{1,0:T(8,128)(2,1)S(1)} %add_convert_fusion.2.refs_1_), channel_id=1, source_target_pairs={{0,8},{2,10},{4,12},{6,14},{8,0},{10,2},{12,4},{14,6},{1,13},{3,15... | collective-permute-start | bytes 196616 | tf_op jit(solution)/shard_map/ppermute | solution.py:228
  12.1 5.4 %collective-permute-start.5 = (bf16[256,128]{1,0:T(8,128)(2,1)S(1)}, bf16[256,128]{1,0:T(8,128)(2,1)S(1)}, u32[]{:S(2)}, u32[]{:S(2)}) collective-permute-start(bf16[256,128]{1,0:T(8,128)(2,1)S(1)} %add_convert_fusion.2.refs_1_), channel_id=1, source_target_pairs={{0,12},{2,14},{4,0},{6,2},{8,4},{10,6},{12,8},{14,10},{1,9},{3,11}... | collective-permute-start | bytes 196616 | tf_op jit(solution)/shard_map/ppermute | solution.py:228
  17.8 4.3 %collective-permute-start.9 = (bf16[256,128]{1,0:T(8,128)(2,1)S(1)}, bf16[256,128]{1,0:T(8,128)(2,1)S(1)}, u32[]{:S(2)}, u32[]{:S(2)}) collective-permute-start(bf16[256,128]{1,0:T(8,128)(2,1)S(1)} %get-tuple-element.36), channel_id=1, source_target_pairs={{0,2},{1,3},{2,0},{3,1},{4,6},{5,7},{6,4},{7,5},{8,10},{9,11},{10,... | collective-permute-start | bytes 196616 | tf_op jit(solution)/shard_map/ppermute | solution.py:216
  19.4 7.9 %collective-permute-start.8 = (bf16[256,128]{1,0:T(8,128)(2,1)S(1)}, bf16[256,128]{1,0:T(8,128)(2,1)S(1)}, u32[]{:S(2)}, u32[]{:S(2)}) collective-permute-start(bf16[256,128]{1,0:T(8,128)(2,1)S(1)} %get-tuple-element.36), channel_id=1, source_target_pairs={{0,6},{2,4},{4,10},{6,8},{8,14},{10,12},{12,2},{14,0},{1,7},{3,5},... | collective-permute-start | bytes 196616 | tf_op jit(solution)/shard_map/ppermute | solution.py:228
  20.6 6.7 %collective-permute-start.7 = (bf16[256,128]{1,0:T(8,128)(2,1)S(1)}, bf16[256,128]{1,0:T(8,128)(2,1)S(1)}, u32[]{:S(2)}, u32[]{:S(2)}) collective-permute-start(bf16[256,128]{1,0:T(8,128)(2,1)S(1)} %get-tuple-element.35), channel_id=1, source_target_pairs={{0,4},{2,6},{4,8},{6,10},{8,12},{10,14},{12,0},{14,2},{1,5},{3,7},... | collective-permute-start | bytes 196616 | tf_op jit(solution)/shard_map/ppermute | solution.py:228
  22.1 6.9 %collective-permute-start.11 = (bf16[256,128]{1,0:T(8,128)(2,1)S(1)}, bf16[256,128]{1,0:T(8,128)(2,1)S(1)}, u32[]{:S(2)}, u32[]{:S(2)}) collective-permute-start(bf16[256,128]{1,0:T(8,128)(2,1)S(1)} %add_convert_fusion.refs_1_), channel_id=1, source_target_pairs={{0,8},{2,10},{4,12},{6,14},{8,0},{10,2},{12,4},{14,6},{1,13},{3,15... | collective-permute-start | bytes 196616 | tf_op jit(solution)/shard_map/ppermute | solution.py:228
  23.8 5.3 %collective-permute-start.10 = (bf16[256,128]{1,0:T(8,128)(2,1)S(1)}, bf16[256,128]{1,0:T(8,128)(2,1)S(1)}, u32[]{:S(2)}, u32[]{:S(2)}) collective-permute-start(bf16[256,128]{1,0:T(8,128)(2,1)S(1)} %add_convert_fusion.refs_1_), channel_id=1, source_target_pairs={{0,12},{2,14},{4,0},{6,2},{8,4},{10,6},{12,8},{14,10},{1,9},{3,11}... | collective-permute-start | bytes 196616 | tf_op jit(solution)/shard_map/ppermute | solution.py:228
  29.3 3.7 %collective-permute-start.12 = (bf16[128,128]{1,0:T(8,128)(2,1)S(1)}, bf16[128,128]{1,0:T(8,128)(2,1)S(1)}, u32[]{:S(2)}, u32[]{:S(2)}) collective-permute-start(bf16[128,128]{1,0:T(8,128)(2,1)S(1)} %get-tuple-element.40), channel_id=1, source_target_pairs={{0,3},{1,2},{2,1},{3,0},{4,7},{5,6},{6,5},{7,4},{8,11},{9,10},{10,... | collective-permute-start | bytes 98312 | tf_op jit(solution)/shard_map/ppermute | solution.py:216
  29.4 4.0 %collective-permute-start.13 = (bf16[128,128]{1,0:T(8,128)(2,1)S(1)}, bf16[128,128]{1,0:T(8,128)(2,1)S(1)}, u32[]{:S(2)}, u32[]{:S(2)}) collective-permute-start(bf16[128,128]{1,0:T(8,128)(2,1)S(1)} %get-tuple-element.41), channel_id=1, source_target_pairs={{0,2},{1,3},{2,0},{3,1},{4,6},{5,7},{6,4},{7,5},{8,10},{9,11},{10,... | collective-permute-start | bytes 98312 | tf_op jit(solution)/shard_map/ppermute | solution.py:216
  31.1 2.3 %collective-permute-start.14 = (bf16[128,128]{1,0:T(8,128)(2,1)S(1)}, bf16[128,128]{1,0:T(8,128)(2,1)S(1)}, u32[]{:S(2)}, u32[]{:S(2)}) collective-permute-start(bf16[128,128]{1,0:T(8,128)(2,1)S(1)} %get-tuple-element.42), channel_id=1, source_target_pairs={{0,1},{1,0},{2,3},{3,2},{4,5},{5,4},{6,7},{7,6},{8,9},{9,8},{10,11... | collective-permute-start | bytes 98312 | tf_op jit(solution)/shard_map/ppermute | solution.py:216

commit v7 on v6

--- a/solution.py
+++ b/solution.py
@@ -99,7 +99,7 @@
     for fetch in fetch_tables[1:]:
         fetch.wait()
     for s in range(steps):
-        upto = number * (steps + 1 + s) // (2 * steps)
+        upto = number * (s + 1) // steps
         counts = add_seeds(counts, ids, split, done, upto)
         done = upto
         fetch_tiles[s].wait()

time: 34.2 us -> 34.2 us (level)
  no operation moved by 1% of the time
where the time goes in v7:
time: 34.2 us; the launch traced here: 34.1 us
  starting transfers between devices  19.6 us (57%)
  waiting for transfers between devices  8.95 us (26%)
  Pallas kernels  5.37 us (16%)
    ppermute x8, starting transfers between devices, from_behind(): return lax.ppermute(value, ('blk', 'col'), route)  12.7 us
    ppermute x7, starting transfers between devices, from_col(): return lax.ppermute(value, 'col', route)  6.89 us
    ppermute x8, waiting for transfers between devices, from_behind(): return lax.ppermute(value, ('blk', 'col'), route)  5.97 us
    ppermute x7, waiting for transfers between devices, from_col(): return lax.ppermute(value, 'col', route)  2.98 us
    pallas_call x1, Pallas kernels, body(): call(functools.partial(first_kernel, steps, columns, scale), [HBM] * 4, [...  2.14 us
    pallas_call x1, Pallas kernels, body(): call(functools.partial(keep_kernel, steps, columns, scale), [VMEM] * 2, [...  1.08 us
  transfers between devices with their start and end apart: 15, of which 8 were waited for; matrix products, arithmetic and copies ran while one was open for 0% of the time, Pallas kernels for 6%

profile of v7, /device:TPU:0, one launch (start us, length us, event | category | flops | bytes accessed | tf_op | source)
XLA Modules:
  0.0 34.1 jit_solution(12316526415641654973)
XLA Ops:
  0.0 2.1 %shard_map.46 = (bf16[512,512]{1,0:T(8,128)(2,1)S(1)}, bf16[512,128]{1,0:T(8,128)(2,1)S(1)}, s32[64,128]{1,0:T(8,128)S(1)}, f32[128,128]{1,0:T(8,128)S(1)}) custom-call(bf16[1,1,4,10,128,128]{5,4,3,2,1,0:T(8,128)(2,1)} %tiles_hbm.1, s32[1,1,4,10]{3,2,1,0:T(4,128)} %dest_hbm.1, s32[1,1,4]{2,1,0:T(1,128)} %count_hbm.1, s32[64,256]{1,0:T(8,128)} %bitcast.1), custom_call_target="tpu_custom_call" | custom-call | tf_op jit(solution)/shard_map/pallas_call | solution.py:255
  2.1 0.5 %collective-permute-start = (bf16[512,128]{1,0:T(8,128)(2,1)S(1)}, bf16[512,128]{1,0:T(8,128)(2,1)S(1)}, u32[]{:S(2)}, u32[]{:S(2)}) collective-permute-start(bf16[512,128]{1,0:T(8,128)(2,1)S(1)} %get-tuple-element.27), channel_id=1, source_target_pairs={{0,1},{1,0},{2,3},{3,2},{4,5},{5,4},{6,7},{7,6},{8,9},{9,8},{10,11... | collective-permute-start | bytes 393224 | tf_op jit(solution)/shard_map/ppermute | solution.py:216
  2.7 1.1 %shard_map.47 = (f32[512,128]{1,0:T(8,128)S(1)}, f32[256,128]{1,0:T(8,128)S(1)}, f32[256,128]{1,0:T(8,128)S(1)}) custom-call(bf16[512,512]{1,0:T(8,128)(2,1)S(1)} %get-tuple-element.29.dense.own, s32[64,128]{1,0:T(8,128)S(1)} %get-tuple-element.25.seed_rows), custom_call_target="tpu_custom_call" | custom-call | tf_op jit(solution)/shard_map/pallas_call | solution.py:279
  3.8 0.0 collective-permute-done.recv
  3.8 0.1 shard_map.48
  3.8 2.8 %collective-permute-start.4 = (bf16[256,128]{1,0:T(8,128)(2,1)S(1)}, bf16[256,128]{1,0:T(8,128)(2,1)S(1)}, u32[]{:S(2)}, u32[]{:S(2)}) collective-permute-start(bf16[256,128]{1,0:T(8,128)(2,1)S(1)} %get-tuple-element.31), channel_id=1, source_target_pairs={{0,2},{1,3},{2,0},{3,1},{4,6},{5,7},{6,4},{7,5},{8,10},{9,11},{10,... | collective-permute-start | bytes 196616 | tf_op jit(solution)/shard_map/ppermute | solution.py:216
  6.6 0.0 collective-permute-start.1
  6.6 1.5 %collective-permute-start.3 = (bf16[256,128]{1,0:T(8,128)(2,1)S(1)}, bf16[256,128]{1,0:T(8,128)(2,1)S(1)}, u32[]{:S(2)}, u32[]{:S(2)}) collective-permute-start(bf16[256,128]{1,0:T(8,128)(2,1)S(1)} %get-tuple-element.31), channel_id=1, source_target_pairs={{0,6},{2,4},{4,10},{6,8},{8,14},{10,12},{12,2},{14,0},{1,7},{3,5},... | collective-permute-start | bytes 196616 | tf_op jit(solution)/shard_map/ppermute | solution.py:228
  8.2 1.6 %collective-permute-start.2 = (bf16[256,128]{1,0:T(8,128)(2,1)S(1)}, bf16[256,128]{1,0:T(8,128)(2,1)S(1)}, u32[]{:S(2)}, u32[]{:S(2)}) collective-permute-start(bf16[256,128]{1,0:T(8,128)(2,1)S(1)} %get-tuple-element.30), channel_id=1, source_target_pairs={{0,4},{2,6},{4,8},{6,10},{8,12},{10,14},{12,0},{14,2},{1,5},{3,7},... | collective-permute-start | bytes 196616 | tf_op jit(solution)/shard_map/ppermute | solution.py:228
  9.7 0.0 collective-permute-done.4
  9.8 2.3 %collective-permute-start.6 = (bf16[256,128]{1,0:T(8,128)(2,1)S(1)}, bf16[256,128]{1,0:T(8,128)(2,1)S(1)}, u32[]{:S(2)}, u32[]{:S(2)}) collective-permute-start(bf16[256,128]{1,0:T(8,128)(2,1)S(1)} %add_convert_fusion.2.refs_1_), channel_id=1, source_target_pairs={{0,8},{2,10},{4,12},{6,14},{8,0},{10,2},{12,4},{14,6},{1,13},{3,15... | collective-permute-start | bytes 196616 | tf_op jit(solution)/shard_map/ppermute | solution.py:228
  12.1 1.7 %collective-permute-start.5 = (bf16[256,128]{1,0:T(8,128)(2,1)S(1)}, bf16[256,128]{1,0:T(8,128)(2,1)S(1)}, u32[]{:S(2)}, u32[]{:S(2)}) collective-permute-start(bf16[256,128]{1,0:T(8,128)(2,1)S(1)} %add_convert_fusion.2.refs_1_), channel_id=1, source_target_pairs={{0,12},{2,14},{4,0},{6,2},{8,4},{10,6},{12,8},{14,10},{1,9},{3,11}... | collective-permute-start | bytes 196616 | tf_op jit(solution)/shard_map/ppermute | solution.py:228
  13.8 0.8 %collective-permute-done.2 = bf16[256,128]{1,0:T(8,128)(2,1)S(1)} collective-permute-done((bf16[256,128]{1,0:T(8,128)(2,1)S(1)}, bf16[256,128]{1,0:T(8,128)(2,1)S(1)}, u32[]{:S(2)}, u32[]{:S(2)}) %collective-permute-start.2) | collective-permute-done | bytes 65568 | tf_op jit(solution)/shard_map/ppermute | solution.py:228
  14.6 0.0 collective-permute-done.3
  14.7 0.0 collective-permute-done.1.other
  14.7 0.3 shard_map.49.near
  15.0 2.1 %collective-permute-done.6.refs_1_ = bf16[256,128]{1,0:T(8,128)(2,1)S(1)} collective-permute-done((bf16[256,128]{1,0:T(8,128)(2,1)S(1)}, bf16[256,128]{1,0:T(8,128)(2,1)S(1)}, u32[]{:S(2)}, u32[]{:S(2)}) %collective-permute-start.6) | collective-permute-done | bytes 65568 | tf_op jit(solution)/shard_map/ppermute | solution.py:228
  17.1 0.4 %collective-permute-done.5.refs_0_ = bf16[256,128]{1,0:T(8,128)(2,1)S(1)} collective-permute-done((bf16[256,128]{1,0:T(8,128)(2,1)S(1)}, bf16[256,128]{1,0:T(8,128)(2,1)S(1)}, u32[]{:S(2)}, u32[]{:S(2)}) %collective-permute-start.5) | collective-permute-done | bytes 65568 | tf_op jit(solution)/shard_map/ppermute | solution.py:228
  17.5 0.3 shard_map.50
  17.8 1.6 %collective-permute-start.9 = (bf16[256,128]{1,0:T(8,128)(2,1)S(1)}, bf16[256,128]{1,0:T(8,128)(2,1)S(1)}, u32[]{:S(2)}, u32[]{:S(2)}) collective-permute-start(bf16[256,128]{1,0:T(8,128)(2,1)S(1)} %get-tuple-element.36), channel_id=1, source_target_pairs={{0,2},{1,3},{2,0},{3,1},{4,6},{5,7},{6,4},{7,5},{8,10},{9,11},{10,... | collective-permute-start | bytes 196616 | tf_op jit(solution)/shard_map/ppermute | solution.py:216
  19.4 1.2 %collective-permute-start.8 = (bf16[256,128]{1,0:T(8,128)(2,1)S(1)}, bf16[256,128]{1,0:T(8,128)(2,1)S(1)}, u32[]{:S(2)}, u32[]{:S(2)}) collective-permute-start(bf16[256,128]{1,0:T(8,128)(2,1)S(1)} %get-tuple-element.36), channel_id=1, source_target_pairs={{0,6},{2,4},{4,10},{6,8},{8,14},{10,12},{12,2},{14,0},{1,7},{3,5},... | collective-permute-start | bytes 196616 | tf_op jit(solution)/shard_map/ppermute | solution.py:228
  20.6 0.4 %collective-permute-start.7 = (bf16[256,128]{1,0:T(8,128)(2,1)S(1)}, bf16[256,128]{1,0:T(8,128)(2,1)S(1)}, u32[]{:S(2)}, u32[]{:S(2)}) collective-permute-start(bf16[256,128]{1,0:T(8,128)(2,1)S(1)} %get-tuple-element.35), channel_id=1, source_target_pairs={{0,4},{2,6},{4,8},{6,10},{8,12},{10,14},{12,0},{14,2},{1,5},{3,7},... | collective-permute-start | bytes 196616 | tf_op jit(solution)/shard_map/ppermute | solution.py:228
  21.0 1.1 %collective-permute-done.9 = bf16[256,128]{1,0:T(8,128)(2,1)S(1)} collective-permute-done((bf16[256,128]{1,0:T(8,128)(2,1)S(1)}, bf16[256,128]{1,0:T(8,128)(2,1)S(1)}, u32[]{:S(2)}, u32[]{:S(2)}) %collective-permute-start.9) | collective-permute-done | bytes 65568 | tf_op jit(solution)/shard_map/ppermute | solution.py:216
  22.1 1.7 %collective-permute-start.11 = (bf16[256,128]{1,0:T(8,128)(2,1)S(1)}, bf16[256,128]{1,0:T(8,128)(2,1)S(1)}, u32[]{:S(2)}, u32[]{:S(2)}) collective-permute-start(bf16[256,128]{1,0:T(8,128)(2,1)S(1)} %add_convert_fusion.refs_1_), channel_id=1, source_target_pairs={{0,8},{2,10},{4,12},{6,14},{8,0},{10,2},{12,4},{14,6},{1,13},{3,15... | collective-permute-start | bytes 196616 | tf_op jit(solution)/shard_map/ppermute | solution.py:228
  23.8 2.3 %collective-permute-start.10 = (bf16[256,128]{1,0:T(8,128)(2,1)S(1)}, bf16[256,128]{1,0:T(8,128)(2,1)S(1)}, u32[]{:S(2)}, u32[]{:S(2)}) collective-permute-start(bf16[256,128]{1,0:T(8,128)(2,1)S(1)} %add_convert_fusion.refs_1_), channel_id=1, source_target_pairs={{0,12},{2,14},{4,0},{6,2},{8,4},{10,6},{12,8},{14,10},{1,9},{3,11}... | collective-permute-start | bytes 196616 | tf_op jit(solution)/shard_map/ppermute | solution.py:228
  26.1 1.2 %collective-permute-done.7 = bf16[256,128]{1,0:T(8,128)(2,1)S(1)} collective-permute-done((bf16[256,128]{1,0:T(8,128)(2,1)S(1)}, bf16[256,128]{1,0:T(8,128)(2,1)S(1)}, u32[]{:S(2)}, u32[]{:S(2)}) %collective-permute-start.7) | collective-permute-done | bytes 65568 | tf_op jit(solution)/shard_map/ppermute | solution.py:228
  27.3 0.0 collective-permute-done.8
  27.3 0.3 shard_map.51.near
  27.7 1.4 %collective-permute-done.11.refs_1_ = bf16[256,128]{1,0:T(8,128)(2,1)S(1)} collective-permute-done((bf16[256,128]{1,0:T(8,128)(2,1)S(1)}, bf16[256,128]{1,0:T(8,128)(2,1)S(1)}, u32[]{:S(2)}, u32[]{:S(2)}) %collective-permute-start.11) | collective-permute-done | bytes 65568 | tf_op jit(solution)/shard_map/ppermute | solution.py:228
  29.1 0.0 collective-permute-done.10.refs_0_
  29.1 0.2 shard_map.53
  29.3 0.1 collective-permute-start.12
  29.4 1.5 %collective-permute-start.13 = (bf16[128,128]{1,0:T(8,128)(2,1)S(1)}, bf16[128,128]{1,0:T(8,128)(2,1)S(1)}, u32[]{:S(2)}, u32[]{:S(2)}) collective-permute-start(bf16[128,128]{1,0:T(8,128)(2,1)S(1)} %get-tuple-element.41), channel_id=1, source_target_pairs={{0,2},{1,3},{2,0},{3,1},{4,6},{5,7},{6,4},{7,5},{8,10},{9,11},{10,... | collective-permute-start | bytes 98312 | tf_op jit(solution)/shard_map/ppermute | solution.py:216
  30.9 0.2 shard_map.52
  31.1 0.4 %collective-permute-start.14 = (bf16[128,128]{1,0:T(8,128)(2,1)S(1)}, bf16[128,128]{1,0:T(8,128)(2,1)S(1)}, u32[]{:S(2)}, u32[]{:S(2)}) collective-permute-start(bf16[128,128]{1,0:T(8,128)(2,1)S(1)} %get-tuple-element.42), channel_id=1, source_target_pairs={{0,1},{1,0},{2,3},{3,2},{4,5},{5,4},{6,7},{7,6},{8,9},{9,8},{10,11... | collective-permute-start | bytes 98312 | tf_op jit(solution)/shard_map/ppermute | solution.py:216
  31.5 1.5 %collective-permute-done.12.refs_0_ = bf16[128,128]{1,0:T(8,128)(2,1)S(1)} collective-permute-done((bf16[128,128]{1,0:T(8,128)(2,1)S(1)}, bf16[128,128]{1,0:T(8,128)(2,1)S(1)}, u32[]{:S(2)}, u32[]{:S(2)}) %collective-permute-start.12) | collective-permute-done | bytes 32800 | tf_op jit(solution)/shard_map/ppermute | solution.py:216
  33.1 0.3 collective-permute-done.13.refs_1_
  33.4 0.0 collective-permute-done.14.refs_2_
  33.4 0.7 %shard_map.54 = f32[128,256]{1,0:T(8,128)} custom-call(f32[128,128]{1,0:T(8,128)S(1)} %get-tuple-element.38.own, f32[128,128]{1,0:T(8,128)S(1)} %get-tuple-element.39.restart, bf16[128,128]{1,0:T(8,128)(2,1)S(1)} %collective-permute-done.12.refs_0_, bf16[128,128]{1,0:T(8,128)(2,1)S(1)} %collective-permute-done.13.refs_1_, ...), custom_call_target="tpu_custom_call" | custom-call | tf_op jit(solution)/shard_map/pallas_call | solution.py:327
  (4 shorter events, 0.1 us)
Async XLA Ops:
  2.1 1.6 %collective-permute-start = (bf16[512,128]{1,0:T(8,128)(2,1)S(1)}, bf16[512,128]{1,0:T(8,128)(2,1)S(1)}, u32[]{:S(2)}, u32[]{:S(2)}) collective-permute-start(bf16[512,128]{1,0:T(8,128)(2,1)S(1)} %get-tuple-element.27), channel_id=1, source_target_pairs={{0,1},{1,0},{2,3},{3,2},{4,5},{5,4},{6,7},{7,6},{8,9},{9,8},{10,11... | collective-permute-start | bytes 393224 | tf_op jit(solution)/shard_map/ppermute | solution.py:216
  3.8 5.9 %collective-permute-start.4 = (bf16[256,128]{1,0:T(8,128)(2,1)S(1)}, bf16[256,128]{1,0:T(8,128)(2,1)S(1)}, u32[]{:S(2)}, u32[]{:S(2)}) collective-permute-start(bf16[256,128]{1,0:T(8,128)(2,1)S(1)} %get-tuple-element.31), channel_id=1, source_target_pairs={{0,2},{1,3},{2,0},{3,1},{4,6},{5,7},{6,4},{7,5},{8,10},{9,11},{10,... | collective-permute-start | bytes 196616 | tf_op jit(solution)/shard_map/ppermute | solution.py:216
  6.6 8.0 %collective-permute-start.1 = (bf16[512,512]{1,0:T(8,128)(2,1)S(1)}, bf16[512,512]{1,0:T(8,128)(2,1)S(1)}, u32[]{:S(2)}, u32[]{:S(2)}) collective-permute-start(bf16[512,512]{1,0:T(8,128)(2,1)S(1)} %get-tuple-element.29.dense.own), channel_id=1, source_target_pairs={{0,1},{1,0},{2,3},{3,2},{4,5},{5,4},{6,7},{7,6},{8,9},{9,8},{10,11... | collective-permute-start | bytes 1572872 | tf_op jit(solution)/shard_map/ppermute | solution.py:216
  6.6 8.0 %collective-permute-start.3 = (bf16[256,128]{1,0:T(8,128)(2,1)S(1)}, bf16[256,128]{1,0:T(8,128)(2,1)S(1)}, u32[]{:S(2)}, u32[]{:S(2)}) collective-permute-start(bf16[256,128]{1,0:T(8,128)(2,1)S(1)} %get-tuple-element.31), channel_id=1, source_target_pairs={{0,6},{2,4},{4,10},{6,8},{8,14},{10,12},{12,2},{14,0},{1,7},{3,5},... | collective-permute-start | bytes 196616 | tf_op jit(solution)/shard_map/ppermute | solution.py:228
  8.2 6.5 %collective-permute-start.2 = (bf16[256,128]{1,0:T(8,128)(2,1)S(1)}, bf16[256,128]{1,0:T(8,128)(2,1)S(1)}, u32[]{:S(2)}, u32[]{:S(2)}) collective-permute-start(bf16[256,128]{1,0:T(8,128)(2,1)S(1)} %get-tuple-element.30), channel_id=1, source_target_pairs={{0,4},{2,6},{4,8},{6,10},{8,12},{10,14},{12,0},{14,2},{1,5},{3,7},... | collective-permute-start | bytes 196616 | tf_op jit(solution)/shard_map/ppermute | solution.py:228
  9.8 7.3 %collective-permute-start.6 = (bf16[256,128]{1,0:T(8,128)(2,1)S(1)}, bf16[256,128]{1,0:T(8,128)(2,1)S(1)}, u32[]{:S(2)}, u32[]{:S(2)}) collective-permute-start(bf16[256,128]{1,0:T(8,128)(2,1)S(1)} %add_convert_fusion.2.refs_1_), channel_id=1, source_target_pairs={{0,8},{2,10},{4,12},{6,14},{8,0},{10,2},{12,4},{14,6},{1,13},{3,15... | collective-permute-start | bytes 196616 | tf_op jit(solution)/shard_map/ppermute | solution.py:228
  12.1 5.4 %collective-permute-start.5 = (bf16[256,128]{1,0:T(8,128)(2,1)S(1)}, bf16[256,128]{1,0:T(8,128)(2,1)S(1)}, u32[]{:S(2)}, u32[]{:S(2)}) collective-permute-start(bf16[256,128]{1,0:T(8,128)(2,1)S(1)} %add_convert_fusion.2.refs_1_), channel_id=1, source_target_pairs={{0,12},{2,14},{4,0},{6,2},{8,4},{10,6},{12,8},{14,10},{1,9},{3,11}... | collective-permute-start | bytes 196616 | tf_op jit(solution)/shard_map/ppermute | solution.py:228
  17.8 4.3 %collective-permute-start.9 = (bf16[256,128]{1,0:T(8,128)(2,1)S(1)}, bf16[256,128]{1,0:T(8,128)(2,1)S(1)}, u32[]{:S(2)}, u32[]{:S(2)}) collective-permute-start(bf16[256,128]{1,0:T(8,128)(2,1)S(1)} %get-tuple-element.36), channel_id=1, source_target_pairs={{0,2},{1,3},{2,0},{3,1},{4,6},{5,7},{6,4},{7,5},{8,10},{9,11},{10,... | collective-permute-start | bytes 196616 | tf_op jit(solution)/shard_map/ppermute | solution.py:216
  19.4 7.9 %collective-permute-start.8 = (bf16[256,128]{1,0:T(8,128)(2,1)S(1)}, bf16[256,128]{1,0:T(8,128)(2,1)S(1)}, u32[]{:S(2)}, u32[]{:S(2)}) collective-permute-start(bf16[256,128]{1,0:T(8,128)(2,1)S(1)} %get-tuple-element.36), channel_id=1, source_target_pairs={{0,6},{2,4},{4,10},{6,8},{8,14},{10,12},{12,2},{14,0},{1,7},{3,5},... | collective-permute-start | bytes 196616 | tf_op jit(solution)/shard_map/ppermute | solution.py:228
  20.6 6.7 %collective-permute-start.7 = (bf16[256,128]{1,0:T(8,128)(2,1)S(1)}, bf16[256,128]{1,0:T(8,128)(2,1)S(1)}, u32[]{:S(2)}, u32[]{:S(2)}) collective-permute-start(bf16[256,128]{1,0:T(8,128)(2,1)S(1)} %get-tuple-element.35), channel_id=1, source_target_pairs={{0,4},{2,6},{4,8},{6,10},{8,12},{10,14},{12,0},{14,2},{1,5},{3,7},... | collective-permute-start | bytes 196616 | tf_op jit(solution)/shard_map/ppermute | solution.py:228
  22.1 6.9 %collective-permute-start.11 = (bf16[256,128]{1,0:T(8,128)(2,1)S(1)}, bf16[256,128]{1,0:T(8,128)(2,1)S(1)}, u32[]{:S(2)}, u32[]{:S(2)}) collective-permute-start(bf16[256,128]{1,0:T(8,128)(2,1)S(1)} %add_convert_fusion.refs_1_), channel_id=1, source_target_pairs={{0,8},{2,10},{4,12},{6,14},{8,0},{10,2},{12,4},{14,6},{1,13},{3,15... | collective-permute-start | bytes 196616 | tf_op jit(solution)/shard_map/ppermute | solution.py:228
  23.8 5.3 %collective-permute-start.10 = (bf16[256,128]{1,0:T(8,128)(2,1)S(1)}, bf16[256,128]{1,0:T(8,128)(2,1)S(1)}, u32[]{:S(2)}, u32[]{:S(2)}) collective-permute-start(bf16[256,128]{1,0:T(8,128)(2,1)S(1)} %add_convert_fusion.refs_1_), channel_id=1, source_target_pairs={{0,12},{2,14},{4,0},{6,2},{8,4},{10,6},{12,8},{14,10},{1,9},{3,11}... | collective-permute-start | bytes 196616 | tf_op jit(solution)/shard_map/ppermute | solution.py:228
  29.3 3.8 %collective-permute-start.12 = (bf16[128,128]{1,0:T(8,128)(2,1)S(1)}, bf16[128,128]{1,0:T(8,128)(2,1)S(1)}, u32[]{:S(2)}, u32[]{:S(2)}) collective-permute-start(bf16[128,128]{1,0:T(8,128)(2,1)S(1)} %get-tuple-element.40), channel_id=1, source_target_pairs={{0,3},{1,2},{2,1},{3,0},{4,7},{5,6},{6,5},{7,4},{8,11},{9,10},{10,... | collective-permute-start | bytes 98312 | tf_op jit(solution)/shard_map/ppermute | solution.py:216
  29.4 4.0 %collective-permute-start.13 = (bf16[128,128]{1,0:T(8,128)(2,1)S(1)}, bf16[128,128]{1,0:T(8,128)(2,1)S(1)}, u32[]{:S(2)}, u32[]{:S(2)}) collective-permute-start(bf16[128,128]{1,0:T(8,128)(2,1)S(1)} %get-tuple-element.41), channel_id=1, source_target_pairs={{0,2},{1,3},{2,0},{3,1},{4,6},{5,7},{6,4},{7,5},{8,10},{9,11},{10,... | collective-permute-start | bytes 98312 | tf_op jit(solution)/shard_map/ppermute | solution.py:216
  31.1 2.3 %collective-permute-start.14 = (bf16[128,128]{1,0:T(8,128)(2,1)S(1)}, bf16[128,128]{1,0:T(8,128)(2,1)S(1)}, u32[]{:S(2)}, u32[]{:S(2)}) collective-permute-start(bf16[128,128]{1,0:T(8,128)(2,1)S(1)} %get-tuple-element.42), channel_id=1, source_target_pairs={{0,1},{1,0},{2,3},{3,2},{4,5},{5,4},{6,7},{7,6},{8,9},{9,8},{10,11... | collective-permute-start | bytes 98312 | tf_op jit(solution)/shard_map/ppermute | solution.py:216

commit v8 on v7

--- a/solution.py
+++ b/solution.py
@@ -198,7 +198,7 @@
 
 
 def final_kernel(chips, own, restart, *refs):
-    parts, out = refs[:-1], refs[-1]
+    parts, out = [*refs[:-3], refs[-2], refs[-3]], refs[-1]
     _, _, core = place()
     topics = own.shape[1]
     for e in range(CORES):
@@ -329,7 +329,7 @@
         [VMEM] * (2 + len(moved)),
         [shape(f32, edge, CORES * topics)],
         4 * MIB,
-    )(own, restart_other, *moved[:0:-1], moved[0])
+    )(own, restart_other, *moved[:1:-1], moved[0], moved[1])
     return out
 
 

time: 34.2 us -> 34.2 us (level)
  no operation moved by 1% of the time
where the time goes in v8:
time: 34.2 us; the launch traced here: 34.1 us
  starting transfers between devices  19.6 us (57%)
  waiting for transfers between devices  8.95 us (26%)
  Pallas kernels  5.36 us (16%)
    ppermute x8, starting transfers between devices, from_behind(): return lax.ppermute(value, ('blk', 'col'), route)  12.7 us
    ppermute x7, starting transfers between devices, from_col(): return lax.ppermute(value, 'col', route)  6.9 us
    ppermute x8, waiting for transfers between devices, from_behind(): return lax.ppermute(value, ('blk', 'col'), route)  5.98 us
    ppermute x7, waiting for transfers between devices, from_col(): return lax.ppermute(value, 'col', route)  2.98 us
    pallas_call x1, Pallas kernels, body(): call(functools.partial(first_kernel, steps, columns, scale), [HBM] * 4, [...  2.13 us
    pallas_call x1, Pallas kernels, body(): call(functools.partial(keep_kernel, steps, columns, scale), [VMEM] * 2, [...  1.08 us
  transfers between devices with their start and end apart: 15, of which 8 were waited for; matrix products, arithmetic and copies ran while one was open for 0% of the time, Pallas kernels for 6%

profile of v8, /device:TPU:0, one launch (start us, length us, event | category | flops | bytes accessed | tf_op | source)
XLA Modules:
  0.0 34.1 jit_solution(4777372275278467947)
XLA Ops:
  0.0 2.1 %shard_map.46 = (bf16[512,512]{1,0:T(8,128)(2,1)S(1)}, bf16[512,128]{1,0:T(8,128)(2,1)S(1)}, s32[64,128]{1,0:T(8,128)S(1)}, f32[128,128]{1,0:T(8,128)S(1)}) custom-call(bf16[1,1,4,10,128,128]{5,4,3,2,1,0:T(8,128)(2,1)} %tiles_hbm.1, s32[1,1,4,10]{3,2,1,0:T(4,128)} %dest_hbm.1, s32[1,1,4]{2,1,0:T(1,128)} %count_hbm.1, s32[64,256]{1,0:T(8,128)} %bitcast.1), custom_call_target="tpu_custom_call" | custom-call | tf_op jit(solution)/shard_map/pallas_call | solution.py:255
  2.1 0.5 %collective-permute-start = (bf16[512,128]{1,0:T(8,128)(2,1)S(1)}, bf16[512,128]{1,0:T(8,128)(2,1)S(1)}, u32[]{:S(2)}, u32[]{:S(2)}) collective-permute-start(bf16[512,128]{1,0:T(8,128)(2,1)S(1)} %get-tuple-element.27), channel_id=1, source_target_pairs={{0,1},{1,0},{2,3},{3,2},{4,5},{5,4},{6,7},{7,6},{8,9},{9,8},{10,11... | collective-permute-start | bytes 393224 | tf_op jit(solution)/shard_map/ppermute | solution.py:216
  2.7 1.1 %shard_map.47 = (f32[512,128]{1,0:T(8,128)S(1)}, f32[256,128]{1,0:T(8,128)S(1)}, f32[256,128]{1,0:T(8,128)S(1)}) custom-call(bf16[512,512]{1,0:T(8,128)(2,1)S(1)} %get-tuple-element.29.dense.own, s32[64,128]{1,0:T(8,128)S(1)} %get-tuple-element.25.seed_rows), custom_call_target="tpu_custom_call" | custom-call | tf_op jit(solution)/shard_map/pallas_call | solution.py:279
  3.8 0.0 collective-permute-done.recv
  3.8 0.1 shard_map.48
  3.8 2.8 %collective-permute-start.4 = (bf16[256,128]{1,0:T(8,128)(2,1)S(1)}, bf16[256,128]{1,0:T(8,128)(2,1)S(1)}, u32[]{:S(2)}, u32[]{:S(2)}) collective-permute-start(bf16[256,128]{1,0:T(8,128)(2,1)S(1)} %get-tuple-element.31), channel_id=1, source_target_pairs={{0,2},{1,3},{2,0},{3,1},{4,6},{5,7},{6,4},{7,5},{8,10},{9,11},{10,... | collective-permute-start | bytes 196616 | tf_op jit(solution)/shard_map/ppermute | solution.py:216
  6.6 0.0 collective-permute-start.1
  6.6 1.5 %collective-permute-start.3 = (bf16[256,128]{1,0:T(8,128)(2,1)S(1)}, bf16[256,128]{1,0:T(8,128)(2,1)S(1)}, u32[]{:S(2)}, u32[]{:S(2)}) collective-permute-start(bf16[256,128]{1,0:T(8,128)(2,1)S(1)} %get-tuple-element.31), channel_id=1, source_target_pairs={{0,6},{2,4},{4,10},{6,8},{8,14},{10,12},{12,2},{14,0},{1,7},{3,5},... | collective-permute-start | bytes 196616 | tf_op jit(solution)/shard_map/ppermute | solution.py:228
  8.1 1.6 %collective-permute-start.2 = (bf16[256,128]{1,0:T(8,128)(2,1)S(1)}, bf16[256,128]{1,0:T(8,128)(2,1)S(1)}, u32[]{:S(2)}, u32[]{:S(2)}) collective-permute-start(bf16[256,128]{1,0:T(8,128)(2,1)S(1)} %get-tuple-element.30), channel_id=1, source_target_pairs={{0,4},{2,6},{4,8},{6,10},{8,12},{10,14},{12,0},{14,2},{1,5},{3,7},... | collective-permute-start | bytes 196616 | tf_op jit(solution)/shard_map/ppermute | solution.py:228
  9.7 0.0 collective-permute-done.4
  9.8 2.3 %collective-permute-start.6 = (bf16[256,128]{1,0:T(8,128)(2,1)S(1)}, bf16[256,128]{1,0:T(8,128)(2,1)S(1)}, u32[]{:S(2)}, u32[]{:S(2)}) collective-permute-start(bf16[256,128]{1,0:T(8,128)(2,1)S(1)} %add_convert_fusion.2.refs_1_), channel_id=1, source_target_pairs={{0,8},{2,10},{4,12},{6,14},{8,0},{10,2},{12,4},{14,6},{1,13},{3,15... | collective-permute-start | bytes 196616 | tf_op jit(solution)/shard_map/ppermute | solution.py:228
  12.1 1.7 %collective-permute-start.5 = (bf16[256,128]{1,0:T(8,128)(2,1)S(1)}, bf16[256,128]{1,0:T(8,128)(2,1)S(1)}, u32[]{:S(2)}, u32[]{:S(2)}) collective-permute-start(bf16[256,128]{1,0:T(8,128)(2,1)S(1)} %add_convert_fusion.2.refs_1_), channel_id=1, source_target_pairs={{0,12},{2,14},{4,0},{6,2},{8,4},{10,6},{12,8},{14,10},{1,9},{3,11}... | collective-permute-start | bytes 196616 | tf_op jit(solution)/shard_map/ppermute | solution.py:228
  13.8 0.8 %collective-permute-done.2 = bf16[256,128]{1,0:T(8,128)(2,1)S(1)} collective-permute-done((bf16[256,128]{1,0:T(8,128)(2,1)S(1)}, bf16[256,128]{1,0:T(8,128)(2,1)S(1)}, u32[]{:S(2)}, u32[]{:S(2)}) %collective-permute-start.2) | collective-permute-done | bytes 65568 | tf_op jit(solution)/shard_map/ppermute | solution.py:228
  14.6 0.0 collective-permute-done.3
  14.6 0.0 collective-permute-done.1.other
  14.7 0.3 shard_map.49.near
  15.0 2.1 %collective-permute-done.6.refs_1_ = bf16[256,128]{1,0:T(8,128)(2,1)S(1)} collective-permute-done((bf16[256,128]{1,0:T(8,128)(2,1)S(1)}, bf16[256,128]{1,0:T(8,128)(2,1)S(1)}, u32[]{:S(2)}, u32[]{:S(2)}) %collective-permute-start.6) | collective-permute-done | bytes 65568 | tf_op jit(solution)/shard_map/ppermute | solution.py:228
  17.0 0.4 %collective-permute-done.5.refs_0_ = bf16[256,128]{1,0:T(8,128)(2,1)S(1)} collective-permute-done((bf16[256,128]{1,0:T(8,128)(2,1)S(1)}, bf16[256,128]{1,0:T(8,128)(2,1)S(1)}, u32[]{:S(2)}, u32[]{:S(2)}) %collective-permute-start.5) | collective-permute-done | bytes 65568 | tf_op jit(solution)/shard_map/ppermute | solution.py:228
  17.5 0.3 shard_map.50
  17.8 1.6 %collective-permute-start.9 = (bf16[256,128]{1,0:T(8,128)(2,1)S(1)}, bf16[256,128]{1,0:T(8,128)(2,1)S(1)}, u32[]{:S(2)}, u32[]{:S(2)}) collective-permute-start(bf16[256,128]{1,0:T(8,128)(2,1)S(1)} %get-tuple-element.36), channel_id=1, source_target_pairs={{0,2},{1,3},{2,0},{3,1},{4,6},{5,7},{6,4},{7,5},{8,10},{9,11},{10,... | collective-permute-start | bytes 196616 | tf_op jit(solution)/shard_map/ppermute | solution.py:216
  19.4 1.2 %collective-permute-start.8 = (bf16[256,128]{1,0:T(8,128)(2,1)S(1)}, bf16[256,128]{1,0:T(8,128)(2,1)S(1)}, u32[]{:S(2)}, u32[]{:S(2)}) collective-permute-start(bf16[256,128]{1,0:T(8,128)(2,1)S(1)} %get-tuple-element.36), channel_id=1, source_target_pairs={{0,6},{2,4},{4,10},{6,8},{8,14},{10,12},{12,2},{14,0},{1,7},{3,5},... | collective-permute-start | bytes 196616 | tf_op jit(solution)/shard_map/ppermute | solution.py:228
  20.6 0.4 %collective-permute-start.7 = (bf16[256,128]{1,0:T(8,128)(2,1)S(1)}, bf16[256,128]{1,0:T(8,128)(2,1)S(1)}, u32[]{:S(2)}, u32[]{:S(2)}) collective-permute-start(bf16[256,128]{1,0:T(8,128)(2,1)S(1)} %get-tuple-element.35), channel_id=1, source_target_pairs={{0,4},{2,6},{4,8},{6,10},{8,12},{10,14},{12,0},{14,2},{1,5},{3,7},... | collective-permute-start | bytes 196616 | tf_op jit(solution)/shard_map/ppermute | solution.py:228
  21.0 1.1 %collective-permute-done.9 = bf16[256,128]{1,0:T(8,128)(2,1)S(1)} collective-permute-done((bf16[256,128]{1,0:T(8,128)(2,1)S(1)}, bf16[256,128]{1,0:T(8,128)(2,1)S(1)}, u32[]{:S(2)}, u32[]{:S(2)}) %collective-permute-start.9) | collective-permute-done | bytes 65568 | tf_op jit(solution)/shard_map/ppermute | solution.py:216
  22.1 1.7 %collective-permute-start.11 = (bf16[256,128]{1,0:T(8,128)(2,1)S(1)}, bf16[256,128]{1,0:T(8,128)(2,1)S(1)}, u32[]{:S(2)}, u32[]{:S(2)}) collective-permute-start(bf16[256,128]{1,0:T(8,128)(2,1)S(1)} %add_convert_fusion.refs_1_), channel_id=1, source_target_pairs={{0,8},{2,10},{4,12},{6,14},{8,0},{10,2},{12,4},{14,6},{1,13},{3,15... | collective-permute-start | bytes 196616 | tf_op jit(solution)/shard_map/ppermute | solution.py:228
  23.8 2.3 %collective-permute-start.10 = (bf16[256,128]{1,0:T(8,128)(2,1)S(1)}, bf16[256,128]{1,0:T(8,128)(2,1)S(1)}, u32[]{:S(2)}, u32[]{:S(2)}) collective-permute-start(bf16[256,128]{1,0:T(8,128)(2,1)S(1)} %add_convert_fusion.refs_1_), channel_id=1, source_target_pairs={{0,12},{2,14},{4,0},{6,2},{8,4},{10,6},{12,8},{14,10},{1,9},{3,11}... | collective-permute-start | bytes 196616 | tf_op jit(solution)/shard_map/ppermute | solution.py:228
  26.1 1.2 %collective-permute-done.7 = bf16[256,128]{1,0:T(8,128)(2,1)S(1)} collective-permute-done((bf16[256,128]{1,0:T(8,128)(2,1)S(1)}, bf16[256,128]{1,0:T(8,128)(2,1)S(1)}, u32[]{:S(2)}, u32[]{:S(2)}) %collective-permute-start.7) | collective-permute-done | bytes 65568 | tf_op jit(solution)/shard_map/ppermute | solution.py:228
  27.3 0.0 collective-permute-done.8
  27.3 0.3 shard_map.51.near
  27.7 1.4 %collective-permute-done.11.refs_1_ = bf16[256,128]{1,0:T(8,128)(2,1)S(1)} collective-permute-done((bf16[256,128]{1,0:T(8,128)(2,1)S(1)}, bf16[256,128]{1,0:T(8,128)(2,1)S(1)}, u32[]{:S(2)}, u32[]{:S(2)}) %collective-permute-start.11) | collective-permute-done | bytes 65568 | tf_op jit(solution)/shard_map/ppermute | solution.py:228
  29.1 0.0 collective-permute-done.10.refs_0_
  29.1 0.2 shard_map.53
  29.3 0.1 collective-permute-start.12
  29.4 1.5 %collective-permute-start.14 = (bf16[128,128]{1,0:T(8,128)(2,1)S(1)}, bf16[128,128]{1,0:T(8,128)(2,1)S(1)}, u32[]{:S(2)}, u32[]{:S(2)}) collective-permute-start(bf16[128,128]{1,0:T(8,128)(2,1)S(1)} %get-tuple-element.42), channel_id=1, source_target_pairs={{0,2},{1,3},{2,0},{3,1},{4,6},{5,7},{6,4},{7,5},{8,10},{9,11},{10,... | collective-permute-start | bytes 98312 | tf_op jit(solution)/shard_map/ppermute | solution.py:216
  30.9 0.2 shard_map.52
  31.1 0.4 %collective-permute-start.13 = (bf16[128,128]{1,0:T(8,128)(2,1)S(1)}, bf16[128,128]{1,0:T(8,128)(2,1)S(1)}, u32[]{:S(2)}, u32[]{:S(2)}) collective-permute-start(bf16[128,128]{1,0:T(8,128)(2,1)S(1)} %get-tuple-element.41), channel_id=1, source_target_pairs={{0,1},{1,0},{2,3},{3,2},{4,5},{5,4},{6,7},{7,6},{8,9},{9,8},{10,11... | collective-permute-start | bytes 98312 | tf_op jit(solution)/shard_map/ppermute | solution.py:216
  31.5 1.5 %collective-permute-done.12.refs_0_ = bf16[128,128]{1,0:T(8,128)(2,1)S(1)} collective-permute-done((bf16[128,128]{1,0:T(8,128)(2,1)S(1)}, bf16[128,128]{1,0:T(8,128)(2,1)S(1)}, u32[]{:S(2)}, u32[]{:S(2)}) %collective-permute-start.12) | collective-permute-done | bytes 32800 | tf_op jit(solution)/shard_map/ppermute | solution.py:216
  33.1 0.3 collective-permute-done.14.refs_2_
  33.4 0.0 collective-permute-done.13.refs_1_
  33.4 0.7 %shard_map.54 = f32[128,256]{1,0:T(8,128)} custom-call(f32[128,128]{1,0:T(8,128)S(1)} %get-tuple-element.38.own, f32[128,128]{1,0:T(8,128)S(1)} %get-tuple-element.39.restart, bf16[128,128]{1,0:T(8,128)(2,1)S(1)} %collective-permute-done.12.refs_0_, bf16[128,128]{1,0:T(8,128)(2,1)S(1)} %collective-permute-done.13.refs_1_, ...), custom_call_target="tpu_custom_call" | custom-call | tf_op jit(solution)/shard_map/pallas_call | solution.py:327
  (4 shorter events, 0.1 us)
Async XLA Ops:
  2.1 1.6 %collective-permute-start = (bf16[512,128]{1,0:T(8,128)(2,1)S(1)}, bf16[512,128]{1,0:T(8,128)(2,1)S(1)}, u32[]{:S(2)}, u32[]{:S(2)}) collective-permute-start(bf16[512,128]{1,0:T(8,128)(2,1)S(1)} %get-tuple-element.27), channel_id=1, source_target_pairs={{0,1},{1,0},{2,3},{3,2},{4,5},{5,4},{6,7},{7,6},{8,9},{9,8},{10,11... | collective-permute-start | bytes 393224 | tf_op jit(solution)/shard_map/ppermute | solution.py:216
  3.8 5.9 %collective-permute-start.4 = (bf16[256,128]{1,0:T(8,128)(2,1)S(1)}, bf16[256,128]{1,0:T(8,128)(2,1)S(1)}, u32[]{:S(2)}, u32[]{:S(2)}) collective-permute-start(bf16[256,128]{1,0:T(8,128)(2,1)S(1)} %get-tuple-element.31), channel_id=1, source_target_pairs={{0,2},{1,3},{2,0},{3,1},{4,6},{5,7},{6,4},{7,5},{8,10},{9,11},{10,... | collective-permute-start | bytes 196616 | tf_op jit(solution)/shard_map/ppermute | solution.py:216
  6.6 8.0 %collective-permute-start.1 = (bf16[512,512]{1,0:T(8,128)(2,1)S(1)}, bf16[512,512]{1,0:T(8,128)(2,1)S(1)}, u32[]{:S(2)}, u32[]{:S(2)}) collective-permute-start(bf16[512,512]{1,0:T(8,128)(2,1)S(1)} %get-tuple-element.29.dense.own), channel_id=1, source_target_pairs={{0,1},{1,0},{2,3},{3,2},{4,5},{5,4},{6,7},{7,6},{8,9},{9,8},{10,11... | collective-permute-start | bytes 1572872 | tf_op jit(solution)/shard_map/ppermute | solution.py:216
  6.6 8.0 %collective-permute-start.3 = (bf16[256,128]{1,0:T(8,128)(2,1)S(1)}, bf16[256,128]{1,0:T(8,128)(2,1)S(1)}, u32[]{:S(2)}, u32[]{:S(2)}) collective-permute-start(bf16[256,128]{1,0:T(8,128)(2,1)S(1)} %get-tuple-element.31), channel_id=1, source_target_pairs={{0,6},{2,4},{4,10},{6,8},{8,14},{10,12},{12,2},{14,0},{1,7},{3,5},... | collective-permute-start | bytes 196616 | tf_op jit(solution)/shard_map/ppermute | solution.py:228
  8.1 6.5 %collective-permute-start.2 = (bf16[256,128]{1,0:T(8,128)(2,1)S(1)}, bf16[256,128]{1,0:T(8,128)(2,1)S(1)}, u32[]{:S(2)}, u32[]{:S(2)}) collective-permute-start(bf16[256,128]{1,0:T(8,128)(2,1)S(1)} %get-tuple-element.30), channel_id=1, source_target_pairs={{0,4},{2,6},{4,8},{6,10},{8,12},{10,14},{12,0},{14,2},{1,5},{3,7},... | collective-permute-start | bytes 196616 | tf_op jit(solution)/shard_map/ppermute | solution.py:228
  9.8 7.3 %collective-permute-start.6 = (bf16[256,128]{1,0:T(8,128)(2,1)S(1)}, bf16[256,128]{1,0:T(8,128)(2,1)S(1)}, u32[]{:S(2)}, u32[]{:S(2)}) collective-permute-start(bf16[256,128]{1,0:T(8,128)(2,1)S(1)} %add_convert_fusion.2.refs_1_), channel_id=1, source_target_pairs={{0,8},{2,10},{4,12},{6,14},{8,0},{10,2},{12,4},{14,6},{1,13},{3,15... | collective-permute-start | bytes 196616 | tf_op jit(solution)/shard_map/ppermute | solution.py:228
  12.1 5.4 %collective-permute-start.5 = (bf16[256,128]{1,0:T(8,128)(2,1)S(1)}, bf16[256,128]{1,0:T(8,128)(2,1)S(1)}, u32[]{:S(2)}, u32[]{:S(2)}) collective-permute-start(bf16[256,128]{1,0:T(8,128)(2,1)S(1)} %add_convert_fusion.2.refs_1_), channel_id=1, source_target_pairs={{0,12},{2,14},{4,0},{6,2},{8,4},{10,6},{12,8},{14,10},{1,9},{3,11}... | collective-permute-start | bytes 196616 | tf_op jit(solution)/shard_map/ppermute | solution.py:228
  17.8 4.3 %collective-permute-start.9 = (bf16[256,128]{1,0:T(8,128)(2,1)S(1)}, bf16[256,128]{1,0:T(8,128)(2,1)S(1)}, u32[]{:S(2)}, u32[]{:S(2)}) collective-permute-start(bf16[256,128]{1,0:T(8,128)(2,1)S(1)} %get-tuple-element.36), channel_id=1, source_target_pairs={{0,2},{1,3},{2,0},{3,1},{4,6},{5,7},{6,4},{7,5},{8,10},{9,11},{10,... | collective-permute-start | bytes 196616 | tf_op jit(solution)/shard_map/ppermute | solution.py:216
  19.4 7.9 %collective-permute-start.8 = (bf16[256,128]{1,0:T(8,128)(2,1)S(1)}, bf16[256,128]{1,0:T(8,128)(2,1)S(1)}, u32[]{:S(2)}, u32[]{:S(2)}) collective-permute-start(bf16[256,128]{1,0:T(8,128)(2,1)S(1)} %get-tuple-element.36), channel_id=1, source_target_pairs={{0,6},{2,4},{4,10},{6,8},{8,14},{10,12},{12,2},{14,0},{1,7},{3,5},... | collective-permute-start | bytes 196616 | tf_op jit(solution)/shard_map/ppermute | solution.py:228
  20.6 6.7 %collective-permute-start.7 = (bf16[256,128]{1,0:T(8,128)(2,1)S(1)}, bf16[256,128]{1,0:T(8,128)(2,1)S(1)}, u32[]{:S(2)}, u32[]{:S(2)}) collective-permute-start(bf16[256,128]{1,0:T(8,128)(2,1)S(1)} %get-tuple-element.35), channel_id=1, source_target_pairs={{0,4},{2,6},{4,8},{6,10},{8,12},{10,14},{12,0},{14,2},{1,5},{3,7},... | collective-permute-start | bytes 196616 | tf_op jit(solution)/shard_map/ppermute | solution.py:228
  22.1 6.9 %collective-permute-start.11 = (bf16[256,128]{1,0:T(8,128)(2,1)S(1)}, bf16[256,128]{1,0:T(8,128)(2,1)S(1)}, u32[]{:S(2)}, u32[]{:S(2)}) collective-permute-start(bf16[256,128]{1,0:T(8,128)(2,1)S(1)} %add_convert_fusion.refs_1_), channel_id=1, source_target_pairs={{0,8},{2,10},{4,12},{6,14},{8,0},{10,2},{12,4},{14,6},{1,13},{3,15... | collective-permute-start | bytes 196616 | tf_op jit(solution)/shard_map/ppermute | solution.py:228
  23.8 5.3 %collective-permute-start.10 = (bf16[256,128]{1,0:T(8,128)(2,1)S(1)}, bf16[256,128]{1,0:T(8,128)(2,1)S(1)}, u32[]{:S(2)}, u32[]{:S(2)}) collective-permute-start(bf16[256,128]{1,0:T(8,128)(2,1)S(1)} %add_convert_fusion.refs_1_), channel_id=1, source_target_pairs={{0,12},{2,14},{4,0},{6,2},{8,4},{10,6},{12,8},{14,10},{1,9},{3,11}... | collective-permute-start | bytes 196616 | tf_op jit(solution)/shard_map/ppermute | solution.py:228
  29.3 3.8 %collective-permute-start.12 = (bf16[128,128]{1,0:T(8,128)(2,1)S(1)}, bf16[128,128]{1,0:T(8,128)(2,1)S(1)}, u32[]{:S(2)}, u32[]{:S(2)}) collective-permute-start(bf16[128,128]{1,0:T(8,128)(2,1)S(1)} %get-tuple-element.40), channel_id=1, source_target_pairs={{0,3},{1,2},{2,1},{3,0},{4,7},{5,6},{6,5},{7,4},{8,11},{9,10},{10,... | collective-permute-start | bytes 98312 | tf_op jit(solution)/shard_map/ppermute | solution.py:216
  29.4 4.0 %collective-permute-start.14 = (bf16[128,128]{1,0:T(8,128)(2,1)S(1)}, bf16[128,128]{1,0:T(8,128)(2,1)S(1)}, u32[]{:S(2)}, u32[]{:S(2)}) collective-permute-start(bf16[128,128]{1,0:T(8,128)(2,1)S(1)} %get-tuple-element.42), channel_id=1, source_target_pairs={{0,2},{1,3},{2,0},{3,1},{4,6},{5,7},{6,4},{7,5},{8,10},{9,11},{10,... | collective-permute-start | bytes 98312 | tf_op jit(solution)/shard_map/ppermute | solution.py:216
  31.1 2.3 %collective-permute-start.13 = (bf16[128,128]{1,0:T(8,128)(2,1)S(1)}, bf16[128,128]{1,0:T(8,128)(2,1)S(1)}, u32[]{:S(2)}, u32[]{:S(2)}) collective-permute-start(bf16[128,128]{1,0:T(8,128)(2,1)S(1)} %get-tuple-element.41), channel_id=1, source_target_pairs={{0,1},{1,0},{2,3},{3,2},{4,5},{5,4},{6,7},{7,6},{8,9},{9,8},{10,11... | collective-permute-start | bytes 98312 | tf_op jit(solution)/shard_map/ppermute | solution.py:216
